TPU v7x, 32 devices: a whole 2x2x4 slice. The times are simulated.
32 devices in a mesh: users: 8 (over y, x, core), items: 4 (over z).
Axes of the slice: x: 2, y: 2, z: 4, core: 2. Of those that a mesh axis runs over, the one named last changes fastest.
Arguments:
- tiles: float32 [8, 4, 4, 32, 128, 128], P('users', 'items'), may hold values from -6 to 6
- user_blocks: int32 [8, 4, 4], P('users', 'items'), may hold values from 0 to 15, as said below
- item_blocks: int32 [8, 4, 4], P('users', 'items'), may hold values from 0 to 127, as said below
- counts: int32 [8, 4], P('users', 'items'), may hold values from 1 to 4, as said below
- user_factor: float32 [64, 16384], P(None, ('users', 'items')), may hold values from -0.5 to 0.5
- item_factor: float32 [64, 65536], P(None, ('items', 'users')), may hold values from -0.5 to 0.5
- week_factor: float32 [32, 64], replicated, may hold values from -1 to 1
Outputs:
- m_users: float32 [64, 16384], P(None, ('users', 'items'))
- m_items: float32 [64, 65536], P(None, ('items', 'users'))
Inputs may be any that keep to these rules, and one draw needn't show every extreme that they name: `user_blocks`: within one device the first 4 slots name distinct (user block, item block) pairs of its grid row and grid column. `item_blocks`: paired with user_blocks slot by slot. `counts`: some device holds 4 tiles in every draw.
All inputs are finite; a program needn't handle non-finite values.
Results may differ from a plain program's by a relative error of at most 0.0001.
Values sent between devices are 32-bit elements; how exact they have to be, the bound alone decides.
No kernel may reach another device: no remote copies, remote signals or barrier semaphores. Data moves between devices by JAX's collectives and lax.ppermute only.
A program may use at most 128 MiB of HBM per device.

v0:
```python
import functools

import jax
import jax.numpy as jnp
from jax import lax
from jax.experimental import pallas as pl
from jax.experimental.pallas import tpu as pltpu
from jax.sharding import PartitionSpec as P

F32 = jnp.float32
BF16 = jnp.bfloat16
ANY = pl.BlockSpec(memory_space=pl.ANY)
HBM = pl.BlockSpec(memory_space=pltpu.HBM)
SMEM = pl.BlockSpec(memory_space=pltpu.SMEM)
VMEM = pl.BlockSpec(memory_space=pltpu.VMEM)


def columns(block, width):
    return pl.ds(pl.multiple_of(block * width, width), width)


def split(value):
    high = value.astype(BF16)
    return high, (value - high.astype(F32)).astype(BF16)


def hold_kernel(done):
    done[...] = jnp.zeros_like(done)


def prepare_kernel(count_ref, tiles, week_factor, users, _, halves, spread, users_out):
    weeks, width = tiles.shape[1], tiles.shape[3]
    users_out[...] = users[...]
    weeks_t = week_factor[...].T
    for week in range(weeks):
        spread[week] = jnp.broadcast_to(weeks_t[:, week : week + 1], spread.shape[1:])

    def work(slot, carry):
        def one(week, inner):
            high, low = split(tiles[slot, week])
            halves[slot, week, :, :width] = high
            halves[slot, week, :, width:] = low
            return inner

        return lax.fori_loop(0, weeks, one, carry, unroll=8)

    lax.fori_loop(0, count_ref[0, 0], work, 0)


def serve_kernel(chips, width, requests, own, sibling, _, *messages):
    me = lax.axis_index("users")
    per_device = own.shape[1] // width
    for step in range(1, chips):
        for slot in range(requests.shape[1]):
            index = requests[step, slot]
            device = index // per_device
            place = columns(index % per_device, width)
            for owner, source in ((me, own), (me ^ 1, sibling)):

                @pl.when(device == owner)
                def _():
                    messages[step - 1][:, slot * width : (slot + 1) * width] = source[:, place]


def user_term(spread, items, tile, together=8):
    weeks, height, width = tile.shape
    rank = items.shape[0]
    both = jnp.concatenate(split(items), axis=0)
    both = jnp.concatenate([both, both], axis=1)
    total = jnp.zeros((rank, height), F32)
    for week in range(0, weeks, together):
        rows = tile[week : week + together].reshape(together * height, width)
        sums = lax.dot_general(both, rows, (((1,), (1,)), ((), ())), preferred_element_type=F32)
        for part in range(together):
            here = sums[:, part * height : (part + 1) * height]
            total += (here[:rank] + here[rank:]) * spread[week + part]
    return total


def item_term(spread, users, tile):
    weeks, height, width = tile.shape
    width //= 2
    rank = users.shape[0]
    total = jnp.zeros((2 * rank, 2 * width), F32)
    for week in range(0, weeks, 2):
        left = [
            jnp.concatenate(split(spread[part] * users), axis=0) for part in (week, week + 1)
        ]
        total += jnp.dot(
            jnp.concatenate(left, axis=1),
            jnp.concatenate([tile[week], tile[week + 1]], axis=0),
            preferred_element_type=F32,
        )
    half = total[:rank] + total[rank:]
    return half[:, :width] + half[:, width:]


def mode1_kernel(groups, count_ref, users_ref, items_ref, spread, tiles, own, sibling, *refs):
    *messages, even, odd, sums = refs
    height, width = tiles.shape[2], tiles.shape[3] // 2
    me = lax.axis_index("users")
    column = lax.axis_index("items")
    per_device = own.shape[1] // width
    kept = even.shape[2] // height
    sums[...] = jnp.zeros_like(sums)

    def work(slot, carry):
        index = items_ref[0, slot]
        device = index // per_device
        place = columns(index % per_device, width)
        items = jnp.where(device == me, own[:, place], sibling[:, place])
        source = (device // 2) ^ (me // 2)
        here = columns(slot, width)
        for step, message in enumerate(messages):
            items = jnp.where(source == step + 1, message[:, here], items)
        sums[users_ref[0, slot]] += user_term(spread, items, tiles.at[slot])
        return carry

    lax.fori_loop(0, count_ref[0, 0], work, 0)
    for step in range(groups):
        first = (column ^ step) * kept
        for block in range(kept):
            target = (even, odd)[step % 2]
            target[step // 2, :, block * height : (block + 1) * height] = sums[first + block]


def mode2_kernel(count_ref, users_ref, spread, tiles, _, *refs):
    *factors, terms = refs
    height, width = tiles.shape[2], tiles.shape[3] // 2
    column = lax.axis_index("items")
    kept = factors[0].shape[1] // height
    terms[...] = jnp.zeros_like(terms)

    def work(slot, carry):
        block = users_ref[0, slot]
        source = (block // kept) ^ column
        place = columns(block % kept, height)
        users = factors[0][:, place]
        for step in range(1, len(factors)):
            users = jnp.where(source == step, factors[step][:, place], users)
        terms[:, columns(slot, width)] = item_term(spread, users, tiles.at[slot])
        return carry

    lax.fori_loop(0, count_ref[0, 0], work, 0)


def collect_kernel(ids, *refs):
    *terms, own, other = refs
    slots = ids.shape[1]
    width = terms[0].shape[1] // slots
    per_device = own.shape[1] // width
    me = lax.axis_index("users")
    own[...] = jnp.zeros_like(own)
    other[...] = jnp.zeros_like(other)
    for step, term in enumerate(terms):
        for slot in range(slots):
            index = ids[step, slot]
            device = index // per_device
            place = columns(index % per_device, width)
            for owner, target in ((me, own), (me ^ 1, other)):

                @pl.when(device == owner)
                def _():
                    target[:, place] += term[:, slot * width : (slot + 1) * width]


def finish_users_kernel(kept, arrived, total, done):
    total[...] = kept[...] + arrived[...]
    done[...] = jnp.zeros_like(done)


def finish_items_kernel(own, arrived, _, total):
    total[...] = own[...] + arrived[...]


def on_device(sizes, tiles, user_blocks, item_blocks, counts, user_factor, item_factor, week_factor):
    rows, groups = sizes
    chips = rows // 2
    tiles = tiles[0, 0]
    slots, weeks, height, width = tiles.shape
    rank = week_factor.shape[1]
    user_width = user_factor.shape[1]

    def limit(mebibytes):
        return pltpu.CompilerParams(vmem_limit_bytes=mebibytes << 20)

    def cost(times):
        return pl.CostEstimate(
            flops=int(times * 8 * slots * weeks * height * width * rank),
            bytes_accessed=int(times * 4 * slots * weeks * height * width),
            transcendentals=0,
        )

    def across_chips(value, step):
        return lax.ppermute(value, "users", [(i, i ^ (2 * step)) for i in range(rows)])

    def across_cores(value):
        return lax.ppermute(value, "users", [(i, i ^ 1) for i in range(rows)])

    def across_groups(value, step):
        return lax.ppermute(value, "items", [(i, i ^ step) for i in range(groups)])

    def array(*shape, dtype=F32):
        return jax.ShapeDtypeStruct(shape, dtype)

    sibling = across_cores(item_factor)
    asked = [item_blocks[0]] + [across_chips(item_blocks[0], step) for step in range(1, chips)]
    near = jnp.concatenate(asked, axis=0)
    far_users = across_groups(user_factor, groups // 2)
    held = pl.pallas_call(
        hold_kernel,
        out_shape=array(8, 128),
        out_specs=VMEM,
        compiler_params=limit(4),
        cost_estimate=cost(4),
        name="hold",
    )()

    served = pl.pallas_call(
        functools.partial(serve_kernel, chips, width),
        out_shape=[array(rank, slots * width)] * (chips - 1),
        in_specs=[SMEM] + [VMEM] * 2 + [ANY],
        out_specs=[VMEM] * (chips - 1),
        compiler_params=limit(4),
        cost_estimate=cost(1),
        name="serve",
    )(near, item_factor, sibling, held)
    messages = [across_chips(value, step + 1) for step, value in enumerate(served)]

    halves, spread, far_users = pl.pallas_call(
        prepare_kernel,
        out_shape=[
            array(slots, weeks, height, 2 * width, dtype=BF16),
            array(weeks, rank, height),
            array(rank, user_width),
        ],
        in_specs=[SMEM] + [VMEM] * 3 + [ANY],
        out_specs=[VMEM] * 3,
        compiler_params=limit(24),
        name="prepare",
    )(counts, tiles, week_factor, far_users, served[0])
    row_factors = {0: user_factor, groups // 2: far_users}
    step = groups // 4
    while step:
        row_factors |= {at ^ step: across_groups(v, step) for at, v in row_factors.items()}
        step //= 2

    even, odd = pl.pallas_call(
        functools.partial(mode1_kernel, groups),
        out_shape=[array(groups // 2, rank, user_width)] * 2,
        in_specs=[SMEM] * 3 + [VMEM] * (3 + chips),
        out_specs=[VMEM] * 2,
        scratch_shapes=[pltpu.VMEM((groups * user_width // height, rank, height), F32)],
        compiler_params=limit(8),
        cost_estimate=cost(1),
        name="mode1",
    )(
        counts,
        user_blocks[0],
        item_blocks[0],
        spread,
        halves,
        item_factor,
        sibling,
        *messages,
    )
    terms = pl.pallas_call(
        mode2_kernel,
        out_shape=array(rank, slots * width),
        in_specs=[SMEM] * 2 + [VMEM] * 2 + [ANY] + [VMEM] * groups,
        out_specs=VMEM,
        compiler_params=limit(8),
        cost_estimate=cost(2),
        name="mode2",
    )(
        counts,
        user_blocks[0],
        spread,
        halves,
        even,
        *(row_factors[step] for step in range(groups)),
    )
    near_terms = [terms] + [across_chips(terms, step) for step in range(1, chips)]
    own, other = pl.pallas_call(
        collect_kernel,
        out_shape=[array(*item_factor.shape)] * 2,
        in_specs=[SMEM] + [VMEM] * chips,
        out_specs=[VMEM] * 2,
        compiler_params=limit(4),
        name="collect",
    )(near, *near_terms)
    kept, sent, step = even, odd, 1
    while step < groups // 2:
        arrived = across_groups(sent, step)
        kept, sent = kept[0::2] + arrived[0::2], kept[1::2] + arrived[1::2]
        step *= 2
    m_users, done = pl.pallas_call(
        finish_users_kernel,
        out_shape=[array(rank, user_width), array(8, 128)],
        in_specs=[VMEM] * 2,
        out_specs=[VMEM] * 2,
        compiler_params=limit(4),
        cost_estimate=cost(4),
        name="finish_users",
    )(kept[0], across_groups(sent[0], step))
    m_items = pl.pallas_call(
        finish_items_kernel,
        out_shape=array(*item_factor.shape),
        in_specs=[VMEM] * 2 + [ANY],
        out_specs=VMEM,
        compiler_params=limit(4),
        name="finish_items",
    )(own, across_cores(other), done)
    return m_users, m_items


def solution(mesh):
    rows, groups = mesh.shape["users"], mesh.shape["items"]
    assert rows > 1 and rows & (rows - 1) == 0 and groups > 1 and groups & (groups - 1) == 0
    return jax.shard_map(
        functools.partial(on_device, (rows, groups)),
        mesh=mesh,
        in_specs=(
            P("users", "items", None, None, None, None),
            P("users", "items", None),
            P("users", "items", None),
            P("users", "items"),
            P(None, ("users", "items")),
            P(None, ("items", "users")),
            P(),
        ),
        out_specs=(P(None, ("users", "items")), P(None, ("items", "users"))),
        check_vma=False,
    )
```

profile of v0, /device:TPU:0, one launch (start us, length us, event | category | flops | bytes accessed | tf_op | source)
XLA Modules:
  0.0 37.5 jit_solution(13882892792595295747)
XLA Ops:
  0.7 0.5 %collective-permute-start.4 = (f32[64,2048]{1,0:T(8,128)}, f32[64,2048]{1,0:T(8,128)S(1)}, u32[]{:S(2)}, u32[]{:S(2)}) collective-permute-start(f32[64,2048]{1,0:T(8,128)} %own.3), channel_id=1, source_target_pairs={{0,4},{4,0},{8,12},{12,8},{16,20},{20,16},{24,28},{28,24},{1,5},{5... | collective-permute-start | bytes 1572872 | tf_op jit(solution)/shard_map/ppermute | solution.py:198
  1.2 2.6 %collective-permute-start.1 = (s32[1,4]{1,0:T(1,128)}, s32[1,4]{1,0:T(1,128)S(1)}, u32[]{:S(2)}, u32[]{:S(2)}) collective-permute-start(s32[1,4]{1,0:T(1,128)} %bitcast.12), channel_id=1, source_target_pairs={{0,8},{4,12},{8,0},{12,4},{16,24},{20,28},{24,16},{28,20},{1,9},{5... | collective-permute-start | bytes 56 | tf_op jit(solution)/shard_map/ppermute | solution.py:195
  3.8 1.5 %collective-permute-start.2 = (s32[1,4]{1,0:T(1,128)}, s32[1,4]{1,0:T(1,128)S(1)}, u32[]{:S(2)}, u32[]{:S(2)}) collective-permute-start(s32[1,4]{1,0:T(1,128)} %bitcast.13), channel_id=1, source_target_pairs={{0,16},{4,20},{8,24},{12,28},{16,0},{20,4},{24,8},{28,12},{1,17},{... | collective-permute-start | bytes 56 | tf_op jit(solution)/shard_map/ppermute | solution.py:195
  5.3 0.0 collective-permute-start.3
  5.3 3.0 %collective-permute-start = (f32[64,512]{1,0:T(8,128)}, f32[64,512]{1,0:T(8,128)S(1)}, u32[]{:S(2)}, u32[]{:S(2)}) collective-permute-start(f32[64,512]{1,0:T(8,128)} %refs_0_.1), channel_id=1, source_target_pairs={{0,2},{1,3},{2,0},{3,1},{4,6},{5,7},{6,4},{7,5},{8,10},{9,11},{10,... | collective-permute-start | bytes 393224 | tf_op jit(solution)/shard_map/ppermute | solution.py:201
  8.4 1.5 %collective-permute-done.3 = s32[1,4]{1,0:T(1,128)S(1)} collective-permute-done((s32[1,4]{1,0:T(1,128)}, s32[1,4]{1,0:T(1,128)S(1)}, u32[]{:S(2)}, u32[]{:S(2)}) %collective-permute-start.3) | collective-permute-done | bytes 48 | tf_op jit(solution)/shard_map/ppermute | solution.py:195
  9.9 0.0 collective-permute-done.4.sibling
  9.9 0.8 %serve.1 = (f32[64,512]{1,0:T(8,128)S(1)}, f32[64,512]{1,0:T(8,128)S(1)}, f32[64,512]{1,0:T(8,128)S(1)}) custom-call(s32[4,4]{1,0:T(4,128)S(1)} %pad_add_fusion.requests.ids, f32[64,2048]{1,0:T(8,128)S(1)} %copy-done, f32[64,2048]{1,0:T(8,128)S(1)} %collective-permute-done.4.sibling, f32[8,128]{1,0:T(8,128)S(1)} %hold.1._), custom_call_target="tpu_custom_call" | custom-call | flops 1073741824 | bytes 8388608 | tf_op jit(solution)/shard_map/serve/pallas_call | solution.py:219
  10.7 0.6 %collective-permute-start.5 = (f32[64,512]{1,0:T(8,128)S(1)}, f32[64,512]{1,0:T(8,128)S(1)}, u32[]{:S(2)}, u32[]{:S(2)}) collective-permute-start(f32[64,512]{1,0:T(8,128)S(1)} %get-tuple-element.14._), channel_id=1, source_target_pairs={{0,8},{4,12},{8,0},{12,4},{16,24},{20,28},{24,16},{28,20},{1,9},{5... | collective-permute-start | bytes 393224 | tf_op jit(solution)/shard_map/ppermute | solution.py:195
  11.3 1.0 %collective-permute-start.6 = (f32[64,512]{1,0:T(8,128)S(1)}, f32[64,512]{1,0:T(8,128)S(1)}, u32[]{:S(2)}, u32[]{:S(2)}) collective-permute-start(f32[64,512]{1,0:T(8,128)S(1)} %get-tuple-element.17), channel_id=1, source_target_pairs={{0,16},{4,20},{8,24},{12,28},{16,0},{20,4},{24,8},{28,12},{1,17},{... | collective-permute-start | bytes 393224 | tf_op jit(solution)/shard_map/ppermute | solution.py:195
  12.3 2.0 %collective-permute-start.7 = (f32[64,512]{1,0:T(8,128)S(1)}, f32[64,512]{1,0:T(8,128)S(1)}, u32[]{:S(2)}, u32[]{:S(2)}) collective-permute-start(f32[64,512]{1,0:T(8,128)S(1)} %get-tuple-element.18), channel_id=1, source_target_pairs={{0,24},{4,28},{8,16},{12,20},{16,8},{20,12},{24,0},{28,4},{1,25},{... | collective-permute-start | bytes 393224 | tf_op jit(solution)/shard_map/ppermute | solution.py:195
  14.3 1.6 %collective-permute-start.10 = (f32[64,512]{1,0:T(8,128)S(1)}, f32[64,512]{1,0:T(8,128)S(1)}, u32[]{:S(2)}, u32[]{:S(2)}) collective-permute-start(f32[64,512]{1,0:T(8,128)S(1)} %copy-done.1), channel_id=1, source_target_pairs={{0,1},{1,0},{2,3},{3,2},{4,5},{5,4},{6,7},{7,6},{8,9},{9,8},{10,11... | collective-permute-start | bytes 393224 | tf_op jit(solution)/shard_map/ppermute | solution.py:201
  16.6 0.8 %prepare.1 = (bf16[4,32,128,256]{3,2,1,0:T(8,128)(2,1)S(1)}, f32[32,64,128]{2,1,0:T(8,128)S(1)}, f32[64,512]{1,0:T(8,128)S(1)}) custom-call(s32[1,1]{1,0:T(1,128)S(6)} %copy.9.count_ref, f32[4,32,128,128]{3,2,1,0:T(8,128)S(1)} %bitcast.9, f32[32,64]{1,0:T(8,128)S(1)} %copy-done.2, f32[64,512]{1,0:T(8,128)S(1)} %collective-permute-done.users, ...), custom_call_target="tpu_custom_call" | custom-call | tf_op jit(solution)/shard_map/prepare/pallas_call | solution.py:230
  17.4 0.9 %collective-permute-start.11 = (f32[64,512]{1,0:T(8,128)S(1)}, f32[64,512]{1,0:T(8,128)S(1)}, u32[]{:S(2)}, u32[]{:S(2)}) collective-permute-start(f32[64,512]{1,0:T(8,128)S(1)} %get-tuple-element.22.refs_2_), channel_id=1, source_target_pairs={{0,1},{1,0},{2,3},{3,2},{4,5},{5,4},{6,7},{7,6},{8,9},{9,8},{10,11... | collective-permute-start | bytes 393224 | tf_op jit(solution)/shard_map/ppermute | solution.py:201
  18.3 0.0 collective-permute-done.5.refs_0_
  18.3 0.7 %collective-permute-done.6.refs_1_ = f32[64,512]{1,0:T(8,128)S(1)} collective-permute-done((f32[64,512]{1,0:T(8,128)S(1)}, f32[64,512]{1,0:T(8,128)S(1)}, u32[]{:S(2)}, u32[]{:S(2)}) %collective-permute-start.6) | collective-permute-done | bytes 131104 | tf_op jit(solution)/shard_map/ppermute | solution.py:195
  19.0 0.0 collective-permute-done.7.refs_2_
  19.0 1.4 %mode1.1 = (f32[2,64,512]{2,1,0:T(8,128)S(1)}, f32[2,64,512]{2,1,0:T(8,128)S(1)}) custom-call(s32[1,1]{1,0:T(1,128)S(6)} %copy.9.count_ref, s32[1,4]{1,0:T(1,128)S(1)} %bitcast.10, s32[1,4]{1,0:T(1,128)S(1)} %bitcast.16, f32[32,64,128]{2,1,0:T(8,128)S(1)} %get-tuple-element.15.spread, bf16[4,32,128,256]{3,2,1,0:T(8,128)(2,1)S(1)} %get-tuple-element.16.tiles, ...), custom_call_target="tpu_custom_call" | custom-call | flops 1073741824 | bytes 8388608 | tf_op jit(solution)/shard_map/mode1/pallas_call | solution.py:248
  20.4 2.5 %collective-permute-start.8 = (f32[2,64,512]{2,1,0:T(8,128)S(1)}, f32[2,64,512]{2,1,0:T(8,128)S(1)}, u32[]{:S(2)}, u32[]{:S(2)}) collective-permute-start(f32[2,64,512]{2,1,0:T(8,128)S(1)} %get-tuple-element.20), channel_id=1, source_target_pairs={{0,1},{1,0},{2,3},{3,2},{4,5},{5,4},{6,7},{7,6},{8,9},{9,8},{10,11... | collective-permute-start | bytes 786440 | tf_op jit(solution)/shard_map/ppermute | solution.py:201
  22.9 0.0 collective-permute-done.10.refs_1_
  22.9 0.5 %collective-permute-done.11.refs_3_ = f32[64,512]{1,0:T(8,128)S(1)} collective-permute-done((f32[64,512]{1,0:T(8,128)S(1)}, f32[64,512]{1,0:T(8,128)S(1)}, u32[]{:S(2)}, u32[]{:S(2)}) %collective-permute-start.11) | collective-permute-done | bytes 131104 | tf_op jit(solution)/shard_map/ppermute | solution.py:201
  23.4 1.0 %mode2.1.refs_0_ = f32[64,512]{1,0:T(8,128)S(1)} custom-call(s32[1,1]{1,0:T(1,128)S(6)} %copy.9.count_ref, s32[1,4]{1,0:T(1,128)S(1)} %bitcast.11, f32[32,64,128]{2,1,0:T(8,128)S(1)} %get-tuple-element.15.spread, bf16[4,32,128,256]{3,2,1,0:T(8,128)(2,1)S(1)} %get-tuple-element.16.tiles, f32[2,64,512]{2,1,0:T(8,128)S(1)} %get-tuple-element.19._, ...), custom_call_target="tpu_custom_call" | custom-call | flops 2147483648 | bytes 16777216 | tf_op jit(solution)/shard_map/mode2/pallas_call | solution.py:267
  24.4 2.6 %collective-permute-start.12 = (f32[64,512]{1,0:T(8,128)S(1)}, f32[64,512]{1,0:T(8,128)S(1)}, u32[]{:S(2)}, u32[]{:S(2)}) collective-permute-start(f32[64,512]{1,0:T(8,128)S(1)} %mode2.1.refs_0_), channel_id=1, source_target_pairs={{0,8},{4,12},{8,0},{12,4},{16,24},{20,28},{24,16},{28,20},{1,9},{5... | collective-permute-start | bytes 393224 | tf_op jit(solution)/shard_map/ppermute | solution.py:195
  27.0 1.5 %collective-permute-start.14 = (f32[64,512]{1,0:T(8,128)S(1)}, f32[64,512]{1,0:T(8,128)S(1)}, u32[]{:S(2)}, u32[]{:S(2)}) collective-permute-start(f32[64,512]{1,0:T(8,128)S(1)} %mode2.1.refs_0_), channel_id=1, source_target_pairs={{0,24},{4,28},{8,16},{12,20},{16,8},{20,12},{24,0},{28,4},{1,25},{... | collective-permute-start | bytes 393224 | tf_op jit(solution)/shard_map/ppermute | solution.py:195
  28.6 2.5 %collective-permute-start.9 = (f32[64,512]{1,0:T(8,128)S(1)}, f32[64,512]{1,0:T(8,128)S(1)}, u32[]{:S(2)}, u32[]{:S(2)}) collective-permute-start(f32[64,512]{1,0:T(8,128)S(1)} %get-tuple-element.26), channel_id=1, source_target_pairs={{0,2},{1,3},{2,0},{3,1},{4,6},{5,7},{6,4},{7,5},{8,10},{9,11},{10,... | collective-permute-start | bytes 393224 | tf_op jit(solution)/shard_map/ppermute | solution.py:201
  31.1 0.0 collective-permute-done.12.refs_1_
  31.1 2.3 %collective-permute-done.13.refs_2_ = f32[64,512]{1,0:T(8,128)S(1)} collective-permute-done((f32[64,512]{1,0:T(8,128)S(1)}, f32[64,512]{1,0:T(8,128)S(1)}, u32[]{:S(2)}, u32[]{:S(2)}) %collective-permute-start.13) | collective-permute-done | bytes 131104 | tf_op jit(solution)/shard_map/ppermute | solution.py:195
  33.5 1.0 %collect.1 = (f32[64,2048]{1,0:T(8,128)S(1)}, f32[64,2048]{1,0:T(8,128)S(1)}) custom-call(s32[4,4]{1,0:T(4,128)S(1)} %pad_add_fusion.requests.ids, f32[64,512]{1,0:T(8,128)S(1)} %mode2.1.refs_0_, f32[64,512]{1,0:T(8,128)S(1)} %collective-permute-done.12.refs_1_, f32[64,512]{1,0:T(8,128)S(1)} %collective-permute-done.13.refs_2_, ...), custom_call_target="tpu_custom_call" | custom-call | tf_op jit(solution)/shard_map/collect/pallas_call | solution.py:284
  34.4 0.1 collective-permute-start.15
  34.5 1.5 %collective-permute-done.9.arrived = f32[64,512]{1,0:T(8,128)S(1)} collective-permute-done((f32[64,512]{1,0:T(8,128)S(1)}, f32[64,512]{1,0:T(8,128)S(1)}, u32[]{:S(2)}, u32[]{:S(2)}) %collective-permute-start.9) | collective-permute-done | bytes 131104 | tf_op jit(solution)/shard_map/ppermute | solution.py:201
  36.0 0.7 %finish_users.1 = (f32[64,512]{1,0:T(8,128)}, f32[8,128]{1,0:T(8,128)S(1)}) custom-call(f32[64,512]{1,0:T(8,128)S(1)} %get-tuple-element.27.kept, f32[64,512]{1,0:T(8,128)S(1)} %collective-permute-done.9.arrived), custom_call_target="tpu_custom_call" | custom-call | flops 4294967296 | bytes 33554432 | tf_op jit(solution)/shard_map/finish_users/pallas_call | solution.py:297
  36.7 0.8 %finish_items.1 = f32[64,2048]{1,0:T(8,128)} custom-call(f32[64,2048]{1,0:T(8,128)S(1)} %get-tuple-element.23.own, f32[64,2048]{1,0:T(8,128)S(1)} %collective-permute-done.15.arrived, f32[8,128]{1,0:T(8,128)S(1)} %get-tuple-element.25._), custom_call_target="tpu_custom_call" | custom-call | tf_op jit(solution)/shard_map/finish_items/pallas_call | solution.py:306
  (25 shorter events, 0.1 us)
Async XLA Ops:
  0.6 9.3 %copy-start = (f32[64,2048]{1,0:T(8,128)S(1)}, f32[64,2048]{1,0:T(8,128)}, u32[]{:S(2)}) copy-start(f32[64,2048]{1,0:T(8,128)} %own.3) | copy-start | bytes 1572868
  0.6 9.2 %copy-start.4 = (s32[1,1,4]{2,1,0:T(1,128)S(1)}, s32[1,1,4]{2,1,0:T(1,128)}, u32[]{:S(2)}) copy-start(s32[1,1,4]{2,1,0:T(1,128)} %param.9) | copy-start | bytes 52
  0.7 9.2 %collective-permute-start.4 = (f32[64,2048]{1,0:T(8,128)}, f32[64,2048]{1,0:T(8,128)S(1)}, u32[]{:S(2)}, u32[]{:S(2)}) collective-permute-start(f32[64,2048]{1,0:T(8,128)} %own.3), channel_id=1, source_target_pairs={{0,4},{4,0},{8,12},{12,8},{16,20},{20,16},{24,28},{28,24},{1,5},{5... | collective-permute-start | bytes 1572872 | tf_op jit(solution)/shard_map/ppermute | solution.py:198
  1.2 15.4 %slice-start = ((s8[8388608]{0:T(1024)(128)(4,1)}), s8[4194304]{0:T(1024)(128)(4,1)S(1)}, s32[]{:S(2)}) async-start(s8[8388608]{0:T(1024)(128)(4,1)} %bitcast.7), calls=%async_computation | async-start | bytes 8388608
  1.2 13.1 %copy-start.1 = (f32[64,512]{1,0:T(8,128)S(1)}, f32[64,512]{1,0:T(8,128)}, u32[]{:S(2)}) copy-start(f32[64,512]{1,0:T(8,128)} %refs_0_.1) | copy-start | bytes 393220
  1.2 15.4 %slice-start.1 = ((s8[8388608]{0:T(1024)(128)(4,1)}), s8[4194304]{0:T(1024)(128)(4,1)S(1)}, s32[]{:S(2)}) async-start(s8[8388608]{0:T(1024)(128)(4,1)} %bitcast.7), calls=%async_computation.1 | async-start | bytes 8388608
  1.2 15.4 %copy-start.2 = (f32[32,64]{1,0:T(8,128)S(1)}, f32[32,64]{1,0:T(8,128)}, u32[]{:S(2)}) copy-start(f32[32,64]{1,0:T(8,128)} %week_factor.1) | copy-start | bytes 24580
  1.2 7.2 %collective-permute-start.1 = (s32[1,4]{1,0:T(1,128)}, s32[1,4]{1,0:T(1,128)S(1)}, u32[]{:S(2)}, u32[]{:S(2)}) collective-permute-start(s32[1,4]{1,0:T(1,128)} %bitcast.12), channel_id=1, source_target_pairs={{0,8},{4,12},{8,0},{12,4},{16,24},{20,28},{24,16},{28,20},{1,9},{5... | collective-permute-start | bytes 56 | tf_op jit(solution)/shard_map/ppermute | solution.py:195
  3.8 4.6 %collective-permute-start.2 = (s32[1,4]{1,0:T(1,128)}, s32[1,4]{1,0:T(1,128)S(1)}, u32[]{:S(2)}, u32[]{:S(2)}) collective-permute-start(s32[1,4]{1,0:T(1,128)} %bitcast.13), channel_id=1, source_target_pairs={{0,16},{4,20},{8,24},{12,28},{16,0},{20,4},{24,8},{28,12},{1,17},{... | collective-permute-start | bytes 56 | tf_op jit(solution)/shard_map/ppermute | solution.py:195
  5.3 4.6 %collective-permute-start.3 = (s32[1,4]{1,0:T(1,128)}, s32[1,4]{1,0:T(1,128)S(1)}, u32[]{:S(2)}, u32[]{:S(2)}) collective-permute-start(s32[1,4]{1,0:T(1,128)} %bitcast.14), channel_id=1, source_target_pairs={{0,24},{4,28},{8,16},{12,20},{16,8},{20,12},{24,0},{28,4},{1,25},{... | collective-permute-start | bytes 56 | tf_op jit(solution)/shard_map/ppermute | solution.py:195
  5.3 11.2 %collective-permute-start = (f32[64,512]{1,0:T(8,128)}, f32[64,512]{1,0:T(8,128)S(1)}, u32[]{:S(2)}, u32[]{:S(2)}) collective-permute-start(f32[64,512]{1,0:T(8,128)} %refs_0_.1), channel_id=1, source_target_pairs={{0,2},{1,3},{2,0},{3,1},{4,6},{5,7},{6,4},{7,5},{8,10},{9,11},{10,... | collective-permute-start | bytes 393224 | tf_op jit(solution)/shard_map/ppermute | solution.py:201
  8.4 10.6 %copy-start.3 = (s32[1,1,4]{2,1,0:T(1,128)S(1)}, s32[1,1,4]{2,1,0:T(1,128)}, u32[]{:S(2)}) copy-start(s32[1,1,4]{2,1,0:T(1,128)} %param.8) | copy-start | bytes 52
  10.7 7.6 %collective-permute-start.5 = (f32[64,512]{1,0:T(8,128)S(1)}, f32[64,512]{1,0:T(8,128)S(1)}, u32[]{:S(2)}, u32[]{:S(2)}) collective-permute-start(f32[64,512]{1,0:T(8,128)S(1)} %get-tuple-element.14._), channel_id=1, source_target_pairs={{0,8},{4,12},{8,0},{12,4},{16,24},{20,28},{24,16},{28,20},{1,9},{5... | collective-permute-start | bytes 393224 | tf_op jit(solution)/shard_map/ppermute | solution.py:195
  11.3 7.6 %collective-permute-start.6 = (f32[64,512]{1,0:T(8,128)S(1)}, f32[64,512]{1,0:T(8,128)S(1)}, u32[]{:S(2)}, u32[]{:S(2)}) collective-permute-start(f32[64,512]{1,0:T(8,128)S(1)} %get-tuple-element.17), channel_id=1, source_target_pairs={{0,16},{4,20},{8,24},{12,28},{16,0},{20,4},{24,8},{28,12},{1,17},{... | collective-permute-start | bytes 393224 | tf_op jit(solution)/shard_map/ppermute | solution.py:195
  12.3 6.6 %collective-permute-start.7 = (f32[64,512]{1,0:T(8,128)S(1)}, f32[64,512]{1,0:T(8,128)S(1)}, u32[]{:S(2)}, u32[]{:S(2)}) collective-permute-start(f32[64,512]{1,0:T(8,128)S(1)} %get-tuple-element.18), channel_id=1, source_target_pairs={{0,24},{4,28},{8,16},{12,20},{16,8},{20,12},{24,0},{28,4},{1,25},{... | collective-permute-start | bytes 393224 | tf_op jit(solution)/shard_map/ppermute | solution.py:195
  14.3 8.6 %collective-permute-start.10 = (f32[64,512]{1,0:T(8,128)S(1)}, f32[64,512]{1,0:T(8,128)S(1)}, u32[]{:S(2)}, u32[]{:S(2)}) collective-permute-start(f32[64,512]{1,0:T(8,128)S(1)} %copy-done.1), channel_id=1, source_target_pairs={{0,1},{1,0},{2,3},{3,2},{4,5},{5,4},{6,7},{7,6},{8,9},{9,8},{10,11... | collective-permute-start | bytes 393224 | tf_op jit(solution)/shard_map/ppermute | solution.py:201
  17.4 6.0 %collective-permute-start.11 = (f32[64,512]{1,0:T(8,128)S(1)}, f32[64,512]{1,0:T(8,128)S(1)}, u32[]{:S(2)}, u32[]{:S(2)}) collective-permute-start(f32[64,512]{1,0:T(8,128)S(1)} %get-tuple-element.22.refs_2_), channel_id=1, source_target_pairs={{0,1},{1,0},{2,3},{3,2},{4,5},{5,4},{6,7},{7,6},{8,9},{9,8},{10,11... | collective-permute-start | bytes 393224 | tf_op jit(solution)/shard_map/ppermute | solution.py:201
  20.4 8.1 %collective-permute-start.8 = (f32[2,64,512]{2,1,0:T(8,128)S(1)}, f32[2,64,512]{2,1,0:T(8,128)S(1)}, u32[]{:S(2)}, u32[]{:S(2)}) collective-permute-start(f32[2,64,512]{2,1,0:T(8,128)S(1)} %get-tuple-element.20), channel_id=1, source_target_pairs={{0,1},{1,0},{2,3},{3,2},{4,5},{5,4},{6,7},{7,6},{8,9},{9,8},{10,11... | collective-permute-start | bytes 786440 | tf_op jit(solution)/shard_map/ppermute | solution.py:201
  24.4 6.7 %collective-permute-start.12 = (f32[64,512]{1,0:T(8,128)S(1)}, f32[64,512]{1,0:T(8,128)S(1)}, u32[]{:S(2)}, u32[]{:S(2)}) collective-permute-start(f32[64,512]{1,0:T(8,128)S(1)} %mode2.1.refs_0_), channel_id=1, source_target_pairs={{0,8},{4,12},{8,0},{12,4},{16,24},{20,28},{24,16},{28,20},{1,9},{5... | collective-permute-start | bytes 393224 | tf_op jit(solution)/shard_map/ppermute | solution.py:195
  27.0 6.5 %collective-permute-start.13 = (f32[64,512]{1,0:T(8,128)S(1)}, f32[64,512]{1,0:T(8,128)S(1)}, u32[]{:S(2)}, u32[]{:S(2)}) collective-permute-start(f32[64,512]{1,0:T(8,128)S(1)} %mode2.1.refs_0_), channel_id=1, source_target_pairs={{0,16},{4,20},{8,24},{12,28},{16,0},{20,4},{24,8},{28,12},{1,17},{... | collective-permute-start | bytes 393224 | tf_op jit(solution)/shard_map/ppermute | solution.py:195
  27.0 6.5 %collective-permute-start.14 = (f32[64,512]{1,0:T(8,128)S(1)}, f32[64,512]{1,0:T(8,128)S(1)}, u32[]{:S(2)}, u32[]{:S(2)}) collective-permute-start(f32[64,512]{1,0:T(8,128)S(1)} %mode2.1.refs_0_), channel_id=1, source_target_pairs={{0,24},{4,28},{8,16},{12,20},{16,8},{20,12},{24,0},{28,4},{1,25},{... | collective-permute-start | bytes 393224 | tf_op jit(solution)/shard_map/ppermute | solution.py:195
  28.6 7.4 %collective-permute-start.9 = (f32[64,512]{1,0:T(8,128)S(1)}, f32[64,512]{1,0:T(8,128)S(1)}, u32[]{:S(2)}, u32[]{:S(2)}) collective-permute-start(f32[64,512]{1,0:T(8,128)S(1)} %get-tuple-element.26), channel_id=1, source_target_pairs={{0,2},{1,3},{2,0},{3,1},{4,6},{5,7},{6,4},{7,5},{8,10},{9,11},{10,... | collective-permute-start | bytes 393224 | tf_op jit(solution)/shard_map/ppermute | solution.py:201
  34.4 2.3 %collective-permute-start.15 = (f32[64,2048]{1,0:T(8,128)S(1)}, f32[64,2048]{1,0:T(8,128)S(1)}, u32[]{:S(2)}, u32[]{:S(2)}) collective-permute-start(f32[64,2048]{1,0:T(8,128)S(1)} %get-tuple-element.24), channel_id=1, source_target_pairs={{0,4},{4,0},{8,12},{12,8},{16,20},{20,16},{24,28},{28,24},{1,5},{5... | collective-permute-start | bytes 1572872 | tf_op jit(solution)/shard_map/ppermute | solution.py:198
where the time goes:
time: 37.9 us; the launch traced here: 37.5 us
  starting transfers between devices  22.9 us (60%)
  Pallas kernels  6.59 us (17%)
  waiting for transfers between devices  6.54 us (17%)
  between operations  1.43 us (4%)
    ppermute x9, starting transfers between devices, across_chips(): lax.ppermute(value, 'users', [(i, i ^ 2 * step) for i in range(rows)])  11.8 us
    ppermute x5, starting transfers between devices, across_groups(): return lax.ppermute(value, 'items', [(i, i ^ step) for i in range(groups)])  10.5 us
    ppermute x9, waiting for transfers between devices, across_chips(): lax.ppermute(value, 'users', [(i, i ^ 2 * step) for i in range(rows)])  4.51 us
    ppermute x5, waiting for transfers between devices, across_groups(): return lax.ppermute(value, 'items', [(i, i ^ step) for i in range(groups)])  2.03 us
    pallas_call x1, Pallas kernels, on_device(): pl.pallas_call(functools.partial(mode1_kernel, groups), out_shape=[array(...  1.44 us
    pallas_call x1, Pallas kernels, on_device(): pl.pallas_call(mode2_kernel, out_shape=array(rank, slots * width), in_spe...  1 us
    pallas_call x1, Pallas kernels, on_device(): pl.pallas_call(collect_kernel, out_shape=[array(*item_factor.shape)] * 2,...  0.96 us
    pallas_call x1, Pallas kernels, on_device(): pl.pallas_call(finish_items_kernel, out_shape=array(*item_factor.shape),...  0.85 us
  transfers between devices with their start and end apart: 16, of which 5 were waited for; matrix products, arithmetic and copies ran while one was open for 0% of the time, Pallas kernels for 15%

commit v1 on v0

--- a/solution.py
+++ b/solution.py
@@ -28,9 +28,10 @@
     done[...] = jnp.zeros_like(done)
 
 
-def prepare_kernel(count_ref, tiles, week_factor, users, _, halves, spread, users_out):
+def prepare_kernel(count_ref, tiles, week_factor, users, _, halves, spread, doubled, users_out):
     weeks, width = tiles.shape[1], tiles.shape[3]
     users_out[...] = users[...]
+    doubled[...] = jnp.concatenate([week_factor[...]] * 2, axis=1)
     weeks_t = week_factor[...].T
     for week in range(weeks):
         spread[week] = jnp.broadcast_to(weeks_t[:, week : week + 1], spread.shape[1:])
@@ -62,19 +63,28 @@
                     messages[step - 1][:, slot * width : (slot + 1) * width] = source[:, place]
 
 
-def user_term(spread, items, tile, together=8):
+def user_term(spread, doubled, items, tile, together=4):
     weeks, height, width = tile.shape
     rank = items.shape[0]
-    both = jnp.concatenate(split(items), axis=0)
-    both = jnp.concatenate([both, both], axis=1)
+    high, low = split(items)
+    flat = jnp.concatenate([high, low], axis=0)
+    both = jnp.concatenate([flat, flat], axis=1)
+    tall = jnp.concatenate([high.astype(F32), low.astype(F32)], axis=0).T.astype(BF16)
+    tall = jnp.concatenate([tall, tall], axis=0)
     total = jnp.zeros((rank, height), F32)
-    for week in range(0, weeks, together):
-        rows = tile[week : week + together].reshape(together * height, width)
-        sums = lax.dot_general(both, rows, (((1,), (1,)), ((), ())), preferred_element_type=F32)
+    turned = jnp.zeros((height, 2 * rank), F32)
+    for week in range(0, weeks, 2 * together):
+        middle = week + together
+        rows = tile[week:middle].reshape(together * height, width)
+        left = jnp.dot(rows, tall, preferred_element_type=F32)
+        rows = tile[middle : middle + together].reshape(together * height, width)
+        right = lax.dot_general(both, rows, (((1,), (1,)), ((), ())), preferred_element_type=F32)
         for part in range(together):
-            here = sums[:, part * height : (part + 1) * height]
-            total += (here[:rank] + here[rank:]) * spread[week + part]
-    return total
+            here = slice(part * height, (part + 1) * height)
+            turned += left[here] * doubled[week + part, :][None]
+            total += (right[:rank, here] + right[rank:, here]) * spread[middle + part]
+    turned = turned.T
+    return total + turned[:rank] + turned[rank:]
 
 
 def item_term(spread, users, tile):
@@ -95,7 +105,7 @@
     return half[:, :width] + half[:, width:]
 
 
-def mode1_kernel(groups, count_ref, users_ref, items_ref, spread, tiles, own, sibling, *refs):
+def mode1_kernel(groups, count_ref, users_ref, items_ref, spread, doubled, tiles, own, sibling, *refs):
     *messages, even, odd, sums = refs
     height, width = tiles.shape[2], tiles.shape[3] // 2
     me = lax.axis_index("users")
@@ -113,7 +123,7 @@
         here = columns(slot, width)
         for step, message in enumerate(messages):
             items = jnp.where(source == step + 1, message[:, here], items)
-        sums[users_ref[0, slot]] += user_term(spread, items, tiles.at[slot])
+        sums[users_ref[0, slot]] += user_term(spread, doubled, items, tiles.at[slot])
         return carry
 
     lax.fori_loop(0, count_ref[0, 0], work, 0)
@@ -164,13 +174,13 @@
                     target[:, place] += term[:, slot * width : (slot + 1) * width]
 
 
-def finish_users_kernel(kept, arrived, total, done):
+def finish_users_kernel(kept, arrived, total):
     total[...] = kept[...] + arrived[...]
-    done[...] = jnp.zeros_like(done)
-
-
-def finish_items_kernel(own, arrived, _, total):
-    total[...] = own[...] + arrived[...]
+
+
+def finish_items_kernel(own, arrived, users, items_out, users_out):
+    users_out[...] = users[...]
+    items_out[...] = own[...] + arrived[...]
 
 
 def on_device(sizes, tiles, user_blocks, item_blocks, counts, user_factor, item_factor, week_factor):
@@ -227,15 +237,16 @@
     )(near, item_factor, sibling, held)
     messages = [across_chips(value, step + 1) for step, value in enumerate(served)]
 
-    halves, spread, far_users = pl.pallas_call(
+    halves, spread, doubled, far_users = pl.pallas_call(
         prepare_kernel,
         out_shape=[
             array(slots, weeks, height, 2 * width, dtype=BF16),
             array(weeks, rank, height),
+            array(weeks, 2 * rank),
             array(rank, user_width),
         ],
         in_specs=[SMEM] + [VMEM] * 3 + [ANY],
-        out_specs=[VMEM] * 3,
+        out_specs=[VMEM] * 4,
         compiler_params=limit(24),
         name="prepare",
     )(counts, tiles, week_factor, far_users, served[0])
@@ -248,7 +259,7 @@
     even, odd = pl.pallas_call(
         functools.partial(mode1_kernel, groups),
         out_shape=[array(groups // 2, rank, user_width)] * 2,
-        in_specs=[SMEM] * 3 + [VMEM] * (3 + chips),
+        in_specs=[SMEM] * 3 + [VMEM] * (4 + chips),
         out_specs=[VMEM] * 2,
         scratch_shapes=[pltpu.VMEM((groups * user_width // height, rank, height), F32)],
         compiler_params=limit(8),
@@ -259,6 +270,7 @@
         user_blocks[0],
         item_blocks[0],
         spread,
+        doubled,
         halves,
         item_factor,
         sibling,
@@ -294,23 +306,23 @@
         arrived = across_groups(sent, step)
         kept, sent = kept[0::2] + arrived[0::2], kept[1::2] + arrived[1::2]
         step *= 2
-    m_users, done = pl.pallas_call(
+    users = pl.pallas_call(
         finish_users_kernel,
-        out_shape=[array(rank, user_width), array(8, 128)],
+        out_shape=array(rank, user_width),
         in_specs=[VMEM] * 2,
-        out_specs=[VMEM] * 2,
+        out_specs=VMEM,
         compiler_params=limit(4),
         cost_estimate=cost(4),
         name="finish_users",
     )(kept[0], across_groups(sent[0], step))
-    m_items = pl.pallas_call(
+    m_items, m_users = pl.pallas_call(
         finish_items_kernel,
-        out_shape=array(*item_factor.shape),
-        in_specs=[VMEM] * 2 + [ANY],
-        out_specs=VMEM,
+        out_shape=[array(*item_factor.shape), array(rank, user_width)],
+        in_specs=[VMEM] * 3,
+        out_specs=[VMEM] * 2,
         compiler_params=limit(4),
         name="finish_items",
-    )(own, across_cores(other), done)
+    )(own, across_cores(other), users)
     return m_users, m_items
 
 

time: 37.9 us -> 38.5 us (1.016); the launches traced: 37.5 us -> 39.1 us
  Pallas kernels: 6.59 us -> 11.2 us
  starting transfers between devices: 22.9 us -> 18.5 us
  waiting for transfers between devices: 6.54 us -> 7.83 us
    ppermute x5, starting transfers between devices: 10.5 us -> 6.65 us  [across_groups(): return lax.ppermute(value, 'items', [(i, i ^ step) for i in range(groups)])]
    pallas_call x1, Pallas kernels: 1.44 us -> 4.24 us  [on_device(): pl.pallas_call(functools.partial(mode1_kernel, groups), out_shape=[array(...]
    ppermute x5, waiting for transfers between devices: 2.03 us -> 4.16 us  [across_groups(): return lax.ppermute(value, 'items', [(i, i ^ step) for i in range(groups)])]
    pallas_call x1, Pallas kernels: 1 us -> 2.34 us  [on_device(): pl.pallas_call(mode2_kernel, out_shape=array(rank, slots * width), in_spe...]
    pallas_call x1, Pallas kernels: 0.84 us -> 1.93 us  [on_device(): pl.pallas_call(prepare_kernel, out_shape=[array(slots, weeks, height, 2 *...]
    ppermute x9, waiting for transfers between devices: 4.51 us -> 3.67 us  [across_chips(): lax.ppermute(value, 'users', [(i, i ^ 2 * step) for i in range(rows)])]
    pallas_call x2, Pallas kernels: 1.52 us -> 0.92 us  [the longest x1 0.9 us: on_device(): pl.pallas_call(finish_items_kernel, out_shape=[array(*item_factor.shape),...]
    ppermute x9, starting transfers between devices: 11.8 us -> 11.2 us  [across_chips(): lax.ppermute(value, 'users', [(i, i ^ 2 * step) for i in range(rows)])]
  transfers between devices with their start and end apart: 16 -> 16, of which waited for: 5 -> 7; matrix products, arithmetic and copies ran while one was open for 0% -> 0% of each run, Pallas kernels for 15% -> 26%
where the time goes in v1:
time: 38.5 us; the launch traced here: 39.1 us
  starting transfers between devices  18.5 us (48%)
  Pallas kernels  11.2 us (29%)
  waiting for transfers between devices  7.83 us (20%)
  between operations  1.48 us (4%)
    ppermute x9, starting transfers between devices, across_chips(): lax.ppermute(value, 'users', [(i, i ^ 2 * step) for i in range(rows)])  11.2 us
    ppermute x5, starting transfers between devices, across_groups(): return lax.ppermute(value, 'items', [(i, i ^ step) for i in range(groups)])  6.65 us
    pallas_call x1, Pallas kernels, on_device(): pl.pallas_call(functools.partial(mode1_kernel, groups), out_shape=[array(...  4.24 us
    ppermute x5, waiting for transfers between devices, across_groups(): return lax.ppermute(value, 'items', [(i, i ^ step) for i in range(groups)])  4.16 us
    ppermute x9, waiting for transfers between devices, across_chips(): lax.ppermute(value, 'users', [(i, i ^ 2 * step) for i in range(rows)])  3.67 us
    pallas_call x1, Pallas kernels, on_device(): pl.pallas_call(mode2_kernel, out_shape=array(rank, slots * width), in_spe...  2.34 us
    pallas_call x1, Pallas kernels, on_device(): pl.pallas_call(prepare_kernel, out_shape=[array(slots, weeks, height, 2 *...  1.93 us
    pallas_call x1, Pallas kernels, on_device(): pl.pallas_call(collect_kernel, out_shape=[array(*item_factor.shape)] * 2,...  0.96 us
  transfers between devices with their start and end apart: 16, of which 7 were waited for; matrix products, arithmetic and copies ran while one was open for 0% of the time, Pallas kernels for 26%

profile of v1, /device:TPU:0, one launch (start us, length us, event | category | flops | bytes accessed | tf_op | source)
XLA Modules:
  0.0 39.1 jit_solution(18402656220750140709)
XLA Ops:
  0.7 0.5 %collective-permute-start.4 = (f32[64,2048]{1,0:T(8,128)}, f32[64,2048]{1,0:T(8,128)S(1)}, u32[]{:S(2)}, u32[]{:S(2)}) collective-permute-start(f32[64,2048]{1,0:T(8,128)} %own.3), channel_id=1, source_target_pairs={{0,4},{4,0},{8,12},{12,8},{16,20},{20,16},{24,28},{28,24},{1,5},{5... | collective-permute-start | bytes 1572872 | tf_op jit(solution)/shard_map/ppermute | solution.py:208
  1.2 2.6 %collective-permute-start = (s32[1,4]{1,0:T(1,128)}, s32[1,4]{1,0:T(1,128)S(1)}, u32[]{:S(2)}, u32[]{:S(2)}) collective-permute-start(s32[1,4]{1,0:T(1,128)} %bitcast.12), channel_id=1, source_target_pairs={{0,8},{4,12},{8,0},{12,4},{16,24},{20,28},{24,16},{28,20},{1,9},{5... | collective-permute-start | bytes 56 | tf_op jit(solution)/shard_map/ppermute | solution.py:205
  3.8 1.5 %collective-permute-start.1 = (s32[1,4]{1,0:T(1,128)}, s32[1,4]{1,0:T(1,128)S(1)}, u32[]{:S(2)}, u32[]{:S(2)}) collective-permute-start(s32[1,4]{1,0:T(1,128)} %bitcast.13), channel_id=1, source_target_pairs={{0,16},{4,20},{8,24},{12,28},{16,0},{20,4},{24,8},{28,12},{1,17},{... | collective-permute-start | bytes 56 | tf_op jit(solution)/shard_map/ppermute | solution.py:205
  5.3 0.0 collective-permute-start.2
  5.3 3.0 %collective-permute-start.3 = (f32[64,512]{1,0:T(8,128)}, f32[64,512]{1,0:T(8,128)S(1)}, u32[]{:S(2)}, u32[]{:S(2)}) collective-permute-start(f32[64,512]{1,0:T(8,128)} %refs_0_.1), channel_id=1, source_target_pairs={{0,2},{1,3},{2,0},{3,1},{4,6},{5,7},{6,4},{7,5},{8,10},{9,11},{10,... | collective-permute-start | bytes 393224 | tf_op jit(solution)/shard_map/ppermute | solution.py:211
  8.4 1.5 %collective-permute-done.2 = s32[1,4]{1,0:T(1,128)S(1)} collective-permute-done((s32[1,4]{1,0:T(1,128)}, s32[1,4]{1,0:T(1,128)S(1)}, u32[]{:S(2)}, u32[]{:S(2)}) %collective-permute-start.2) | collective-permute-done | bytes 48 | tf_op jit(solution)/shard_map/ppermute | solution.py:205
  9.9 0.0 collective-permute-done.4.sibling
  9.9 0.8 %serve.1 = (f32[64,512]{1,0:T(8,128)S(1)}, f32[64,512]{1,0:T(8,128)S(1)}, f32[64,512]{1,0:T(8,128)S(1)}) custom-call(s32[4,4]{1,0:T(4,128)S(1)} %pad_add_fusion.requests.ids, f32[64,2048]{1,0:T(8,128)S(1)} %copy-done, f32[64,2048]{1,0:T(8,128)S(1)} %collective-permute-done.4.sibling, f32[8,128]{1,0:T(8,128)S(1)} %hold.1._), custom_call_target="tpu_custom_call" | custom-call | flops 1073741824 | bytes 8388608 | tf_op jit(solution)/shard_map/serve/pallas_call | solution.py:229
  10.7 0.6 %collective-permute-start.5 = (f32[64,512]{1,0:T(8,128)S(1)}, f32[64,512]{1,0:T(8,128)S(1)}, u32[]{:S(2)}, u32[]{:S(2)}) collective-permute-start(f32[64,512]{1,0:T(8,128)S(1)} %get-tuple-element.15._), channel_id=1, source_target_pairs={{0,8},{4,12},{8,0},{12,4},{16,24},{20,28},{24,16},{28,20},{1,9},{5... | collective-permute-start | bytes 393224 | tf_op jit(solution)/shard_map/ppermute | solution.py:205
  11.3 1.0 %collective-permute-start.6 = (f32[64,512]{1,0:T(8,128)S(1)}, f32[64,512]{1,0:T(8,128)S(1)}, u32[]{:S(2)}, u32[]{:S(2)}) collective-permute-start(f32[64,512]{1,0:T(8,128)S(1)} %get-tuple-element.19), channel_id=1, source_target_pairs={{0,16},{4,20},{8,24},{12,28},{16,0},{20,4},{24,8},{28,12},{1,17},{... | collective-permute-start | bytes 393224 | tf_op jit(solution)/shard_map/ppermute | solution.py:205
  12.3 1.9 %collective-permute-start.7 = (f32[64,512]{1,0:T(8,128)S(1)}, f32[64,512]{1,0:T(8,128)S(1)}, u32[]{:S(2)}, u32[]{:S(2)}) collective-permute-start(f32[64,512]{1,0:T(8,128)S(1)} %get-tuple-element.20), channel_id=1, source_target_pairs={{0,24},{4,28},{8,16},{12,20},{16,8},{20,12},{24,0},{28,4},{1,25},{... | collective-permute-start | bytes 393224 | tf_op jit(solution)/shard_map/ppermute | solution.py:205
  14.3 1.6 %collective-permute-start.8 = (f32[64,512]{1,0:T(8,128)S(1)}, f32[64,512]{1,0:T(8,128)S(1)}, u32[]{:S(2)}, u32[]{:S(2)}) collective-permute-start(f32[64,512]{1,0:T(8,128)S(1)} %copy-done.1), channel_id=1, source_target_pairs={{0,1},{1,0},{2,3},{3,2},{4,5},{5,4},{6,7},{7,6},{8,9},{9,8},{10,11... | collective-permute-start | bytes 393224 | tf_op jit(solution)/shard_map/ppermute | solution.py:211
  16.5 0.0 collective-permute-done.3.users
  16.6 1.9 %prepare.1 = (bf16[4,32,128,256]{3,2,1,0:T(8,128)(2,1)S(1)}, f32[32,64,128]{2,1,0:T(8,128)S(1)}, f32[32,128]{1,0:T(8,128)S(1)}, f32[64,512]{1,0:T(8,128)S(1)}) custom-call(s32[1,1]{1,0:T(1,128)S(6)} %copy.9.count_ref, f32[4,32,128,128]{3,2,1,0:T(8,128)S(1)} %bitcast.9, f32[32,64]{1,0:T(8,128)S(1)} %copy-done.2, f32[64,512]{1,0:T(8,128)S(1)} %collective-permute-done.3.users, ...), custom_call_target="tpu_custom_call" | custom-call | tf_op jit(solution)/shard_map/prepare/pallas_call | solution.py:240
  18.5 0.1 collective-permute-start.9
  18.6 0.4 collective-permute-done.6.refs_1_
  19.0 0.0 collective-permute-done.7.refs_2_
  19.0 4.2 %mode1.1 = (f32[2,64,512]{2,1,0:T(8,128)S(1)}, f32[2,64,512]{2,1,0:T(8,128)S(1)}) custom-call(s32[1,1]{1,0:T(1,128)S(6)} %copy.9.count_ref, s32[1,4]{1,0:T(1,128)S(1)} %bitcast.10, s32[1,4]{1,0:T(1,128)S(1)} %bitcast.16, f32[32,64,128]{2,1,0:T(8,128)S(1)} %get-tuple-element.16.spread, f32[32,128]{1,0:T(8,128)S(1)} %get-tuple-element.18.doubled, ...), custom_call_target="tpu_custom_call" | custom-call | flops 1073741824 | bytes 8388608 | tf_op jit(solution)/shard_map/mode1/pallas_call | solution.py:259
  23.2 0.1 collective-permute-start.14
  23.3 0.2 collective-permute-done.9.refs_3_
  23.5 2.3 %mode2.1.refs_0_ = f32[64,512]{1,0:T(8,128)S(1)} custom-call(s32[1,1]{1,0:T(1,128)S(6)} %copy.9.count_ref, s32[1,4]{1,0:T(1,128)S(1)} %bitcast.11, f32[32,64,128]{2,1,0:T(8,128)S(1)} %get-tuple-element.16.spread, bf16[4,32,128,256]{3,2,1,0:T(8,128)(2,1)S(1)} %get-tuple-element.17.tiles, f32[2,64,512]{2,1,0:T(8,128)S(1)} %get-tuple-element.21._, ...), custom_call_target="tpu_custom_call" | custom-call | flops 2147483648 | bytes 16777216 | tf_op jit(solution)/shard_map/mode2/pallas_call | solution.py:279
  25.9 0.1 collective-permute-start.10
  26.0 0.6 %collective-permute-start.11 = (f32[64,512]{1,0:T(8,128)S(1)}, f32[64,512]{1,0:T(8,128)S(1)}, u32[]{:S(2)}, u32[]{:S(2)}) collective-permute-start(f32[64,512]{1,0:T(8,128)S(1)} %mode2.1.refs_0_), channel_id=1, source_target_pairs={{0,16},{4,20},{8,24},{12,28},{16,0},{20,4},{24,8},{28,12},{1,17},{... | collective-permute-start | bytes 393224 | tf_op jit(solution)/shard_map/ppermute | solution.py:205
  26.5 2.9 %collective-permute-start.12 = (f32[64,512]{1,0:T(8,128)S(1)}, f32[64,512]{1,0:T(8,128)S(1)}, u32[]{:S(2)}, u32[]{:S(2)}) collective-permute-start(f32[64,512]{1,0:T(8,128)S(1)} %mode2.1.refs_0_), channel_id=1, source_target_pairs={{0,24},{4,28},{8,16},{12,20},{16,8},{20,12},{24,0},{28,4},{1,25},{... | collective-permute-start | bytes 393224 | tf_op jit(solution)/shard_map/ppermute | solution.py:205
  29.4 0.4 %collective-permute-done.14 = f32[2,64,512]{2,1,0:T(8,128)S(1)} collective-permute-done((f32[2,64,512]{2,1,0:T(8,128)S(1)}, f32[2,64,512]{2,1,0:T(8,128)S(1)}, u32[]{:S(2)}, u32[]{:S(2)}) %collective-permute-start.14) | collective-permute-done | bytes 262176 | tf_op jit(solution)/shard_map/ppermute | solution.py:211
  29.9 1.9 %collective-permute-start.15 = (f32[64,512]{1,0:T(8,128)S(1)}, f32[64,512]{1,0:T(8,128)S(1)}, u32[]{:S(2)}, u32[]{:S(2)}) collective-permute-start(f32[64,512]{1,0:T(8,128)S(1)} %get-tuple-element.28), channel_id=1, source_target_pairs={{0,2},{1,3},{2,0},{3,1},{4,6},{5,7},{6,4},{7,5},{8,10},{9,11},{10,... | collective-permute-start | bytes 393224 | tf_op jit(solution)/shard_map/ppermute | solution.py:211
  31.8 0.2 collective-permute-done.10.refs_1_
  31.9 1.6 %collective-permute-done.11.refs_2_ = f32[64,512]{1,0:T(8,128)S(1)} collective-permute-done((f32[64,512]{1,0:T(8,128)S(1)}, f32[64,512]{1,0:T(8,128)S(1)}, u32[]{:S(2)}, u32[]{:S(2)}) %collective-permute-start.11) | collective-permute-done | bytes 131104 | tf_op jit(solution)/shard_map/ppermute | solution.py:205
  33.6 1.0 %collect.1 = (f32[64,2048]{1,0:T(8,128)S(1)}, f32[64,2048]{1,0:T(8,128)S(1)}) custom-call(s32[4,4]{1,0:T(4,128)S(1)} %pad_add_fusion.requests.ids, f32[64,512]{1,0:T(8,128)S(1)} %mode2.1.refs_0_, f32[64,512]{1,0:T(8,128)S(1)} %collective-permute-done.10.refs_1_, f32[64,512]{1,0:T(8,128)S(1)} %collective-permute-done.11.refs_2_, ...), custom_call_target="tpu_custom_call" | custom-call | tf_op jit(solution)/shard_map/collect/pallas_call | solution.py:296
  34.5 0.1 collective-permute-start.13
  34.6 3.5 %collective-permute-done.15.arrived = f32[64,512]{1,0:T(8,128)S(1)} collective-permute-done((f32[64,512]{1,0:T(8,128)S(1)}, f32[64,512]{1,0:T(8,128)S(1)}, u32[]{:S(2)}, u32[]{:S(2)}) %collective-permute-start.15) | collective-permute-done | bytes 131104 | tf_op jit(solution)/shard_map/ppermute | solution.py:211
  38.2 0.9 %finish_items.1 = (f32[64,2048]{1,0:T(8,128)}, f32[64,512]{1,0:T(8,128)}) custom-call(f32[64,2048]{1,0:T(8,128)S(1)} %get-tuple-element.23.own, f32[64,2048]{1,0:T(8,128)S(1)} %collective-permute-done.13.arrived, f32[64,512]{1,0:T(8,128)S(1)} %finish_users.1.users), custom_call_target="tpu_custom_call" | custom-call | tf_op jit(solution)/shard_map/finish_items/pallas_call | solution.py:318
  (25 shorter events, 0.1 us)
Async XLA Ops:
  0.6 9.3 %copy-start = (f32[64,2048]{1,0:T(8,128)S(1)}, f32[64,2048]{1,0:T(8,128)}, u32[]{:S(2)}) copy-start(f32[64,2048]{1,0:T(8,128)} %own.3) | copy-start | bytes 1572868
  0.6 9.2 %copy-start.4 = (s32[1,1,4]{2,1,0:T(1,128)S(1)}, s32[1,1,4]{2,1,0:T(1,128)}, u32[]{:S(2)}) copy-start(s32[1,1,4]{2,1,0:T(1,128)} %param.9) | copy-start | bytes 52
  0.7 9.2 %collective-permute-start.4 = (f32[64,2048]{1,0:T(8,128)}, f32[64,2048]{1,0:T(8,128)S(1)}, u32[]{:S(2)}, u32[]{:S(2)}) collective-permute-start(f32[64,2048]{1,0:T(8,128)} %own.3), channel_id=1, source_target_pairs={{0,4},{4,0},{8,12},{12,8},{16,20},{20,16},{24,28},{28,24},{1,5},{5... | collective-permute-start | bytes 1572872 | tf_op jit(solution)/shard_map/ppermute | solution.py:208
  1.2 15.4 %slice-start = ((s8[8388608]{0:T(1024)(128)(4,1)}), s8[4194304]{0:T(1024)(128)(4,1)S(1)}, s32[]{:S(2)}) async-start(s8[8388608]{0:T(1024)(128)(4,1)} %bitcast.7), calls=%async_computation | async-start | bytes 8388608
  1.2 13.1 %copy-start.1 = (f32[64,512]{1,0:T(8,128)S(1)}, f32[64,512]{1,0:T(8,128)}, u32[]{:S(2)}) copy-start(f32[64,512]{1,0:T(8,128)} %refs_0_.1) | copy-start | bytes 393220
  1.2 15.4 %slice-start.1 = ((s8[8388608]{0:T(1024)(128)(4,1)}), s8[4194304]{0:T(1024)(128)(4,1)S(1)}, s32[]{:S(2)}) async-start(s8[8388608]{0:T(1024)(128)(4,1)} %bitcast.7), calls=%async_computation.1 | async-start | bytes 8388608
  1.2 15.4 %copy-start.2 = (f32[32,64]{1,0:T(8,128)S(1)}, f32[32,64]{1,0:T(8,128)}, u32[]{:S(2)}) copy-start(f32[32,64]{1,0:T(8,128)} %week_factor.1) | copy-start | bytes 24580
  1.2 7.2 %collective-permute-start = (s32[1,4]{1,0:T(1,128)}, s32[1,4]{1,0:T(1,128)S(1)}, u32[]{:S(2)}, u32[]{:S(2)}) collective-permute-start(s32[1,4]{1,0:T(1,128)} %bitcast.12), channel_id=1, source_target_pairs={{0,8},{4,12},{8,0},{12,4},{16,24},{20,28},{24,16},{28,20},{1,9},{5... | collective-permute-start | bytes 56 | tf_op jit(solution)/shard_map/ppermute | solution.py:205
  3.8 4.6 %collective-permute-start.1 = (s32[1,4]{1,0:T(1,128)}, s32[1,4]{1,0:T(1,128)S(1)}, u32[]{:S(2)}, u32[]{:S(2)}) collective-permute-start(s32[1,4]{1,0:T(1,128)} %bitcast.13), channel_id=1, source_target_pairs={{0,16},{4,20},{8,24},{12,28},{16,0},{20,4},{24,8},{28,12},{1,17},{... | collective-permute-start | bytes 56 | tf_op jit(solution)/shard_map/ppermute | solution.py:205
  5.3 4.6 %collective-permute-start.2 = (s32[1,4]{1,0:T(1,128)}, s32[1,4]{1,0:T(1,128)S(1)}, u32[]{:S(2)}, u32[]{:S(2)}) collective-permute-start(s32[1,4]{1,0:T(1,128)} %bitcast.14), channel_id=1, source_target_pairs={{0,24},{4,28},{8,16},{12,20},{16,8},{20,12},{24,0},{28,4},{1,25},{... | collective-permute-start | bytes 56 | tf_op jit(solution)/shard_map/ppermute | solution.py:205
  5.3 11.2 %collective-permute-start.3 = (f32[64,512]{1,0:T(8,128)}, f32[64,512]{1,0:T(8,128)S(1)}, u32[]{:S(2)}, u32[]{:S(2)}) collective-permute-start(f32[64,512]{1,0:T(8,128)} %refs_0_.1), channel_id=1, source_target_pairs={{0,2},{1,3},{2,0},{3,1},{4,6},{5,7},{6,4},{7,5},{8,10},{9,11},{10,... | collective-permute-start | bytes 393224 | tf_op jit(solution)/shard_map/ppermute | solution.py:211
  8.4 10.6 %copy-start.3 = (s32[1,1,4]{2,1,0:T(1,128)S(1)}, s32[1,1,4]{2,1,0:T(1,128)}, u32[]{:S(2)}) copy-start(s32[1,1,4]{2,1,0:T(1,128)} %param.8) | copy-start | bytes 52
  10.7 7.9 %collective-permute-start.5 = (f32[64,512]{1,0:T(8,128)S(1)}, f32[64,512]{1,0:T(8,128)S(1)}, u32[]{:S(2)}, u32[]{:S(2)}) collective-permute-start(f32[64,512]{1,0:T(8,128)S(1)} %get-tuple-element.15._), channel_id=1, source_target_pairs={{0,8},{4,12},{8,0},{12,4},{16,24},{20,28},{24,16},{28,20},{1,9},{5... | collective-permute-start | bytes 393224 | tf_op jit(solution)/shard_map/ppermute | solution.py:205
  11.3 7.6 %collective-permute-start.6 = (f32[64,512]{1,0:T(8,128)S(1)}, f32[64,512]{1,0:T(8,128)S(1)}, u32[]{:S(2)}, u32[]{:S(2)}) collective-permute-start(f32[64,512]{1,0:T(8,128)S(1)} %get-tuple-element.19), channel_id=1, source_target_pairs={{0,16},{4,20},{8,24},{12,28},{16,0},{20,4},{24,8},{28,12},{1,17},{... | collective-permute-start | bytes 393224 | tf_op jit(solution)/shard_map/ppermute | solution.py:205
  12.3 6.6 %collective-permute-start.7 = (f32[64,512]{1,0:T(8,128)S(1)}, f32[64,512]{1,0:T(8,128)S(1)}, u32[]{:S(2)}, u32[]{:S(2)}) collective-permute-start(f32[64,512]{1,0:T(8,128)S(1)} %get-tuple-element.20), channel_id=1, source_target_pairs={{0,24},{4,28},{8,16},{12,20},{16,8},{20,12},{24,0},{28,4},{1,25},{... | collective-permute-start | bytes 393224 | tf_op jit(solution)/shard_map/ppermute | solution.py:205
  14.3 9.0 %collective-permute-start.8 = (f32[64,512]{1,0:T(8,128)S(1)}, f32[64,512]{1,0:T(8,128)S(1)}, u32[]{:S(2)}, u32[]{:S(2)}) collective-permute-start(f32[64,512]{1,0:T(8,128)S(1)} %copy-done.1), channel_id=1, source_target_pairs={{0,1},{1,0},{2,3},{3,2},{4,5},{5,4},{6,7},{7,6},{8,9},{9,8},{10,11... | collective-permute-start | bytes 393224 | tf_op jit(solution)/shard_map/ppermute | solution.py:211
  18.5 5.0 %collective-permute-start.9 = (f32[64,512]{1,0:T(8,128)S(1)}, f32[64,512]{1,0:T(8,128)S(1)}, u32[]{:S(2)}, u32[]{:S(2)}) collective-permute-start(f32[64,512]{1,0:T(8,128)S(1)} %get-tuple-element.22.refs_2_), channel_id=1, source_target_pairs={{0,1},{1,0},{2,3},{3,2},{4,5},{5,4},{6,7},{7,6},{8,9},{9,8},{10,11... | collective-permute-start | bytes 393224 | tf_op jit(solution)/shard_map/ppermute | solution.py:211
  23.2 6.6 %collective-permute-start.14 = (f32[2,64,512]{2,1,0:T(8,128)S(1)}, f32[2,64,512]{2,1,0:T(8,128)S(1)}, u32[]{:S(2)}, u32[]{:S(2)}) collective-permute-start(f32[2,64,512]{2,1,0:T(8,128)S(1)} %get-tuple-element.25), channel_id=1, source_target_pairs={{0,1},{1,0},{2,3},{3,2},{4,5},{5,4},{6,7},{7,6},{8,9},{9,8},{10,11... | collective-permute-start | bytes 786440 | tf_op jit(solution)/shard_map/ppermute | solution.py:211
  25.9 6.0 %collective-permute-start.10 = (f32[64,512]{1,0:T(8,128)S(1)}, f32[64,512]{1,0:T(8,128)S(1)}, u32[]{:S(2)}, u32[]{:S(2)}) collective-permute-start(f32[64,512]{1,0:T(8,128)S(1)} %mode2.1.refs_0_), channel_id=1, source_target_pairs={{0,8},{4,12},{8,0},{12,4},{16,24},{20,28},{24,16},{28,20},{1,9},{5... | collective-permute-start | bytes 393224 | tf_op jit(solution)/shard_map/ppermute | solution.py:205
  26.0 7.6 %collective-permute-start.11 = (f32[64,512]{1,0:T(8,128)S(1)}, f32[64,512]{1,0:T(8,128)S(1)}, u32[]{:S(2)}, u32[]{:S(2)}) collective-permute-start(f32[64,512]{1,0:T(8,128)S(1)} %mode2.1.refs_0_), channel_id=1, source_target_pairs={{0,16},{4,20},{8,24},{12,28},{16,0},{20,4},{24,8},{28,12},{1,17},{... | collective-permute-start | bytes 393224 | tf_op jit(solution)/shard_map/ppermute | solution.py:205
  26.5 7.0 %collective-permute-start.12 = (f32[64,512]{1,0:T(8,128)S(1)}, f32[64,512]{1,0:T(8,128)S(1)}, u32[]{:S(2)}, u32[]{:S(2)}) collective-permute-start(f32[64,512]{1,0:T(8,128)S(1)} %mode2.1.refs_0_), channel_id=1, source_target_pairs={{0,24},{4,28},{8,16},{12,20},{16,8},{20,12},{24,0},{28,4},{1,25},{... | collective-permute-start | bytes 393224 | tf_op jit(solution)/shard_map/ppermute | solution.py:205
  29.9 8.2 %collective-permute-start.15 = (f32[64,512]{1,0:T(8,128)S(1)}, f32[64,512]{1,0:T(8,128)S(1)}, u32[]{:S(2)}, u32[]{:S(2)}) collective-permute-start(f32[64,512]{1,0:T(8,128)S(1)} %get-tuple-element.28), channel_id=1, source_target_pairs={{0,2},{1,3},{2,0},{3,1},{4,6},{5,7},{6,4},{7,5},{8,10},{9,11},{10,... | collective-permute-start | bytes 393224 | tf_op jit(solution)/shard_map/ppermute | solution.py:211
  34.5 3.6 %collective-permute-start.13 = (f32[64,2048]{1,0:T(8,128)S(1)}, f32[64,2048]{1,0:T(8,128)S(1)}, u32[]{:S(2)}, u32[]{:S(2)}) collective-permute-start(f32[64,2048]{1,0:T(8,128)S(1)} %get-tuple-element.24), channel_id=1, source_target_pairs={{0,4},{4,0},{8,12},{12,8},{16,20},{20,16},{24,28},{28,24},{1,5},{5... | collective-permute-start | bytes 1572872 | tf_op jit(solution)/shard_map/ppermute | solution.py:208

commit v2 on v1

--- a/solution.py
+++ b/solution.py
@@ -28,10 +28,9 @@
     done[...] = jnp.zeros_like(done)
 
 
-def prepare_kernel(count_ref, tiles, week_factor, users, _, halves, spread, doubled, users_out):
+def prepare_kernel(count_ref, tiles, week_factor, users, _, halves, spread, users_out):
     weeks, width = tiles.shape[1], tiles.shape[3]
     users_out[...] = users[...]
-    doubled[...] = jnp.concatenate([week_factor[...]] * 2, axis=1)
     weeks_t = week_factor[...].T
     for week in range(weeks):
         spread[week] = jnp.broadcast_to(weeks_t[:, week : week + 1], spread.shape[1:])
@@ -63,49 +62,45 @@
                     messages[step - 1][:, slot * width : (slot + 1) * width] = source[:, place]
 
 
-def user_term(spread, doubled, items, tile, together=4):
-    weeks, height, width = tile.shape
-    rank = items.shape[0]
-    high, low = split(items)
-    flat = jnp.concatenate([high, low], axis=0)
-    both = jnp.concatenate([flat, flat], axis=1)
-    tall = jnp.concatenate([high.astype(F32), low.astype(F32)], axis=0).T.astype(BF16)
-    tall = jnp.concatenate([tall, tall], axis=0)
-    total = jnp.zeros((rank, height), F32)
-    turned = jnp.zeros((height, 2 * rank), F32)
-    for week in range(0, weeks, 2 * together):
-        middle = week + together
-        rows = tile[week:middle].reshape(together * height, width)
-        left = jnp.dot(rows, tall, preferred_element_type=F32)
-        rows = tile[middle : middle + together].reshape(together * height, width)
-        right = lax.dot_general(both, rows, (((1,), (1,)), ((), ())), preferred_element_type=F32)
-        for part in range(together):
-            here = slice(part * height, (part + 1) * height)
-            turned += left[here] * doubled[week + part, :][None]
-            total += (right[:rank, here] + right[rank:, here]) * spread[middle + part]
-    turned = turned.T
-    return total + turned[:rank] + turned[rank:]
-
-
-def item_term(spread, users, tile):
+def quarters(sums, size):
+    total = pltpu.matmul_pop(sums[0])
+    for other in sums[1:]:
+        total += pltpu.matmul_pop(other)
+    half = total[: total.shape[0] // 2] + total[total.shape[0] // 2 :]
+    return half[:, :size] + half[:, size:]
+
+
+def multiply(sums, at, left, right, transpose):
+    unit, stage = at % len(sums), at // len(sums) % 2
+    pltpu.matmul_push_rhs(right, stage, unit, transpose=transpose)
+    pltpu.matmul_acc_lhs(sums[unit], left, load_staged_rhs=stage)
+
+
+def user_term(spread, items, tile, sums):
     weeks, height, width = tile.shape
     width //= 2
-    rank = users.shape[0]
-    total = jnp.zeros((2 * rank, 2 * width), F32)
-    for week in range(0, weeks, 2):
+    for at in range(weeks // 2):
+        left, right = [], []
+        for part in (2 * at, 2 * at + 1):
+            left.append(jnp.concatenate(split(spread[part] * items), axis=0))
+            right.append(jnp.concatenate([tile[part, :, :width], tile[part, :, width:]], axis=0))
+        left, right = jnp.concatenate(left, axis=1), jnp.concatenate(right, axis=1)
+        multiply(sums, at, left, right, True)
+    return quarters(sums, height)
+
+
+def item_term(spread, users, tile, sums):
+    weeks, height, width = tile.shape
+    for at in range(weeks // 2):
         left = [
-            jnp.concatenate(split(spread[part] * users), axis=0) for part in (week, week + 1)
+            jnp.concatenate(split(spread[part] * users), axis=0) for part in (2 * at, 2 * at + 1)
         ]
-        total += jnp.dot(
-            jnp.concatenate(left, axis=1),
-            jnp.concatenate([tile[week], tile[week + 1]], axis=0),
-            preferred_element_type=F32,
-        )
-    half = total[:rank] + total[rank:]
-    return half[:, :width] + half[:, width:]
-
-
-def mode1_kernel(groups, count_ref, users_ref, items_ref, spread, doubled, tiles, own, sibling, *refs):
+        right = tile[2 * at : 2 * at + 2].reshape(2 * height, width)
+        multiply(sums, at, jnp.concatenate(left, axis=1), right, False)
+    return quarters(sums, width // 2)
+
+
+def mode1_kernel(groups, units, count_ref, users_ref, items_ref, spread, tiles, own, sibling, *refs):
     *messages, even, odd, sums = refs
     height, width = tiles.shape[2], tiles.shape[3] // 2
     me = lax.axis_index("users")
@@ -123,7 +118,9 @@
         here = columns(slot, width)
         for step, message in enumerate(messages):
             items = jnp.where(source == step + 1, message[:, here], items)
-        sums[users_ref[0, slot]] += user_term(spread, doubled, items, tiles.at[slot])
+        sums[users_ref[0, slot]] += pl.run_scoped(
+            lambda *held: user_term(spread, items, tiles.at[slot], held), *units
+        )
         return carry
 
     lax.fori_loop(0, count_ref[0, 0], work, 0)
@@ -134,7 +131,7 @@
             target[step // 2, :, block * height : (block + 1) * height] = sums[first + block]
 
 
-def mode2_kernel(count_ref, users_ref, spread, tiles, _, *refs):
+def mode2_kernel(units, count_ref, users_ref, spread, tiles, _, *refs):
     *factors, terms = refs
     height, width = tiles.shape[2], tiles.shape[3] // 2
     column = lax.axis_index("items")
@@ -148,7 +145,9 @@
         users = factors[0][:, place]
         for step in range(1, len(factors)):
             users = jnp.where(source == step, factors[step][:, place], users)
-        terms[:, columns(slot, width)] = item_term(spread, users, tiles.at[slot])
+        terms[:, columns(slot, width)] = pl.run_scoped(
+            lambda *held: item_term(spread, users, tiles.at[slot], held), *units
+        )
         return carry
 
     lax.fori_loop(0, count_ref[0, 0], work, 0)
@@ -183,8 +182,8 @@
     items_out[...] = own[...] + arrived[...]
 
 
-def on_device(sizes, tiles, user_blocks, item_blocks, counts, user_factor, item_factor, week_factor):
-    rows, groups = sizes
+def on_device(mesh, tiles, user_blocks, item_blocks, counts, user_factor, item_factor, week_factor):
+    rows, groups = mesh.shape["users"], mesh.shape["items"]
     chips = rows // 2
     tiles = tiles[0, 0]
     slots, weeks, height, width = tiles.shape
@@ -200,6 +199,9 @@
             bytes_accessed=int(times * 4 * slots * weeks * height * width),
             transcendentals=0,
         )
+
+    with jax.sharding.use_abstract_mesh(mesh.abstract_mesh):
+        units = [pltpu.ACC(unit)((2 * rank, 2 * width), F32) for unit in range(2)]
 
     def across_chips(value, step):
         return lax.ppermute(value, "users", [(i, i ^ (2 * step)) for i in range(rows)])
@@ -237,16 +239,15 @@
     )(near, item_factor, sibling, held)
     messages = [across_chips(value, step + 1) for step, value in enumerate(served)]
 
-    halves, spread, doubled, far_users = pl.pallas_call(
+    halves, spread, far_users = pl.pallas_call(
         prepare_kernel,
         out_shape=[
             array(slots, weeks, height, 2 * width, dtype=BF16),
             array(weeks, rank, height),
-            array(weeks, 2 * rank),
             array(rank, user_width),
         ],
         in_specs=[SMEM] + [VMEM] * 3 + [ANY],
-        out_specs=[VMEM] * 4,
+        out_specs=[VMEM] * 3,
         compiler_params=limit(24),
         name="prepare",
     )(counts, tiles, week_factor, far_users, served[0])
@@ -257,9 +258,9 @@
         step //= 2
 
     even, odd = pl.pallas_call(
-        functools.partial(mode1_kernel, groups),
+        functools.partial(mode1_kernel, groups, units),
         out_shape=[array(groups // 2, rank, user_width)] * 2,
-        in_specs=[SMEM] * 3 + [VMEM] * (4 + chips),
+        in_specs=[SMEM] * 3 + [VMEM] * (3 + chips),
         out_specs=[VMEM] * 2,
         scratch_shapes=[pltpu.VMEM((groups * user_width // height, rank, height), F32)],
         compiler_params=limit(8),
@@ -270,14 +271,13 @@
         user_blocks[0],
         item_blocks[0],
         spread,
-        doubled,
         halves,
         item_factor,
         sibling,
         *messages,
     )
     terms = pl.pallas_call(
-        mode2_kernel,
+        functools.partial(mode2_kernel, units),
         out_shape=array(rank, slots * width),
         in_specs=[SMEM] * 2 + [VMEM] * 2 + [ANY] + [VMEM] * groups,
         out_specs=VMEM,
@@ -330,7 +330,7 @@
     rows, groups = mesh.shape["users"], mesh.shape["items"]
     assert rows > 1 and rows & (rows - 1) == 0 and groups > 1 and groups & (groups - 1) == 0
     return jax.shard_map(
-        functools.partial(on_device, (rows, groups)),
+        functools.partial(on_device, mesh),
         mesh=mesh,
         in_specs=(
             P("users", "items", None, None, None, None),

time: 38.5 us -> 37.5 us (0.974)
  starting transfers between devices: 18.5 us -> 23.2 us
  Pallas kernels: 11.2 us -> 7.55 us
  waiting for transfers between devices: 7.83 us -> 5.41 us
    ppermute x5, starting transfers between devices: 6.65 us -> 11.4 us  [across_groups(): return lax.ppermute(value, 'items', [(i, i ^ step) for i in range(groups)])]
    pallas_call x2, Pallas kernels: 6.58 us -> 3.64 us  [the longest x1 2.19 us: on_device(): pl.pallas_call(functools.partial(mode1_kernel, groups, units), out_shape=...]
    ppermute x5, waiting for transfers between devices: 4.16 us -> 2.51 us  [across_groups(): return lax.ppermute(value, 'items', [(i, i ^ step) for i in range(groups)])]
    ppermute x9, waiting for transfers between devices: 3.67 us -> 2.89 us  [across_chips(): lax.ppermute(value, 'users', [(i, i ^ 2 * step) for i in range(rows)])]
    pallas_call x1, Pallas kernels: 1.93 us -> 1.2 us  [on_device(): pl.pallas_call(prepare_kernel, out_shape=[array(slots, weeks, height, 2 *...]
  transfers between devices with their start and end apart: 16 -> 16, of which waited for: 7 -> 3; matrix products, arithmetic and copies ran while one was open for 0% -> 0% of each run, Pallas kernels for 26% -> 18%
where the time goes in v2:
time: 37.5 us; the launch traced here: 37.7 us
  starting transfers between devices  23.2 us (62%)
  Pallas kernels  7.55 us (20%)
  waiting for transfers between devices  5.41 us (14%)
  between operations  1.45 us (4%)
    ppermute x5, starting transfers between devices, across_groups(): return lax.ppermute(value, 'items', [(i, i ^ step) for i in range(groups)])  11.4 us
    ppermute x9, starting transfers between devices, across_chips(): lax.ppermute(value, 'users', [(i, i ^ 2 * step) for i in range(rows)])  11.2 us
    ppermute x9, waiting for transfers between devices, across_chips(): lax.ppermute(value, 'users', [(i, i ^ 2 * step) for i in range(rows)])  2.89 us
    ppermute x5, waiting for transfers between devices, across_groups(): return lax.ppermute(value, 'items', [(i, i ^ step) for i in range(groups)])  2.51 us
    pallas_call x1, Pallas kernels, on_device(): pl.pallas_call(functools.partial(mode1_kernel, groups, units), out_shape=...  2.19 us
    pallas_call x1, Pallas kernels, on_device(): pl.pallas_call(functools.partial(mode2_kernel, units), out_shape=array(ra...  1.45 us
    pallas_call x1, Pallas kernels, on_device(): pl.pallas_call(prepare_kernel, out_shape=[array(slots, weeks, height, 2 *...  1.2 us
    pallas_call x1, Pallas kernels, on_device(): pl.pallas_call(collect_kernel, out_shape=[array(*item_factor.shape)] * 2,...  0.96 us
  transfers between devices with their start and end apart: 16, of which 3 were waited for; matrix products, arithmetic and copies ran while one was open for 0% of the time, Pallas kernels for 18%

profile of v2, /device:TPU:0, one launch (start us, length us, event | category | flops | bytes accessed | tf_op | source)
XLA Modules:
  0.0 37.7 jit_solution(10652248350094618908)
XLA Ops:
  0.7 0.5 %collective-permute-start.4 = (f32[64,2048]{1,0:T(8,128)}, f32[64,2048]{1,0:T(8,128)S(1)}, u32[]{:S(2)}, u32[]{:S(2)}) collective-permute-start(f32[64,2048]{1,0:T(8,128)} %own.3), channel_id=1, source_target_pairs={{0,4},{4,0},{8,12},{12,8},{16,20},{20,16},{24,28},{28,24},{1,5},{5... | collective-permute-start | bytes 1572872 | tf_op jit(solution)/shard_map/ppermute | solution.py:210
  1.2 2.6 %collective-permute-start = (s32[1,4]{1,0:T(1,128)}, s32[1,4]{1,0:T(1,128)S(1)}, u32[]{:S(2)}, u32[]{:S(2)}) collective-permute-start(s32[1,4]{1,0:T(1,128)} %bitcast.12), channel_id=1, source_target_pairs={{0,8},{4,12},{8,0},{12,4},{16,24},{20,28},{24,16},{28,20},{1,9},{5... | collective-permute-start | bytes 56 | tf_op jit(solution)/shard_map/ppermute | solution.py:207
  3.8 1.5 %collective-permute-start.1 = (s32[1,4]{1,0:T(1,128)}, s32[1,4]{1,0:T(1,128)S(1)}, u32[]{:S(2)}, u32[]{:S(2)}) collective-permute-start(s32[1,4]{1,0:T(1,128)} %bitcast.13), channel_id=1, source_target_pairs={{0,16},{4,20},{8,24},{12,28},{16,0},{20,4},{24,8},{28,12},{1,17},{... | collective-permute-start | bytes 56 | tf_op jit(solution)/shard_map/ppermute | solution.py:207
  5.3 0.0 collective-permute-start.2
  5.3 3.0 %collective-permute-start.3 = (f32[64,512]{1,0:T(8,128)}, f32[64,512]{1,0:T(8,128)S(1)}, u32[]{:S(2)}, u32[]{:S(2)}) collective-permute-start(f32[64,512]{1,0:T(8,128)} %refs_0_.1), channel_id=1, source_target_pairs={{0,2},{1,3},{2,0},{3,1},{4,6},{5,7},{6,4},{7,5},{8,10},{9,11},{10,... | collective-permute-start | bytes 393224 | tf_op jit(solution)/shard_map/ppermute | solution.py:213
  8.4 1.5 %collective-permute-done.2 = s32[1,4]{1,0:T(1,128)S(1)} collective-permute-done((s32[1,4]{1,0:T(1,128)}, s32[1,4]{1,0:T(1,128)S(1)}, u32[]{:S(2)}, u32[]{:S(2)}) %collective-permute-start.2) | collective-permute-done | bytes 48 | tf_op jit(solution)/shard_map/ppermute | solution.py:207
  9.9 0.0 collective-permute-done.4.sibling
  9.9 0.8 %serve.1 = (f32[64,512]{1,0:T(8,128)S(1)}, f32[64,512]{1,0:T(8,128)S(1)}, f32[64,512]{1,0:T(8,128)S(1)}) custom-call(s32[4,4]{1,0:T(4,128)S(1)} %pad_add_fusion.requests.ids, f32[64,2048]{1,0:T(8,128)S(1)} %copy-done, f32[64,2048]{1,0:T(8,128)S(1)} %collective-permute-done.4.sibling, f32[8,128]{1,0:T(8,128)S(1)} %hold.1._), custom_call_target="tpu_custom_call" | custom-call | flops 1073741824 | bytes 8388608 | tf_op jit(solution)/shard_map/serve/pallas_call | solution.py:231
  10.7 0.6 %collective-permute-start.5 = (f32[64,512]{1,0:T(8,128)S(1)}, f32[64,512]{1,0:T(8,128)S(1)}, u32[]{:S(2)}, u32[]{:S(2)}) collective-permute-start(f32[64,512]{1,0:T(8,128)S(1)} %get-tuple-element.14._), channel_id=1, source_target_pairs={{0,8},{4,12},{8,0},{12,4},{16,24},{20,28},{24,16},{28,20},{1,9},{5... | collective-permute-start | bytes 393224 | tf_op jit(solution)/shard_map/ppermute | solution.py:207
  11.3 1.0 %collective-permute-start.6 = (f32[64,512]{1,0:T(8,128)S(1)}, f32[64,512]{1,0:T(8,128)S(1)}, u32[]{:S(2)}, u32[]{:S(2)}) collective-permute-start(f32[64,512]{1,0:T(8,128)S(1)} %get-tuple-element.17), channel_id=1, source_target_pairs={{0,16},{4,20},{8,24},{12,28},{16,0},{20,4},{24,8},{28,12},{1,17},{... | collective-permute-start | bytes 393224 | tf_op jit(solution)/shard_map/ppermute | solution.py:207
  12.3 2.0 %collective-permute-start.7 = (f32[64,512]{1,0:T(8,128)S(1)}, f32[64,512]{1,0:T(8,128)S(1)}, u32[]{:S(2)}, u32[]{:S(2)}) collective-permute-start(f32[64,512]{1,0:T(8,128)S(1)} %get-tuple-element.18), channel_id=1, source_target_pairs={{0,24},{4,28},{8,16},{12,20},{16,8},{20,12},{24,0},{28,4},{1,25},{... | collective-permute-start | bytes 393224 | tf_op jit(solution)/shard_map/ppermute | solution.py:207
  14.3 1.6 %collective-permute-start.8 = (f32[64,512]{1,0:T(8,128)S(1)}, f32[64,512]{1,0:T(8,128)S(1)}, u32[]{:S(2)}, u32[]{:S(2)}) collective-permute-start(f32[64,512]{1,0:T(8,128)S(1)} %copy-done.1), channel_id=1, source_target_pairs={{0,1},{1,0},{2,3},{3,2},{4,5},{5,4},{6,7},{7,6},{8,9},{9,8},{10,11... | collective-permute-start | bytes 393224 | tf_op jit(solution)/shard_map/ppermute | solution.py:213
  16.5 0.0 collective-permute-done.3.users
  16.6 1.2 %prepare.1 = (bf16[4,32,128,256]{3,2,1,0:T(8,128)(2,1)S(1)}, f32[32,64,128]{2,1,0:T(8,128)S(1)}, f32[64,512]{1,0:T(8,128)S(1)}) custom-call(s32[1,1]{1,0:T(1,128)S(6)} %copy.9.count_ref, f32[4,32,128,128]{3,2,1,0:T(8,128)S(1)} %bitcast.9, f32[32,64]{1,0:T(8,128)S(1)} %copy-done.2, f32[64,512]{1,0:T(8,128)S(1)} %collective-permute-done.3.users, ...), custom_call_target="tpu_custom_call" | custom-call | tf_op jit(solution)/shard_map/prepare/pallas_call | solution.py:242
  17.8 1.2 %collective-permute-start.9 = (f32[64,512]{1,0:T(8,128)S(1)}, f32[64,512]{1,0:T(8,128)S(1)}, u32[]{:S(2)}, u32[]{:S(2)}) collective-permute-start(f32[64,512]{1,0:T(8,128)S(1)} %get-tuple-element.20.refs_2_), channel_id=1, source_target_pairs={{0,1},{1,0},{2,3},{3,2},{4,5},{5,4},{6,7},{7,6},{8,9},{9,8},{10,11... | collective-permute-start | bytes 393224 | tf_op jit(solution)/shard_map/ppermute | solution.py:213
  19.0 0.0 collective-permute-done.5.refs_0_
  19.0 0.0 collective-permute-done.6.refs_1_
  19.0 0.0 collective-permute-done.7.refs_2_
  19.0 2.2 %mode1.1 = (f32[2,64,512]{2,1,0:T(8,128)S(1)}, f32[2,64,512]{2,1,0:T(8,128)S(1)}) custom-call(s32[1,1]{1,0:T(1,128)S(6)} %copy.9.count_ref, s32[1,4]{1,0:T(1,128)S(1)} %bitcast.10, s32[1,4]{1,0:T(1,128)S(1)} %bitcast.16, f32[32,64,128]{2,1,0:T(8,128)S(1)} %get-tuple-element.15.spread, bf16[4,32,128,256]{3,2,1,0:T(8,128)(2,1)S(1)} %get-tuple-element.16.tiles, ...), custom_call_target="tpu_custom_call" | custom-call | flops 1073741824 | bytes 8388608 | tf_op jit(solution)/shard_map/mode1/pallas_call | solution.py:260
  21.2 3.1 %collective-permute-start.14 = (f32[2,64,512]{2,1,0:T(8,128)S(1)}, f32[2,64,512]{2,1,0:T(8,128)S(1)}, u32[]{:S(2)}, u32[]{:S(2)}) collective-permute-start(f32[2,64,512]{2,1,0:T(8,128)S(1)} %get-tuple-element.23), channel_id=1, source_target_pairs={{0,1},{1,0},{2,3},{3,2},{4,5},{5,4},{6,7},{7,6},{8,9},{9,8},{10,11... | collective-permute-start | bytes 786440 | tf_op jit(solution)/shard_map/ppermute | solution.py:213
  24.4 0.0 collective-permute-done.8.refs_1_
  24.4 0.0 collective-permute-done.9.refs_3_
  24.4 1.5 %mode2.1.refs_0_ = f32[64,512]{1,0:T(8,128)S(1)} custom-call(s32[1,1]{1,0:T(1,128)S(6)} %copy.9.count_ref, s32[1,4]{1,0:T(1,128)S(1)} %bitcast.11, f32[32,64,128]{2,1,0:T(8,128)S(1)} %get-tuple-element.15.spread, bf16[4,32,128,256]{3,2,1,0:T(8,128)(2,1)S(1)} %get-tuple-element.16.tiles, f32[2,64,512]{2,1,0:T(8,128)S(1)} %get-tuple-element.19._, ...), custom_call_target="tpu_custom_call" | custom-call | flops 2147483648 | bytes 16777216 | tf_op jit(solution)/shard_map/mode2/pallas_call | solution.py:279
  25.8 0.4 %collective-permute-start.10 = (f32[64,512]{1,0:T(8,128)S(1)}, f32[64,512]{1,0:T(8,128)S(1)}, u32[]{:S(2)}, u32[]{:S(2)}) collective-permute-start(f32[64,512]{1,0:T(8,128)S(1)} %mode2.1.refs_0_), channel_id=1, source_target_pairs={{0,8},{4,12},{8,0},{12,4},{16,24},{20,28},{24,16},{28,20},{1,9},{5... | collective-permute-start | bytes 393224 | tf_op jit(solution)/shard_map/ppermute | solution.py:207
  26.3 0.3 collective-permute-start.11
  26.5 2.8 %collective-permute-start.12 = (f32[64,512]{1,0:T(8,128)S(1)}, f32[64,512]{1,0:T(8,128)S(1)}, u32[]{:S(2)}, u32[]{:S(2)}) collective-permute-start(f32[64,512]{1,0:T(8,128)S(1)} %mode2.1.refs_0_), channel_id=1, source_target_pairs={{0,24},{4,28},{8,16},{12,20},{16,8},{20,12},{24,0},{28,4},{1,25},{... | collective-permute-start | bytes 393224 | tf_op jit(solution)/shard_map/ppermute | solution.py:207
  29.4 2.4 %collective-permute-start.15 = (f32[64,512]{1,0:T(8,128)S(1)}, f32[64,512]{1,0:T(8,128)S(1)}, u32[]{:S(2)}, u32[]{:S(2)}) collective-permute-start(f32[64,512]{1,0:T(8,128)S(1)} %get-tuple-element.26), channel_id=1, source_target_pairs={{0,2},{1,3},{2,0},{3,1},{4,6},{5,7},{6,4},{7,5},{8,10},{9,11},{10,... | collective-permute-start | bytes 393224 | tf_op jit(solution)/shard_map/ppermute | solution.py:213
  31.8 1.4 %collective-permute-done.11.refs_2_ = f32[64,512]{1,0:T(8,128)S(1)} collective-permute-done((f32[64,512]{1,0:T(8,128)S(1)}, f32[64,512]{1,0:T(8,128)S(1)}, u32[]{:S(2)}, u32[]{:S(2)}) %collective-permute-start.11) | collective-permute-done | bytes 131104 | tf_op jit(solution)/shard_map/ppermute | solution.py:207
  33.2 1.0 %collect.1 = (f32[64,2048]{1,0:T(8,128)S(1)}, f32[64,2048]{1,0:T(8,128)S(1)}) custom-call(s32[4,4]{1,0:T(4,128)S(1)} %pad_add_fusion.requests.ids, f32[64,512]{1,0:T(8,128)S(1)} %mode2.1.refs_0_, f32[64,512]{1,0:T(8,128)S(1)} %collective-permute-done.10.refs_1_, f32[64,512]{1,0:T(8,128)S(1)} %collective-permute-done.11.refs_2_, ...), custom_call_target="tpu_custom_call" | custom-call | tf_op jit(solution)/shard_map/collect/pallas_call | solution.py:296
  34.2 0.1 collective-permute-start.13
  34.3 2.5 %collective-permute-done.15.arrived = f32[64,512]{1,0:T(8,128)S(1)} collective-permute-done((f32[64,512]{1,0:T(8,128)S(1)}, f32[64,512]{1,0:T(8,128)S(1)}, u32[]{:S(2)}, u32[]{:S(2)}) %collective-permute-start.15) | collective-permute-done | bytes 131104 | tf_op jit(solution)/shard_map/ppermute | solution.py:213
  36.8 0.9 %finish_items.1 = (f32[64,2048]{1,0:T(8,128)}, f32[64,512]{1,0:T(8,128)}) custom-call(f32[64,2048]{1,0:T(8,128)S(1)} %get-tuple-element.21.own, f32[64,2048]{1,0:T(8,128)S(1)} %collective-permute-done.13.arrived, f32[64,512]{1,0:T(8,128)S(1)} %finish_users.1.users), custom_call_target="tpu_custom_call" | custom-call | tf_op jit(solution)/shard_map/finish_items/pallas_call | solution.py:318
  (25 shorter events, 0.1 us)
Async XLA Ops:
  0.6 9.3 %copy-start = (f32[64,2048]{1,0:T(8,128)S(1)}, f32[64,2048]{1,0:T(8,128)}, u32[]{:S(2)}) copy-start(f32[64,2048]{1,0:T(8,128)} %own.3) | copy-start | bytes 1572868
  0.6 9.2 %copy-start.4 = (s32[1,1,4]{2,1,0:T(1,128)S(1)}, s32[1,1,4]{2,1,0:T(1,128)}, u32[]{:S(2)}) copy-start(s32[1,1,4]{2,1,0:T(1,128)} %param.9) | copy-start | bytes 52
  0.7 9.2 %collective-permute-start.4 = (f32[64,2048]{1,0:T(8,128)}, f32[64,2048]{1,0:T(8,128)S(1)}, u32[]{:S(2)}, u32[]{:S(2)}) collective-permute-start(f32[64,2048]{1,0:T(8,128)} %own.3), channel_id=1, source_target_pairs={{0,4},{4,0},{8,12},{12,8},{16,20},{20,16},{24,28},{28,24},{1,5},{5... | collective-permute-start | bytes 1572872 | tf_op jit(solution)/shard_map/ppermute | solution.py:210
  1.2 15.4 %slice-start = ((s8[8388608]{0:T(1024)(128)(4,1)}), s8[4194304]{0:T(1024)(128)(4,1)S(1)}, s32[]{:S(2)}) async-start(s8[8388608]{0:T(1024)(128)(4,1)} %bitcast.7), calls=%async_computation | async-start | bytes 8388608
  1.2 13.1 %copy-start.1 = (f32[64,512]{1,0:T(8,128)S(1)}, f32[64,512]{1,0:T(8,128)}, u32[]{:S(2)}) copy-start(f32[64,512]{1,0:T(8,128)} %refs_0_.1) | copy-start | bytes 393220
  1.2 15.4 %slice-start.1 = ((s8[8388608]{0:T(1024)(128)(4,1)}), s8[4194304]{0:T(1024)(128)(4,1)S(1)}, s32[]{:S(2)}) async-start(s8[8388608]{0:T(1024)(128)(4,1)} %bitcast.7), calls=%async_computation.1 | async-start | bytes 8388608
  1.2 15.4 %copy-start.2 = (f32[32,64]{1,0:T(8,128)S(1)}, f32[32,64]{1,0:T(8,128)}, u32[]{:S(2)}) copy-start(f32[32,64]{1,0:T(8,128)} %week_factor.1) | copy-start | bytes 24580
  1.2 7.2 %collective-permute-start = (s32[1,4]{1,0:T(1,128)}, s32[1,4]{1,0:T(1,128)S(1)}, u32[]{:S(2)}, u32[]{:S(2)}) collective-permute-start(s32[1,4]{1,0:T(1,128)} %bitcast.12), channel_id=1, source_target_pairs={{0,8},{4,12},{8,0},{12,4},{16,24},{20,28},{24,16},{28,20},{1,9},{5... | collective-permute-start | bytes 56 | tf_op jit(solution)/shard_map/ppermute | solution.py:207
  3.8 4.6 %collective-permute-start.1 = (s32[1,4]{1,0:T(1,128)}, s32[1,4]{1,0:T(1,128)S(1)}, u32[]{:S(2)}, u32[]{:S(2)}) collective-permute-start(s32[1,4]{1,0:T(1,128)} %bitcast.13), channel_id=1, source_target_pairs={{0,16},{4,20},{8,24},{12,28},{16,0},{20,4},{24,8},{28,12},{1,17},{... | collective-permute-start | bytes 56 | tf_op jit(solution)/shard_map/ppermute | solution.py:207
  5.3 4.6 %collective-permute-start.2 = (s32[1,4]{1,0:T(1,128)}, s32[1,4]{1,0:T(1,128)S(1)}, u32[]{:S(2)}, u32[]{:S(2)}) collective-permute-start(s32[1,4]{1,0:T(1,128)} %bitcast.14), channel_id=1, source_target_pairs={{0,24},{4,28},{8,16},{12,20},{16,8},{20,12},{24,0},{28,4},{1,25},{... | collective-permute-start | bytes 56 | tf_op jit(solution)/shard_map/ppermute | solution.py:207
  5.3 11.2 %collective-permute-start.3 = (f32[64,512]{1,0:T(8,128)}, f32[64,512]{1,0:T(8,128)S(1)}, u32[]{:S(2)}, u32[]{:S(2)}) collective-permute-start(f32[64,512]{1,0:T(8,128)} %refs_0_.1), channel_id=1, source_target_pairs={{0,2},{1,3},{2,0},{3,1},{4,6},{5,7},{6,4},{7,5},{8,10},{9,11},{10,... | collective-permute-start | bytes 393224 | tf_op jit(solution)/shard_map/ppermute | solution.py:213
  8.4 10.7 %copy-start.3 = (s32[1,1,4]{2,1,0:T(1,128)S(1)}, s32[1,1,4]{2,1,0:T(1,128)}, u32[]{:S(2)}) copy-start(s32[1,1,4]{2,1,0:T(1,128)} %param.8) | copy-start | bytes 52
  10.7 8.3 %collective-permute-start.5 = (f32[64,512]{1,0:T(8,128)S(1)}, f32[64,512]{1,0:T(8,128)S(1)}, u32[]{:S(2)}, u32[]{:S(2)}) collective-permute-start(f32[64,512]{1,0:T(8,128)S(1)} %get-tuple-element.14._), channel_id=1, source_target_pairs={{0,8},{4,12},{8,0},{12,4},{16,24},{20,28},{24,16},{28,20},{1,9},{5... | collective-permute-start | bytes 393224 | tf_op jit(solution)/shard_map/ppermute | solution.py:207
  11.3 7.7 %collective-permute-start.6 = (f32[64,512]{1,0:T(8,128)S(1)}, f32[64,512]{1,0:T(8,128)S(1)}, u32[]{:S(2)}, u32[]{:S(2)}) collective-permute-start(f32[64,512]{1,0:T(8,128)S(1)} %get-tuple-element.17), channel_id=1, source_target_pairs={{0,16},{4,20},{8,24},{12,28},{16,0},{20,4},{24,8},{28,12},{1,17},{... | collective-permute-start | bytes 393224 | tf_op jit(solution)/shard_map/ppermute | solution.py:207
  12.3 6.7 %collective-permute-start.7 = (f32[64,512]{1,0:T(8,128)S(1)}, f32[64,512]{1,0:T(8,128)S(1)}, u32[]{:S(2)}, u32[]{:S(2)}) collective-permute-start(f32[64,512]{1,0:T(8,128)S(1)} %get-tuple-element.18), channel_id=1, source_target_pairs={{0,24},{4,28},{8,16},{12,20},{16,8},{20,12},{24,0},{28,4},{1,25},{... | collective-permute-start | bytes 393224 | tf_op jit(solution)/shard_map/ppermute | solution.py:207
  14.3 10.1 %collective-permute-start.8 = (f32[64,512]{1,0:T(8,128)S(1)}, f32[64,512]{1,0:T(8,128)S(1)}, u32[]{:S(2)}, u32[]{:S(2)}) collective-permute-start(f32[64,512]{1,0:T(8,128)S(1)} %copy-done.1), channel_id=1, source_target_pairs={{0,1},{1,0},{2,3},{3,2},{4,5},{5,4},{6,7},{7,6},{8,9},{9,8},{10,11... | collective-permute-start | bytes 393224 | tf_op jit(solution)/shard_map/ppermute | solution.py:213
  17.8 6.6 %collective-permute-start.9 = (f32[64,512]{1,0:T(8,128)S(1)}, f32[64,512]{1,0:T(8,128)S(1)}, u32[]{:S(2)}, u32[]{:S(2)}) collective-permute-start(f32[64,512]{1,0:T(8,128)S(1)} %get-tuple-element.20.refs_2_), channel_id=1, source_target_pairs={{0,1},{1,0},{2,3},{3,2},{4,5},{5,4},{6,7},{7,6},{8,9},{9,8},{10,11... | collective-permute-start | bytes 393224 | tf_op jit(solution)/shard_map/ppermute | solution.py:213
  21.2 8.2 %collective-permute-start.14 = (f32[2,64,512]{2,1,0:T(8,128)S(1)}, f32[2,64,512]{2,1,0:T(8,128)S(1)}, u32[]{:S(2)}, u32[]{:S(2)}) collective-permute-start(f32[2,64,512]{2,1,0:T(8,128)S(1)} %get-tuple-element.23), channel_id=1, source_target_pairs={{0,1},{1,0},{2,3},{3,2},{4,5},{5,4},{6,7},{7,6},{8,9},{9,8},{10,11... | collective-permute-start | bytes 786440 | tf_op jit(solution)/shard_map/ppermute | solution.py:213
  25.8 6.0 %collective-permute-start.10 = (f32[64,512]{1,0:T(8,128)S(1)}, f32[64,512]{1,0:T(8,128)S(1)}, u32[]{:S(2)}, u32[]{:S(2)}) collective-permute-start(f32[64,512]{1,0:T(8,128)S(1)} %mode2.1.refs_0_), channel_id=1, source_target_pairs={{0,8},{4,12},{8,0},{12,4},{16,24},{20,28},{24,16},{28,20},{1,9},{5... | collective-permute-start | bytes 393224 | tf_op jit(solution)/shard_map/ppermute | solution.py:207
  26.3 6.9 %collective-permute-start.11 = (f32[64,512]{1,0:T(8,128)S(1)}, f32[64,512]{1,0:T(8,128)S(1)}, u32[]{:S(2)}, u32[]{:S(2)}) collective-permute-start(f32[64,512]{1,0:T(8,128)S(1)} %mode2.1.refs_0_), channel_id=1, source_target_pairs={{0,16},{4,20},{8,24},{12,28},{16,0},{20,4},{24,8},{28,12},{1,17},{... | collective-permute-start | bytes 393224 | tf_op jit(solution)/shard_map/ppermute | solution.py:207
  26.5 6.7 %collective-permute-start.12 = (f32[64,512]{1,0:T(8,128)S(1)}, f32[64,512]{1,0:T(8,128)S(1)}, u32[]{:S(2)}, u32[]{:S(2)}) collective-permute-start(f32[64,512]{1,0:T(8,128)S(1)} %mode2.1.refs_0_), channel_id=1, source_target_pairs={{0,24},{4,28},{8,16},{12,20},{16,8},{20,12},{24,0},{28,4},{1,25},{... | collective-permute-start | bytes 393224 | tf_op jit(solution)/shard_map/ppermute | solution.py:207
  29.4 7.3 %collective-permute-start.15 = (f32[64,512]{1,0:T(8,128)S(1)}, f32[64,512]{1,0:T(8,128)S(1)}, u32[]{:S(2)}, u32[]{:S(2)}) collective-permute-start(f32[64,512]{1,0:T(8,128)S(1)} %get-tuple-element.26), channel_id=1, source_target_pairs={{0,2},{1,3},{2,0},{3,1},{4,6},{5,7},{6,4},{7,5},{8,10},{9,11},{10,... | collective-permute-start | bytes 393224 | tf_op jit(solution)/shard_map/ppermute | solution.py:213
  34.2 2.6 %collective-permute-start.13 = (f32[64,2048]{1,0:T(8,128)S(1)}, f32[64,2048]{1,0:T(8,128)S(1)}, u32[]{:S(2)}, u32[]{:S(2)}) collective-permute-start(f32[64,2048]{1,0:T(8,128)S(1)} %get-tuple-element.22), channel_id=1, source_target_pairs={{0,4},{4,0},{8,12},{12,8},{16,20},{20,16},{24,28},{28,24},{1,5},{5... | collective-permute-start | bytes 1572872 | tf_op jit(solution)/shard_map/ppermute | solution.py:210

commit v3 on v0

--- a/solution.py
+++ b/solution.py
@@ -24,7 +24,7 @@
     return high, (value - high.astype(F32)).astype(BF16)
 
 
-def hold_kernel(done):
+def hold_kernel(_, done):
     done[...] = jnp.zeros_like(done)
 
 
@@ -164,13 +164,13 @@
                     target[:, place] += term[:, slot * width : (slot + 1) * width]
 
 
-def finish_users_kernel(kept, arrived, total, done):
+def finish_users_kernel(kept, arrived, total):
     total[...] = kept[...] + arrived[...]
-    done[...] = jnp.zeros_like(done)
-
-
-def finish_items_kernel(own, arrived, _, total):
-    total[...] = own[...] + arrived[...]
+
+
+def finish_items_kernel(own, arrived, users, items_out, users_out):
+    users_out[...] = users[...]
+    items_out[...] = own[...] + arrived[...]
 
 
 def on_device(sizes, tiles, user_blocks, item_blocks, counts, user_factor, item_factor, week_factor):
@@ -210,11 +210,12 @@
     held = pl.pallas_call(
         hold_kernel,
         out_shape=array(8, 128),
+        in_specs=[SMEM],
         out_specs=VMEM,
         compiler_params=limit(4),
         cost_estimate=cost(4),
         name="hold",
-    )()
+    )(counts)
 
     served = pl.pallas_call(
         functools.partial(serve_kernel, chips, width),
@@ -294,23 +295,23 @@
         arrived = across_groups(sent, step)
         kept, sent = kept[0::2] + arrived[0::2], kept[1::2] + arrived[1::2]
         step *= 2
-    m_users, done = pl.pallas_call(
+    users = pl.pallas_call(
         finish_users_kernel,
-        out_shape=[array(rank, user_width), array(8, 128)],
+        out_shape=array(rank, user_width),
         in_specs=[VMEM] * 2,
-        out_specs=[VMEM] * 2,
+        out_specs=VMEM,
         compiler_params=limit(4),
         cost_estimate=cost(4),
         name="finish_users",
     )(kept[0], across_groups(sent[0], step))
-    m_items = pl.pallas_call(
+    m_items, m_users = pl.pallas_call(
         finish_items_kernel,
-        out_shape=array(*item_factor.shape),
-        in_specs=[VMEM] * 2 + [ANY],
-        out_specs=VMEM,
+        out_shape=[array(*item_factor.shape), array(rank, user_width)],
+        in_specs=[VMEM] * 3,
+        out_specs=[VMEM] * 2,
         compiler_params=limit(4),
         name="finish_items",
-    )(own, across_cores(other), done)
+    )(own, across_cores(other), users)
     return m_users, m_items
 
 

time: 37.9 us -> 38.1 us (level)
  Pallas kernels: 6.59 us -> 5.95 us
  waiting for transfers between devices: 6.54 us -> 7.12 us
    ppermute x5, starting transfers between devices: 10.5 us -> 9.49 us  [across_groups(): return lax.ppermute(value, 'items', [(i, i ^ step) for i in range(groups)])]
    ppermute x9, starting transfers between devices: 11.8 us -> 12.8 us  [across_chips(): lax.ppermute(value, 'users', [(i, i ^ 2 * step) for i in range(rows)])]
    pallas_call x3, Pallas kernels: 1.52 us -> 0.92 us  [the longest x1 0.9 us: on_device(): pl.pallas_call(finish_items_kernel, out_shape=[array(*item_factor.shape),...]
    ppermute x5, waiting for transfers between devices: 2.03 us -> 2.57 us  [across_groups(): return lax.ppermute(value, 'items', [(i, i ^ step) for i in range(groups)])]
  transfers between devices with their start and end apart: 16 -> 16, of which waited for: 5 -> 4; matrix products, arithmetic and copies ran while one was open for 0% -> 0% of each run, Pallas kernels for 15% -> 13%
where the time goes in v3:
time: 38.1 us; the launch traced here: 37.7 us
  starting transfers between devices  22.9 us (60%)
  waiting for transfers between devices  7.12 us (19%)
  Pallas kernels  5.95 us (16%)
  between operations  1.62 us (4%)
    ppermute x9, starting transfers between devices, across_chips(): lax.ppermute(value, 'users', [(i, i ^ 2 * step) for i in range(rows)])  12.8 us
    ppermute x5, starting transfers between devices, across_groups(): return lax.ppermute(value, 'items', [(i, i ^ step) for i in range(groups)])  9.49 us
    ppermute x9, waiting for transfers between devices, across_chips(): lax.ppermute(value, 'users', [(i, i ^ 2 * step) for i in range(rows)])  4.54 us
    ppermute x5, waiting for transfers between devices, across_groups(): return lax.ppermute(value, 'items', [(i, i ^ step) for i in range(groups)])  2.57 us
    pallas_call x1, Pallas kernels, on_device(): pl.pallas_call(functools.partial(mode1_kernel, groups), out_shape=[array(...  1.44 us
    pallas_call x1, Pallas kernels, on_device(): pl.pallas_call(mode2_kernel, out_shape=array(rank, slots * width), in_spe...  0.99 us
    pallas_call x1, Pallas kernels, on_device(): pl.pallas_call(collect_kernel, out_shape=[array(*item_factor.shape)] * 2,...  0.95 us
    pallas_call x1, Pallas kernels, on_device(): pl.pallas_call(finish_items_kernel, out_shape=[array(*item_factor.shape),...  0.9 us
  transfers between devices with their start and end apart: 16, of which 4 were waited for; matrix products, arithmetic and copies ran while one was open for 0% of the time, Pallas kernels for 13%

profile of v3, /device:TPU:0, one launch (start us, length us, event | category | flops | bytes accessed | tf_op | source)
XLA Modules:
  0.0 37.7 jit_solution(7677622184109989417)
XLA Ops:
  0.7 0.5 %collective-permute-start.4 = (f32[64,2048]{1,0:T(8,128)}, f32[64,2048]{1,0:T(8,128)S(1)}, u32[]{:S(2)}, u32[]{:S(2)}) collective-permute-start(f32[64,2048]{1,0:T(8,128)} %own.3), channel_id=1, source_target_pairs={{0,4},{4,0},{8,12},{12,8},{16,20},{20,16},{24,28},{28,24},{1,5},{5... | collective-permute-start | bytes 1572872 | tf_op jit(solution)/shard_map/ppermute | solution.py:198
  1.2 2.6 %collective-permute-start = (s32[1,4]{1,0:T(1,128)}, s32[1,4]{1,0:T(1,128)S(1)}, u32[]{:S(2)}, u32[]{:S(2)}) collective-permute-start(s32[1,4]{1,0:T(1,128)} %bitcast.12), channel_id=1, source_target_pairs={{0,8},{4,12},{8,0},{12,4},{16,24},{20,28},{24,16},{28,20},{1,9},{5... | collective-permute-start | bytes 56 | tf_op jit(solution)/shard_map/ppermute | solution.py:195
  3.7 1.5 %collective-permute-start.1 = (s32[1,4]{1,0:T(1,128)}, s32[1,4]{1,0:T(1,128)S(1)}, u32[]{:S(2)}, u32[]{:S(2)}) collective-permute-start(s32[1,4]{1,0:T(1,128)} %bitcast.13), channel_id=1, source_target_pairs={{0,16},{4,20},{8,24},{12,28},{16,0},{20,4},{24,8},{28,12},{1,17},{... | collective-permute-start | bytes 56 | tf_op jit(solution)/shard_map/ppermute | solution.py:195
  5.3 0.0 collective-permute-start.2
  5.3 3.0 %collective-permute-start.3 = (f32[64,512]{1,0:T(8,128)}, f32[64,512]{1,0:T(8,128)S(1)}, u32[]{:S(2)}, u32[]{:S(2)}) collective-permute-start(f32[64,512]{1,0:T(8,128)} %refs_0_.1), channel_id=1, source_target_pairs={{0,2},{1,3},{2,0},{3,1},{4,6},{5,7},{6,4},{7,5},{8,10},{9,11},{10,... | collective-permute-start | bytes 393224 | tf_op jit(solution)/shard_map/ppermute | solution.py:201
  9.2 0.0 copy-start.3
  9.2 0.0 collective-permute-done
  9.2 0.6 %collective-permute-done.2 = s32[1,4]{1,0:T(1,128)S(1)} collective-permute-done((s32[1,4]{1,0:T(1,128)}, s32[1,4]{1,0:T(1,128)S(1)}, u32[]{:S(2)}, u32[]{:S(2)}) %collective-permute-start.2) | collective-permute-done | bytes 48 | tf_op jit(solution)/shard_map/ppermute | solution.py:195
  9.9 0.8 %serve.1 = (f32[64,512]{1,0:T(8,128)S(1)}, f32[64,512]{1,0:T(8,128)S(1)}, f32[64,512]{1,0:T(8,128)S(1)}) custom-call(s32[4,4]{1,0:T(4,128)S(1)} %pad_add_fusion.requests.ids, f32[64,2048]{1,0:T(8,128)S(1)} %copy-done, f32[64,2048]{1,0:T(8,128)S(1)} %collective-permute-done.4.sibling, f32[8,128]{1,0:T(8,128)S(1)} %hold.1._), custom_call_target="tpu_custom_call" | custom-call | flops 1073741824 | bytes 8388608 | tf_op jit(solution)/shard_map/serve/pallas_call | solution.py:220
  10.7 1.0 %collective-permute-start.5 = (f32[64,512]{1,0:T(8,128)S(1)}, f32[64,512]{1,0:T(8,128)S(1)}, u32[]{:S(2)}, u32[]{:S(2)}) collective-permute-start(f32[64,512]{1,0:T(8,128)S(1)} %get-tuple-element.14._), channel_id=1, source_target_pairs={{0,8},{4,12},{8,0},{12,4},{16,24},{20,28},{24,16},{28,20},{1,9},{5... | collective-permute-start | bytes 393224 | tf_op jit(solution)/shard_map/ppermute | solution.py:195
  11.6 1.5 %collective-permute-start.6 = (f32[64,512]{1,0:T(8,128)S(1)}, f32[64,512]{1,0:T(8,128)S(1)}, u32[]{:S(2)}, u32[]{:S(2)}) collective-permute-start(f32[64,512]{1,0:T(8,128)S(1)} %get-tuple-element.17), channel_id=1, source_target_pairs={{0,16},{4,20},{8,24},{12,28},{16,0},{20,4},{24,8},{28,12},{1,17},{... | collective-permute-start | bytes 393224 | tf_op jit(solution)/shard_map/ppermute | solution.py:195
  13.2 1.1 %collective-permute-start.7 = (f32[64,512]{1,0:T(8,128)S(1)}, f32[64,512]{1,0:T(8,128)S(1)}, u32[]{:S(2)}, u32[]{:S(2)}) collective-permute-start(f32[64,512]{1,0:T(8,128)S(1)} %get-tuple-element.18), channel_id=1, source_target_pairs={{0,24},{4,28},{8,16},{12,20},{16,8},{20,12},{24,0},{28,4},{1,25},{... | collective-permute-start | bytes 393224 | tf_op jit(solution)/shard_map/ppermute | solution.py:195
  14.2 1.6 %collective-permute-start.8 = (f32[64,512]{1,0:T(8,128)S(1)}, f32[64,512]{1,0:T(8,128)S(1)}, u32[]{:S(2)}, u32[]{:S(2)}) collective-permute-start(f32[64,512]{1,0:T(8,128)S(1)} %copy-done.1), channel_id=1, source_target_pairs={{0,1},{1,0},{2,3},{3,2},{4,5},{5,4},{6,7},{7,6},{8,9},{9,8},{10,11... | collective-permute-start | bytes 393224 | tf_op jit(solution)/shard_map/ppermute | solution.py:201
  15.8 0.0 collective-permute-done.3.users
  15.9 0.8 %prepare.1 = (bf16[4,32,128,256]{3,2,1,0:T(8,128)(2,1)S(1)}, f32[32,64,128]{2,1,0:T(8,128)S(1)}, f32[64,512]{1,0:T(8,128)S(1)}) custom-call(s32[1,1]{1,0:T(1,128)S(6)} %copy.9._.count_ref, f32[4,32,128,128]{3,2,1,0:T(8,128)S(1)} %bitcast.9, f32[32,64]{1,0:T(8,128)S(1)} %copy-done.2, f32[64,512]{1,0:T(8,128)S(1)} %collective-permute-done.3.users, ...), custom_call_target="tpu_custom_call" | custom-call | tf_op jit(solution)/shard_map/prepare/pallas_call | solution.py:231
  16.7 0.5 %collective-permute-start.9 = (f32[64,512]{1,0:T(8,128)S(1)}, f32[64,512]{1,0:T(8,128)S(1)}, u32[]{:S(2)}, u32[]{:S(2)}) collective-permute-start(f32[64,512]{1,0:T(8,128)S(1)} %get-tuple-element.20.refs_2_), channel_id=1, source_target_pairs={{0,1},{1,0},{2,3},{3,2},{4,5},{5,4},{6,7},{7,6},{8,9},{9,8},{10,11... | collective-permute-start | bytes 393224 | tf_op jit(solution)/shard_map/ppermute | solution.py:201
  17.2 0.0 collective-permute-done.5.refs_0_
  17.2 2.2 %collective-permute-done.6.refs_1_ = f32[64,512]{1,0:T(8,128)S(1)} collective-permute-done((f32[64,512]{1,0:T(8,128)S(1)}, f32[64,512]{1,0:T(8,128)S(1)}, u32[]{:S(2)}, u32[]{:S(2)}) %collective-permute-start.6) | collective-permute-done | bytes 131104 | tf_op jit(solution)/shard_map/ppermute | solution.py:195
  19.4 0.0 collective-permute-done.7.refs_2_
  19.4 1.4 %mode1.1 = (f32[2,64,512]{2,1,0:T(8,128)S(1)}, f32[2,64,512]{2,1,0:T(8,128)S(1)}) custom-call(s32[1,1]{1,0:T(1,128)S(6)} %copy.9._.count_ref, s32[1,4]{1,0:T(1,128)S(1)} %bitcast.10, s32[1,4]{1,0:T(1,128)S(1)} %bitcast.16, f32[32,64,128]{2,1,0:T(8,128)S(1)} %get-tuple-element.15.spread, bf16[4,32,128,256]{3,2,1,0:T(8,128)(2,1)S(1)} %get-tuple-element.16.tiles, ...), custom_call_target="tpu_custom_call" | custom-call | flops 1073741824 | bytes 8388608 | tf_op jit(solution)/shard_map/mode1/pallas_call | solution.py:249
  20.9 1.6 %collective-permute-start.14 = (f32[2,64,512]{2,1,0:T(8,128)S(1)}, f32[2,64,512]{2,1,0:T(8,128)S(1)}, u32[]{:S(2)}, u32[]{:S(2)}) collective-permute-start(f32[2,64,512]{2,1,0:T(8,128)S(1)} %get-tuple-element.23), channel_id=1, source_target_pairs={{0,1},{1,0},{2,3},{3,2},{4,5},{5,4},{6,7},{7,6},{8,9},{9,8},{10,11... | collective-permute-start | bytes 786440 | tf_op jit(solution)/shard_map/ppermute | solution.py:201
  22.5 1.0 %mode2.1.refs_0_ = f32[64,512]{1,0:T(8,128)S(1)} custom-call(s32[1,1]{1,0:T(1,128)S(6)} %copy.9._.count_ref, s32[1,4]{1,0:T(1,128)S(1)} %bitcast.11, f32[32,64,128]{2,1,0:T(8,128)S(1)} %get-tuple-element.15.spread, bf16[4,32,128,256]{3,2,1,0:T(8,128)(2,1)S(1)} %get-tuple-element.16.tiles, f32[2,64,512]{2,1,0:T(8,128)S(1)} %get-tuple-element.19._, ...), custom_call_target="tpu_custom_call" | custom-call | flops 2147483648 | bytes 16777216 | tf_op jit(solution)/shard_map/mode2/pallas_call | solution.py:268
  23.5 2.2 %collective-permute-start.10 = (f32[64,512]{1,0:T(8,128)S(1)}, f32[64,512]{1,0:T(8,128)S(1)}, u32[]{:S(2)}, u32[]{:S(2)}) collective-permute-start(f32[64,512]{1,0:T(8,128)S(1)} %mode2.1.refs_0_), channel_id=1, source_target_pairs={{0,8},{4,12},{8,0},{12,4},{16,24},{20,28},{24,16},{28,20},{1,9},{5... | collective-permute-start | bytes 393224 | tf_op jit(solution)/shard_map/ppermute | solution.py:195
  25.7 1.6 %collective-permute-start.11 = (f32[64,512]{1,0:T(8,128)S(1)}, f32[64,512]{1,0:T(8,128)S(1)}, u32[]{:S(2)}, u32[]{:S(2)}) collective-permute-start(f32[64,512]{1,0:T(8,128)S(1)} %mode2.1.refs_0_), channel_id=1, source_target_pairs={{0,16},{4,20},{8,24},{12,28},{16,0},{20,4},{24,8},{28,12},{1,17},{... | collective-permute-start | bytes 393224 | tf_op jit(solution)/shard_map/ppermute | solution.py:195
  27.3 1.4 %collective-permute-start.12 = (f32[64,512]{1,0:T(8,128)S(1)}, f32[64,512]{1,0:T(8,128)S(1)}, u32[]{:S(2)}, u32[]{:S(2)}) collective-permute-start(f32[64,512]{1,0:T(8,128)S(1)} %mode2.1.refs_0_), channel_id=1, source_target_pairs={{0,24},{4,28},{8,16},{12,20},{16,8},{20,12},{24,0},{28,4},{1,25},{... | collective-permute-start | bytes 393224 | tf_op jit(solution)/shard_map/ppermute | solution.py:195
  28.7 2.7 %collective-permute-start.15 = (f32[64,512]{1,0:T(8,128)S(1)}, f32[64,512]{1,0:T(8,128)S(1)}, u32[]{:S(2)}, u32[]{:S(2)}) collective-permute-start(f32[64,512]{1,0:T(8,128)S(1)} %get-tuple-element.26), channel_id=1, source_target_pairs={{0,2},{1,3},{2,0},{3,1},{4,6},{5,7},{6,4},{7,5},{8,10},{9,11},{10,... | collective-permute-start | bytes 393224 | tf_op jit(solution)/shard_map/ppermute | solution.py:201
  31.4 0.0 collective-permute-done.10.refs_1_
  31.4 1.7 %collective-permute-done.12.refs_3_ = f32[64,512]{1,0:T(8,128)S(1)} collective-permute-done((f32[64,512]{1,0:T(8,128)S(1)}, f32[64,512]{1,0:T(8,128)S(1)}, u32[]{:S(2)}, u32[]{:S(2)}) %collective-permute-start.12) | collective-permute-done | bytes 131104 | tf_op jit(solution)/shard_map/ppermute | solution.py:195
  33.1 0.9 %collect.1 = (f32[64,2048]{1,0:T(8,128)S(1)}, f32[64,2048]{1,0:T(8,128)S(1)}) custom-call(s32[4,4]{1,0:T(4,128)S(1)} %pad_add_fusion.requests.ids, f32[64,512]{1,0:T(8,128)S(1)} %mode2.1.refs_0_, f32[64,512]{1,0:T(8,128)S(1)} %collective-permute-done.10.refs_1_, f32[64,512]{1,0:T(8,128)S(1)} %collective-permute-done.11.refs_2_, ...), custom_call_target="tpu_custom_call" | custom-call | tf_op jit(solution)/shard_map/collect/pallas_call | solution.py:285
  34.1 0.1 collective-permute-start.13
  34.2 2.6 %collective-permute-done.15.arrived = f32[64,512]{1,0:T(8,128)S(1)} collective-permute-done((f32[64,512]{1,0:T(8,128)S(1)}, f32[64,512]{1,0:T(8,128)S(1)}, u32[]{:S(2)}, u32[]{:S(2)}) %collective-permute-start.15) | collective-permute-done | bytes 131104 | tf_op jit(solution)/shard_map/ppermute | solution.py:201
  36.8 0.9 %finish_items.1 = (f32[64,2048]{1,0:T(8,128)}, f32[64,512]{1,0:T(8,128)}) custom-call(f32[64,2048]{1,0:T(8,128)S(1)} %get-tuple-element.21.own, f32[64,2048]{1,0:T(8,128)S(1)} %collective-permute-done.13.arrived, f32[64,512]{1,0:T(8,128)S(1)} %finish_users.1.users), custom_call_target="tpu_custom_call" | custom-call | tf_op jit(solution)/shard_map/finish_items/pallas_call | solution.py:307
  (25 shorter events, 0.1 us)
Async XLA Ops:
  0.6 9.2 %copy-start = (f32[64,2048]{1,0:T(8,128)S(1)}, f32[64,2048]{1,0:T(8,128)}, u32[]{:S(2)}) copy-start(f32[64,2048]{1,0:T(8,128)} %own.3) | copy-start | bytes 1572868
  0.6 9.2 %copy-start.4 = (s32[1,1,4]{2,1,0:T(1,128)S(1)}, s32[1,1,4]{2,1,0:T(1,128)}, u32[]{:S(2)}) copy-start(s32[1,1,4]{2,1,0:T(1,128)} %param.9) | copy-start | bytes 52
  0.7 9.2 %collective-permute-start.4 = (f32[64,2048]{1,0:T(8,128)}, f32[64,2048]{1,0:T(8,128)S(1)}, u32[]{:S(2)}, u32[]{:S(2)}) collective-permute-start(f32[64,2048]{1,0:T(8,128)} %own.3), channel_id=1, source_target_pairs={{0,4},{4,0},{8,12},{12,8},{16,20},{20,16},{24,28},{28,24},{1,5},{5... | collective-permute-start | bytes 1572872 | tf_op jit(solution)/shard_map/ppermute | solution.py:198
  1.2 8.0 %collective-permute-start = (s32[1,4]{1,0:T(1,128)}, s32[1,4]{1,0:T(1,128)S(1)}, u32[]{:S(2)}, u32[]{:S(2)}) collective-permute-start(s32[1,4]{1,0:T(1,128)} %bitcast.12), channel_id=1, source_target_pairs={{0,8},{4,12},{8,0},{12,4},{16,24},{20,28},{24,16},{28,20},{1,9},{5... | collective-permute-start | bytes 56 | tf_op jit(solution)/shard_map/ppermute | solution.py:195
  3.7 5.5 %collective-permute-start.1 = (s32[1,4]{1,0:T(1,128)}, s32[1,4]{1,0:T(1,128)S(1)}, u32[]{:S(2)}, u32[]{:S(2)}) collective-permute-start(s32[1,4]{1,0:T(1,128)} %bitcast.13), channel_id=1, source_target_pairs={{0,16},{4,20},{8,24},{12,28},{16,0},{20,4},{24,8},{28,12},{1,17},{... | collective-permute-start | bytes 56 | tf_op jit(solution)/shard_map/ppermute | solution.py:195
  5.3 4.6 %collective-permute-start.2 = (s32[1,4]{1,0:T(1,128)}, s32[1,4]{1,0:T(1,128)S(1)}, u32[]{:S(2)}, u32[]{:S(2)}) collective-permute-start(s32[1,4]{1,0:T(1,128)} %bitcast.14), channel_id=1, source_target_pairs={{0,24},{4,28},{8,16},{12,20},{16,8},{20,12},{24,0},{28,4},{1,25},{... | collective-permute-start | bytes 56 | tf_op jit(solution)/shard_map/ppermute | solution.py:195
  5.3 10.5 %collective-permute-start.3 = (f32[64,512]{1,0:T(8,128)}, f32[64,512]{1,0:T(8,128)S(1)}, u32[]{:S(2)}, u32[]{:S(2)}) collective-permute-start(f32[64,512]{1,0:T(8,128)} %refs_0_.1), channel_id=1, source_target_pairs={{0,2},{1,3},{2,0},{3,1},{4,6},{5,7},{6,4},{7,5},{8,10},{9,11},{10,... | collective-permute-start | bytes 393224 | tf_op jit(solution)/shard_map/ppermute | solution.py:201
  8.3 7.5 %slice-start = ((s8[8388608]{0:T(1024)(128)(4,1)}), s8[4194304]{0:T(1024)(128)(4,1)S(1)}, s32[]{:S(2)}) async-start(s8[8388608]{0:T(1024)(128)(4,1)} %bitcast.7), calls=%async_computation | async-start | bytes 8388608
  9.1 5.1 %copy-start.1 = (f32[64,512]{1,0:T(8,128)S(1)}, f32[64,512]{1,0:T(8,128)}, u32[]{:S(2)}) copy-start(f32[64,512]{1,0:T(8,128)} %refs_0_.1) | copy-start | bytes 393220
  9.1 6.7 %slice-start.1 = ((s8[8388608]{0:T(1024)(128)(4,1)}), s8[4194304]{0:T(1024)(128)(4,1)S(1)}, s32[]{:S(2)}) async-start(s8[8388608]{0:T(1024)(128)(4,1)} %bitcast.7), calls=%async_computation.1 | async-start | bytes 8388608
  9.1 6.7 %copy-start.2 = (f32[32,64]{1,0:T(8,128)S(1)}, f32[32,64]{1,0:T(8,128)}, u32[]{:S(2)}) copy-start(f32[32,64]{1,0:T(8,128)} %week_factor.1) | copy-start | bytes 24580
  9.2 10.3 %copy-start.3 = (s32[1,1,4]{2,1,0:T(1,128)S(1)}, s32[1,1,4]{2,1,0:T(1,128)}, u32[]{:S(2)}) copy-start(s32[1,1,4]{2,1,0:T(1,128)} %param.8) | copy-start | bytes 52
  10.7 6.5 %collective-permute-start.5 = (f32[64,512]{1,0:T(8,128)S(1)}, f32[64,512]{1,0:T(8,128)S(1)}, u32[]{:S(2)}, u32[]{:S(2)}) collective-permute-start(f32[64,512]{1,0:T(8,128)S(1)} %get-tuple-element.14._), channel_id=1, source_target_pairs={{0,8},{4,12},{8,0},{12,4},{16,24},{20,28},{24,16},{28,20},{1,9},{5... | collective-permute-start | bytes 393224 | tf_op jit(solution)/shard_map/ppermute | solution.py:195
  11.6 7.8 %collective-permute-start.6 = (f32[64,512]{1,0:T(8,128)S(1)}, f32[64,512]{1,0:T(8,128)S(1)}, u32[]{:S(2)}, u32[]{:S(2)}) collective-permute-start(f32[64,512]{1,0:T(8,128)S(1)} %get-tuple-element.17), channel_id=1, source_target_pairs={{0,16},{4,20},{8,24},{12,28},{16,0},{20,4},{24,8},{28,12},{1,17},{... | collective-permute-start | bytes 393224 | tf_op jit(solution)/shard_map/ppermute | solution.py:195
  13.2 6.3 %collective-permute-start.7 = (f32[64,512]{1,0:T(8,128)S(1)}, f32[64,512]{1,0:T(8,128)S(1)}, u32[]{:S(2)}, u32[]{:S(2)}) collective-permute-start(f32[64,512]{1,0:T(8,128)S(1)} %get-tuple-element.18), channel_id=1, source_target_pairs={{0,24},{4,28},{8,16},{12,20},{16,8},{20,12},{24,0},{28,4},{1,25},{... | collective-permute-start | bytes 393224 | tf_op jit(solution)/shard_map/ppermute | solution.py:195
  14.2 8.3 %collective-permute-start.8 = (f32[64,512]{1,0:T(8,128)S(1)}, f32[64,512]{1,0:T(8,128)S(1)}, u32[]{:S(2)}, u32[]{:S(2)}) collective-permute-start(f32[64,512]{1,0:T(8,128)S(1)} %copy-done.1), channel_id=1, source_target_pairs={{0,1},{1,0},{2,3},{3,2},{4,5},{5,4},{6,7},{7,6},{8,9},{9,8},{10,11... | collective-permute-start | bytes 393224 | tf_op jit(solution)/shard_map/ppermute | solution.py:201
  16.7 5.8 %collective-permute-start.9 = (f32[64,512]{1,0:T(8,128)S(1)}, f32[64,512]{1,0:T(8,128)S(1)}, u32[]{:S(2)}, u32[]{:S(2)}) collective-permute-start(f32[64,512]{1,0:T(8,128)S(1)} %get-tuple-element.20.refs_2_), channel_id=1, source_target_pairs={{0,1},{1,0},{2,3},{3,2},{4,5},{5,4},{6,7},{7,6},{8,9},{9,8},{10,11... | collective-permute-start | bytes 393224 | tf_op jit(solution)/shard_map/ppermute | solution.py:201
  20.9 7.8 %collective-permute-start.14 = (f32[2,64,512]{2,1,0:T(8,128)S(1)}, f32[2,64,512]{2,1,0:T(8,128)S(1)}, u32[]{:S(2)}, u32[]{:S(2)}) collective-permute-start(f32[2,64,512]{2,1,0:T(8,128)S(1)} %get-tuple-element.23), channel_id=1, source_target_pairs={{0,1},{1,0},{2,3},{3,2},{4,5},{5,4},{6,7},{7,6},{8,9},{9,8},{10,11... | collective-permute-start | bytes 786440 | tf_op jit(solution)/shard_map/ppermute | solution.py:201
  23.5 7.9 %collective-permute-start.10 = (f32[64,512]{1,0:T(8,128)S(1)}, f32[64,512]{1,0:T(8,128)S(1)}, u32[]{:S(2)}, u32[]{:S(2)}) collective-permute-start(f32[64,512]{1,0:T(8,128)S(1)} %mode2.1.refs_0_), channel_id=1, source_target_pairs={{0,8},{4,12},{8,0},{12,4},{16,24},{20,28},{24,16},{28,20},{1,9},{5... | collective-permute-start | bytes 393224 | tf_op jit(solution)/shard_map/ppermute | solution.py:195
  25.7 5.7 %collective-permute-start.11 = (f32[64,512]{1,0:T(8,128)S(1)}, f32[64,512]{1,0:T(8,128)S(1)}, u32[]{:S(2)}, u32[]{:S(2)}) collective-permute-start(f32[64,512]{1,0:T(8,128)S(1)} %mode2.1.refs_0_), channel_id=1, source_target_pairs={{0,16},{4,20},{8,24},{12,28},{16,0},{20,4},{24,8},{28,12},{1,17},{... | collective-permute-start | bytes 393224 | tf_op jit(solution)/shard_map/ppermute | solution.py:195
  27.3 5.9 %collective-permute-start.12 = (f32[64,512]{1,0:T(8,128)S(1)}, f32[64,512]{1,0:T(8,128)S(1)}, u32[]{:S(2)}, u32[]{:S(2)}) collective-permute-start(f32[64,512]{1,0:T(8,128)S(1)} %mode2.1.refs_0_), channel_id=1, source_target_pairs={{0,24},{4,28},{8,16},{12,20},{16,8},{20,12},{24,0},{28,4},{1,25},{... | collective-permute-start | bytes 393224 | tf_op jit(solution)/shard_map/ppermute | solution.py:195
  28.7 8.0 %collective-permute-start.15 = (f32[64,512]{1,0:T(8,128)S(1)}, f32[64,512]{1,0:T(8,128)S(1)}, u32[]{:S(2)}, u32[]{:S(2)}) collective-permute-start(f32[64,512]{1,0:T(8,128)S(1)} %get-tuple-element.26), channel_id=1, source_target_pairs={{0,2},{1,3},{2,0},{3,1},{4,6},{5,7},{6,4},{7,5},{8,10},{9,11},{10,... | collective-permute-start | bytes 393224 | tf_op jit(solution)/shard_map/ppermute | solution.py:201
  34.1 2.7 %collective-permute-start.13 = (f32[64,2048]{1,0:T(8,128)S(1)}, f32[64,2048]{1,0:T(8,128)S(1)}, u32[]{:S(2)}, u32[]{:S(2)}) collective-permute-start(f32[64,2048]{1,0:T(8,128)S(1)} %get-tuple-element.22), channel_id=1, source_target_pairs={{0,4},{4,0},{8,12},{12,8},{16,20},{20,16},{24,28},{28,24},{1,5},{5... | collective-permute-start | bytes 1572872 | tf_op jit(solution)/shard_map/ppermute | solution.py:198

commit v4 on v2

--- a/solution.py
+++ b/solution.py
@@ -100,14 +100,15 @@
     return quarters(sums, width // 2)
 
 
-def mode1_kernel(groups, units, count_ref, users_ref, items_ref, spread, tiles, own, sibling, *refs):
-    *messages, even, odd, sums = refs
+def mode1_kernel(units, count_ref, users_ref, items_ref, spread, tiles, own, sibling, *refs):
+    *messages, even, odd = refs
     height, width = tiles.shape[2], tiles.shape[3] // 2
     me = lax.axis_index("users")
     column = lax.axis_index("items")
     per_device = own.shape[1] // width
     kept = even.shape[2] // height
-    sums[...] = jnp.zeros_like(sums)
+    even[...] = jnp.zeros_like(even)
+    odd[...] = jnp.zeros_like(odd)
 
     def work(slot, carry):
         index = items_ref[0, slot]
@@ -118,17 +119,21 @@
         here = columns(slot, width)
         for step, message in enumerate(messages):
             items = jnp.where(source == step + 1, message[:, here], items)
-        sums[users_ref[0, slot]] += pl.run_scoped(
+        term = pl.run_scoped(
             lambda *held: user_term(spread, items, tiles.at[slot], held), *units
         )
+        block = users_ref[0, slot]
+        step = (block // kept) ^ column
+        place = columns(block % kept, height)
+        for parity, target in enumerate((even, odd)):
+
+            @pl.when(step % 2 == parity)
+            def _():
+                target[step // 2, :, place] += term
+
         return carry
 
     lax.fori_loop(0, count_ref[0, 0], work, 0)
-    for step in range(groups):
-        first = (column ^ step) * kept
-        for block in range(kept):
-            target = (even, odd)[step % 2]
-            target[step // 2, :, block * height : (block + 1) * height] = sums[first + block]
 
 
 def mode2_kernel(units, count_ref, users_ref, spread, tiles, _, *refs):
@@ -258,11 +263,10 @@
         step //= 2
 
     even, odd = pl.pallas_call(
-        functools.partial(mode1_kernel, groups, units),
+        functools.partial(mode1_kernel, units),
         out_shape=[array(groups // 2, rank, user_width)] * 2,
         in_specs=[SMEM] * 3 + [VMEM] * (3 + chips),
         out_specs=[VMEM] * 2,
-        scratch_shapes=[pltpu.VMEM((groups * user_width // height, rank, height), F32)],
         compiler_params=limit(8),
         cost_estimate=cost(1),
         name="mode1",
@@ -292,7 +296,8 @@
         even,
         *(row_factors[step] for step in range(groups)),
     )
-    near_terms = [terms] + [across_chips(terms, step) for step in range(1, chips)]
+    far_first = {step: across_chips(terms, step) for step in reversed(range(1, chips))}
+    near_terms = [terms] + [far_first[step] for step in range(1, chips)]
     own, other = pl.pallas_call(
         collect_kernel,
         out_shape=[array(*item_factor.shape)] * 2,

time: 37.5 us -> 38.1 us (1.016)
  waiting for transfers between devices: 5.41 us -> 9.86 us
  starting transfers between devices: 23.2 us -> 19.2 us
    ppermute x5, starting transfers between devices: 11.4 us -> 7.37 us  [across_groups(): return lax.ppermute(value, 'items', [(i, i ^ step) for i in range(groups)])]
    ppermute x5, waiting for transfers between devices: 2.51 us -> 5.32 us  [across_groups(): return lax.ppermute(value, 'items', [(i, i ^ step) for i in range(groups)])]
    ppermute x9, waiting for transfers between devices: 2.89 us -> 4.53 us  [across_chips(): lax.ppermute(value, 'users', [(i, i ^ 2 * step) for i in range(rows)])]
  transfers between devices with their start and end apart: 16 -> 16, of which waited for: 3 -> 7; matrix products, arithmetic and copies ran while one was open for 0% -> 0% of each run, Pallas kernels for 18% -> 17%
where the time goes in v4:
time: 38.1 us
  starting transfers between devices  19.2 us (50%)
  waiting for transfers between devices  9.86 us (26%)
  Pallas kernels  7.51 us (20%)
  between operations  1.44 us (4%)
    ppermute x9, starting transfers between devices, across_chips(): lax.ppermute(value, 'users', [(i, i ^ 2 * step) for i in range(rows)])  11.2 us
    ppermute x5, starting transfers between devices, across_groups(): return lax.ppermute(value, 'items', [(i, i ^ step) for i in range(groups)])  7.37 us
    ppermute x5, waiting for transfers between devices, across_groups(): return lax.ppermute(value, 'items', [(i, i ^ step) for i in range(groups)])  5.32 us
    ppermute x9, waiting for transfers between devices, across_chips(): lax.ppermute(value, 'users', [(i, i ^ 2 * step) for i in range(rows)])  4.53 us
    pallas_call x1, Pallas kernels, on_device(): pl.pallas_call(functools.partial(mode1_kernel, units), out_shape=[array(g...  2.16 us
    pallas_call x1, Pallas kernels, on_device(): pl.pallas_call(functools.partial(mode2_kernel, units), out_shape=array(ra...  1.45 us
    pallas_call x1, Pallas kernels, on_device(): pl.pallas_call(prepare_kernel, out_shape=[array(slots, weeks, height, 2 *...  1.2 us
    pallas_call x1, Pallas kernels, on_device(): pl.pallas_call(collect_kernel, out_shape=[array(*item_factor.shape)] * 2,...  0.96 us
  transfers between devices with their start and end apart: 16, of which 7 were waited for; matrix products, arithmetic and copies ran while one was open for 0% of the time, Pallas kernels for 17%

profile of v4, /device:TPU:0, one launch (start us, length us, event | category | flops | bytes accessed | tf_op | source)
XLA Modules:
  0.0 38.1 jit_solution(14903504898746224383)
XLA Ops:
  0.7 0.5 %collective-permute-start.4 = (f32[64,2048]{1,0:T(8,128)}, f32[64,2048]{1,0:T(8,128)S(1)}, u32[]{:S(2)}, u32[]{:S(2)}) collective-permute-start(f32[64,2048]{1,0:T(8,128)} %own.3), channel_id=1, source_target_pairs={{0,4},{4,0},{8,12},{12,8},{16,20},{20,16},{24,28},{28,24},{1,5},{5... | collective-permute-start | bytes 1572872 | tf_op jit(solution)/shard_map/ppermute | solution.py:215
  1.2 2.6 %collective-permute-start = (s32[1,4]{1,0:T(1,128)}, s32[1,4]{1,0:T(1,128)S(1)}, u32[]{:S(2)}, u32[]{:S(2)}) collective-permute-start(s32[1,4]{1,0:T(1,128)} %bitcast.12), channel_id=1, source_target_pairs={{0,8},{4,12},{8,0},{12,4},{16,24},{20,28},{24,16},{28,20},{1,9},{5... | collective-permute-start | bytes 56 | tf_op jit(solution)/shard_map/ppermute | solution.py:212
  3.8 1.5 %collective-permute-start.1 = (s32[1,4]{1,0:T(1,128)}, s32[1,4]{1,0:T(1,128)S(1)}, u32[]{:S(2)}, u32[]{:S(2)}) collective-permute-start(s32[1,4]{1,0:T(1,128)} %bitcast.13), channel_id=1, source_target_pairs={{0,16},{4,20},{8,24},{12,28},{16,0},{20,4},{24,8},{28,12},{1,17},{... | collective-permute-start | bytes 56 | tf_op jit(solution)/shard_map/ppermute | solution.py:212
  5.3 0.0 collective-permute-start.2
  5.3 3.0 %collective-permute-start.3 = (f32[64,512]{1,0:T(8,128)}, f32[64,512]{1,0:T(8,128)S(1)}, u32[]{:S(2)}, u32[]{:S(2)}) collective-permute-start(f32[64,512]{1,0:T(8,128)} %refs_0_.1), channel_id=1, source_target_pairs={{0,2},{1,3},{2,0},{3,1},{4,6},{5,7},{6,4},{7,5},{8,10},{9,11},{10,... | collective-permute-start | bytes 393224 | tf_op jit(solution)/shard_map/ppermute | solution.py:218
  8.4 0.0 collective-permute-done
  8.4 0.0 collective-permute-done.1
  8.4 1.5 %collective-permute-done.2 = s32[1,4]{1,0:T(1,128)S(1)} collective-permute-done((s32[1,4]{1,0:T(1,128)}, s32[1,4]{1,0:T(1,128)S(1)}, u32[]{:S(2)}, u32[]{:S(2)}) %collective-permute-start.2) | collective-permute-done | bytes 48 | tf_op jit(solution)/shard_map/ppermute | solution.py:212
  9.9 0.8 %serve.1 = (f32[64,512]{1,0:T(8,128)S(1)}, f32[64,512]{1,0:T(8,128)S(1)}, f32[64,512]{1,0:T(8,128)S(1)}) custom-call(s32[4,4]{1,0:T(4,128)S(1)} %pad_add_fusion.requests.ids, f32[64,2048]{1,0:T(8,128)S(1)} %copy-done, f32[64,2048]{1,0:T(8,128)S(1)} %collective-permute-done.4.sibling, f32[8,128]{1,0:T(8,128)S(1)} %hold.1._), custom_call_target="tpu_custom_call" | custom-call | flops 1073741824 | bytes 8388608 | tf_op jit(solution)/shard_map/serve/pallas_call | solution.py:236
  10.7 0.6 %collective-permute-start.5 = (f32[64,512]{1,0:T(8,128)S(1)}, f32[64,512]{1,0:T(8,128)S(1)}, u32[]{:S(2)}, u32[]{:S(2)}) collective-permute-start(f32[64,512]{1,0:T(8,128)S(1)} %get-tuple-element.14._), channel_id=1, source_target_pairs={{0,8},{4,12},{8,0},{12,4},{16,24},{20,28},{24,16},{28,20},{1,9},{5... | collective-permute-start | bytes 393224 | tf_op jit(solution)/shard_map/ppermute | solution.py:212
  11.3 1.0 %collective-permute-start.6 = (f32[64,512]{1,0:T(8,128)S(1)}, f32[64,512]{1,0:T(8,128)S(1)}, u32[]{:S(2)}, u32[]{:S(2)}) collective-permute-start(f32[64,512]{1,0:T(8,128)S(1)} %get-tuple-element.17), channel_id=1, source_target_pairs={{0,16},{4,20},{8,24},{12,28},{16,0},{20,4},{24,8},{28,12},{1,17},{... | collective-permute-start | bytes 393224 | tf_op jit(solution)/shard_map/ppermute | solution.py:212
  12.3 1.9 %collective-permute-start.7 = (f32[64,512]{1,0:T(8,128)S(1)}, f32[64,512]{1,0:T(8,128)S(1)}, u32[]{:S(2)}, u32[]{:S(2)}) collective-permute-start(f32[64,512]{1,0:T(8,128)S(1)} %get-tuple-element.18), channel_id=1, source_target_pairs={{0,24},{4,28},{8,16},{12,20},{16,8},{20,12},{24,0},{28,4},{1,25},{... | collective-permute-start | bytes 393224 | tf_op jit(solution)/shard_map/ppermute | solution.py:212
  14.3 1.6 %collective-permute-start.8 = (f32[64,512]{1,0:T(8,128)S(1)}, f32[64,512]{1,0:T(8,128)S(1)}, u32[]{:S(2)}, u32[]{:S(2)}) collective-permute-start(f32[64,512]{1,0:T(8,128)S(1)} %copy-done.1), channel_id=1, source_target_pairs={{0,1},{1,0},{2,3},{3,2},{4,5},{5,4},{6,7},{7,6},{8,9},{9,8},{10,11... | collective-permute-start | bytes 393224 | tf_op jit(solution)/shard_map/ppermute | solution.py:218
  16.6 1.2 %prepare.1 = (bf16[4,32,128,256]{3,2,1,0:T(8,128)(2,1)S(1)}, f32[32,64,128]{2,1,0:T(8,128)S(1)}, f32[64,512]{1,0:T(8,128)S(1)}) custom-call(s32[1,1]{1,0:T(1,128)S(6)} %copy.9.count_ref, f32[4,32,128,128]{3,2,1,0:T(8,128)S(1)} %bitcast.9, f32[32,64]{1,0:T(8,128)S(1)} %copy-done.2, f32[64,512]{1,0:T(8,128)S(1)} %collective-permute-done.3.users, ...), custom_call_target="tpu_custom_call" | custom-call | tf_op jit(solution)/shard_map/prepare/pallas_call | solution.py:247
  17.8 0.1 collective-permute-start.9
  17.9 1.0 %collective-permute-done.6.refs_1_ = f32[64,512]{1,0:T(8,128)S(1)} collective-permute-done((f32[64,512]{1,0:T(8,128)S(1)}, f32[64,512]{1,0:T(8,128)S(1)}, u32[]{:S(2)}, u32[]{:S(2)}) %collective-permute-start.6) | collective-permute-done | bytes 131104 | tf_op jit(solution)/shard_map/ppermute | solution.py:212
  19.0 0.0 collective-permute-done.7.refs_2_
  19.0 2.2 %mode1.1 = (f32[2,64,512]{2,1,0:T(8,128)S(1)}, f32[2,64,512]{2,1,0:T(8,128)S(1)}) custom-call(s32[1,1]{1,0:T(1,128)S(6)} %copy.9.count_ref, s32[1,4]{1,0:T(1,128)S(1)} %bitcast.10, s32[1,4]{1,0:T(1,128)S(1)} %bitcast.16, f32[32,64,128]{2,1,0:T(8,128)S(1)} %get-tuple-element.15.spread, bf16[4,32,128,256]{3,2,1,0:T(8,128)(2,1)S(1)} %get-tuple-element.16.tiles, ...), custom_call_target="tpu_custom_call" | custom-call | flops 1073741824 | bytes 8388608 | tf_op jit(solution)/shard_map/mode1/pallas_call | solution.py:265
  21.1 0.9 %collective-permute-start.14 = (f32[2,64,512]{2,1,0:T(8,128)S(1)}, f32[2,64,512]{2,1,0:T(8,128)S(1)}, u32[]{:S(2)}, u32[]{:S(2)}) collective-permute-start(f32[2,64,512]{2,1,0:T(8,128)S(1)} %get-tuple-element.23), channel_id=1, source_target_pairs={{0,1},{1,0},{2,3},{3,2},{4,5},{5,4},{6,7},{7,6},{8,9},{9,8},{10,11... | collective-permute-start | bytes 786440 | tf_op jit(solution)/shard_map/ppermute | solution.py:218
  22.0 0.8 %collective-permute-done.9.refs_3_ = f32[64,512]{1,0:T(8,128)S(1)} collective-permute-done((f32[64,512]{1,0:T(8,128)S(1)}, f32[64,512]{1,0:T(8,128)S(1)}, u32[]{:S(2)}, u32[]{:S(2)}) %collective-permute-start.9) | collective-permute-done | bytes 131104 | tf_op jit(solution)/shard_map/ppermute | solution.py:218
  22.8 1.4 %mode2.1.refs_0_ = f32[64,512]{1,0:T(8,128)S(1)} custom-call(s32[1,1]{1,0:T(1,128)S(6)} %copy.9.count_ref, s32[1,4]{1,0:T(1,128)S(1)} %bitcast.11, f32[32,64,128]{2,1,0:T(8,128)S(1)} %get-tuple-element.15.spread, bf16[4,32,128,256]{3,2,1,0:T(8,128)(2,1)S(1)} %get-tuple-element.16.tiles, f32[2,64,512]{2,1,0:T(8,128)S(1)} %get-tuple-element.19._, ...), custom_call_target="tpu_custom_call" | custom-call | flops 2147483648 | bytes 16777216 | tf_op jit(solution)/shard_map/mode2/pallas_call | solution.py:283
  24.3 1.1 %collective-permute-start.10 = (f32[64,512]{1,0:T(8,128)S(1)}, f32[64,512]{1,0:T(8,128)S(1)}, u32[]{:S(2)}, u32[]{:S(2)}) collective-permute-start(f32[64,512]{1,0:T(8,128)S(1)} %mode2.1.refs_0_), channel_id=1, source_target_pairs={{0,8},{4,12},{8,0},{12,4},{16,24},{20,28},{24,16},{28,20},{1,9},{5... | collective-permute-start | bytes 393224 | tf_op jit(solution)/shard_map/ppermute | solution.py:212
  25.3 2.1 %collective-permute-start.11 = (f32[64,512]{1,0:T(8,128)S(1)}, f32[64,512]{1,0:T(8,128)S(1)}, u32[]{:S(2)}, u32[]{:S(2)}) collective-permute-start(f32[64,512]{1,0:T(8,128)S(1)} %mode2.1.refs_0_), channel_id=1, source_target_pairs={{0,16},{4,20},{8,24},{12,28},{16,0},{20,4},{24,8},{28,12},{1,17},{... | collective-permute-start | bytes 393224 | tf_op jit(solution)/shard_map/ppermute | solution.py:212
  27.4 0.4 %collective-permute-start.12 = (f32[64,512]{1,0:T(8,128)S(1)}, f32[64,512]{1,0:T(8,128)S(1)}, u32[]{:S(2)}, u32[]{:S(2)}) collective-permute-start(f32[64,512]{1,0:T(8,128)S(1)} %mode2.1.refs_0_), channel_id=1, source_target_pairs={{0,24},{4,28},{8,16},{12,20},{16,8},{20,12},{24,0},{28,4},{1,25},{... | collective-permute-start | bytes 393224 | tf_op jit(solution)/shard_map/ppermute | solution.py:212
  27.8 1.7 %collective-permute-done.14 = f32[2,64,512]{2,1,0:T(8,128)S(1)} collective-permute-done((f32[2,64,512]{2,1,0:T(8,128)S(1)}, f32[2,64,512]{2,1,0:T(8,128)S(1)}, u32[]{:S(2)}, u32[]{:S(2)}) %collective-permute-start.14) | collective-permute-done | bytes 262176 | tf_op jit(solution)/shard_map/ppermute | solution.py:218
  29.6 1.7 %collective-permute-start.15 = (f32[64,512]{1,0:T(8,128)S(1)}, f32[64,512]{1,0:T(8,128)S(1)}, u32[]{:S(2)}, u32[]{:S(2)}) collective-permute-start(f32[64,512]{1,0:T(8,128)S(1)} %get-tuple-element.26), channel_id=1, source_target_pairs={{0,2},{1,3},{2,0},{3,1},{4,6},{5,7},{6,4},{7,5},{8,10},{9,11},{10,... | collective-permute-start | bytes 393224 | tf_op jit(solution)/shard_map/ppermute | solution.py:218
  31.3 0.4 %collective-permute-done.11.refs_2_ = f32[64,512]{1,0:T(8,128)S(1)} collective-permute-done((f32[64,512]{1,0:T(8,128)S(1)}, f32[64,512]{1,0:T(8,128)S(1)}, u32[]{:S(2)}, u32[]{:S(2)}) %collective-permute-start.11) | collective-permute-done | bytes 131104 | tf_op jit(solution)/shard_map/ppermute | solution.py:212
  31.7 1.6 %collective-permute-done.12.refs_3_ = f32[64,512]{1,0:T(8,128)S(1)} collective-permute-done((f32[64,512]{1,0:T(8,128)S(1)}, f32[64,512]{1,0:T(8,128)S(1)}, u32[]{:S(2)}, u32[]{:S(2)}) %collective-permute-start.12) | collective-permute-done | bytes 131104 | tf_op jit(solution)/shard_map/ppermute | solution.py:212
  33.3 1.0 %collect.1 = (f32[64,2048]{1,0:T(8,128)S(1)}, f32[64,2048]{1,0:T(8,128)S(1)}) custom-call(s32[4,4]{1,0:T(4,128)S(1)} %pad_add_fusion.requests.ids, f32[64,512]{1,0:T(8,128)S(1)} %mode2.1.refs_0_, f32[64,512]{1,0:T(8,128)S(1)} %collective-permute-done.10.refs_1_, f32[64,512]{1,0:T(8,128)S(1)} %collective-permute-done.11.refs_2_, ...), custom_call_target="tpu_custom_call" | custom-call | tf_op jit(solution)/shard_map/collect/pallas_call | solution.py:301
  34.3 0.1 collective-permute-start.13
  34.3 2.8 %collective-permute-done.15.arrived = f32[64,512]{1,0:T(8,128)S(1)} collective-permute-done((f32[64,512]{1,0:T(8,128)S(1)}, f32[64,512]{1,0:T(8,128)S(1)}, u32[]{:S(2)}, u32[]{:S(2)}) %collective-permute-start.15) | collective-permute-done | bytes 131104 | tf_op jit(solution)/shard_map/ppermute | solution.py:218
  37.2 0.9 %finish_items.1 = (f32[64,2048]{1,0:T(8,128)}, f32[64,512]{1,0:T(8,128)}) custom-call(f32[64,2048]{1,0:T(8,128)S(1)} %get-tuple-element.21.own, f32[64,2048]{1,0:T(8,128)S(1)} %collective-permute-done.13.arrived, f32[64,512]{1,0:T(8,128)S(1)} %finish_users.1.users), custom_call_target="tpu_custom_call" | custom-call | tf_op jit(solution)/shard_map/finish_items/pallas_call | solution.py:323
  (25 shorter events, 0.1 us)
Async XLA Ops:
  0.6 9.3 %copy-start = (f32[64,2048]{1,0:T(8,128)S(1)}, f32[64,2048]{1,0:T(8,128)}, u32[]{:S(2)}) copy-start(f32[64,2048]{1,0:T(8,128)} %own.3) | copy-start | bytes 1572868
  0.6 9.2 %copy-start.4 = (s32[1,1,4]{2,1,0:T(1,128)S(1)}, s32[1,1,4]{2,1,0:T(1,128)}, u32[]{:S(2)}) copy-start(s32[1,1,4]{2,1,0:T(1,128)} %param.9) | copy-start | bytes 52
  0.7 9.2 %collective-permute-start.4 = (f32[64,2048]{1,0:T(8,128)}, f32[64,2048]{1,0:T(8,128)S(1)}, u32[]{:S(2)}, u32[]{:S(2)}) collective-permute-start(f32[64,2048]{1,0:T(8,128)} %own.3), channel_id=1, source_target_pairs={{0,4},{4,0},{8,12},{12,8},{16,20},{20,16},{24,28},{28,24},{1,5},{5... | collective-permute-start | bytes 1572872 | tf_op jit(solution)/shard_map/ppermute | solution.py:215
  1.2 15.4 %slice-start = ((s8[8388608]{0:T(1024)(128)(4,1)}), s8[4194304]{0:T(1024)(128)(4,1)S(1)}, s32[]{:S(2)}) async-start(s8[8388608]{0:T(1024)(128)(4,1)} %bitcast.7), calls=%async_computation | async-start | bytes 8388608
  1.2 13.1 %copy-start.1 = (f32[64,512]{1,0:T(8,128)S(1)}, f32[64,512]{1,0:T(8,128)}, u32[]{:S(2)}) copy-start(f32[64,512]{1,0:T(8,128)} %refs_0_.1) | copy-start | bytes 393220
  1.2 15.4 %slice-start.1 = ((s8[8388608]{0:T(1024)(128)(4,1)}), s8[4194304]{0:T(1024)(128)(4,1)S(1)}, s32[]{:S(2)}) async-start(s8[8388608]{0:T(1024)(128)(4,1)} %bitcast.7), calls=%async_computation.1 | async-start | bytes 8388608
  1.2 15.4 %copy-start.2 = (f32[32,64]{1,0:T(8,128)S(1)}, f32[32,64]{1,0:T(8,128)}, u32[]{:S(2)}) copy-start(f32[32,64]{1,0:T(8,128)} %week_factor.1) | copy-start | bytes 24580
  1.2 7.2 %collective-permute-start = (s32[1,4]{1,0:T(1,128)}, s32[1,4]{1,0:T(1,128)S(1)}, u32[]{:S(2)}, u32[]{:S(2)}) collective-permute-start(s32[1,4]{1,0:T(1,128)} %bitcast.12), channel_id=1, source_target_pairs={{0,8},{4,12},{8,0},{12,4},{16,24},{20,28},{24,16},{28,20},{1,9},{5... | collective-permute-start | bytes 56 | tf_op jit(solution)/shard_map/ppermute | solution.py:212
  3.8 4.6 %collective-permute-start.1 = (s32[1,4]{1,0:T(1,128)}, s32[1,4]{1,0:T(1,128)S(1)}, u32[]{:S(2)}, u32[]{:S(2)}) collective-permute-start(s32[1,4]{1,0:T(1,128)} %bitcast.13), channel_id=1, source_target_pairs={{0,16},{4,20},{8,24},{12,28},{16,0},{20,4},{24,8},{28,12},{1,17},{... | collective-permute-start | bytes 56 | tf_op jit(solution)/shard_map/ppermute | solution.py:212
  5.3 4.6 %collective-permute-start.2 = (s32[1,4]{1,0:T(1,128)}, s32[1,4]{1,0:T(1,128)S(1)}, u32[]{:S(2)}, u32[]{:S(2)}) collective-permute-start(s32[1,4]{1,0:T(1,128)} %bitcast.14), channel_id=1, source_target_pairs={{0,24},{4,28},{8,16},{12,20},{16,8},{20,12},{24,0},{28,4},{1,25},{... | collective-permute-start | bytes 56 | tf_op jit(solution)/shard_map/ppermute | solution.py:212
  5.3 11.2 %collective-permute-start.3 = (f32[64,512]{1,0:T(8,128)}, f32[64,512]{1,0:T(8,128)S(1)}, u32[]{:S(2)}, u32[]{:S(2)}) collective-permute-start(f32[64,512]{1,0:T(8,128)} %refs_0_.1), channel_id=1, source_target_pairs={{0,2},{1,3},{2,0},{3,1},{4,6},{5,7},{6,4},{7,5},{8,10},{9,11},{10,... | collective-permute-start | bytes 393224 | tf_op jit(solution)/shard_map/ppermute | solution.py:218
  8.4 10.6 %copy-start.3 = (s32[1,1,4]{2,1,0:T(1,128)S(1)}, s32[1,1,4]{2,1,0:T(1,128)}, u32[]{:S(2)}) copy-start(s32[1,1,4]{2,1,0:T(1,128)} %param.8) | copy-start | bytes 52
  10.7 7.2 %collective-permute-start.5 = (f32[64,512]{1,0:T(8,128)S(1)}, f32[64,512]{1,0:T(8,128)S(1)}, u32[]{:S(2)}, u32[]{:S(2)}) collective-permute-start(f32[64,512]{1,0:T(8,128)S(1)} %get-tuple-element.14._), channel_id=1, source_target_pairs={{0,8},{4,12},{8,0},{12,4},{16,24},{20,28},{24,16},{28,20},{1,9},{5... | collective-permute-start | bytes 393224 | tf_op jit(solution)/shard_map/ppermute | solution.py:212
  11.3 7.6 %collective-permute-start.6 = (f32[64,512]{1,0:T(8,128)S(1)}, f32[64,512]{1,0:T(8,128)S(1)}, u32[]{:S(2)}, u32[]{:S(2)}) collective-permute-start(f32[64,512]{1,0:T(8,128)S(1)} %get-tuple-element.17), channel_id=1, source_target_pairs={{0,16},{4,20},{8,24},{12,28},{16,0},{20,4},{24,8},{28,12},{1,17},{... | collective-permute-start | bytes 393224 | tf_op jit(solution)/shard_map/ppermute | solution.py:212
  12.3 6.6 %collective-permute-start.7 = (f32[64,512]{1,0:T(8,128)S(1)}, f32[64,512]{1,0:T(8,128)S(1)}, u32[]{:S(2)}, u32[]{:S(2)}) collective-permute-start(f32[64,512]{1,0:T(8,128)S(1)} %get-tuple-element.18), channel_id=1, source_target_pairs={{0,24},{4,28},{8,16},{12,20},{16,8},{20,12},{24,0},{28,4},{1,25},{... | collective-permute-start | bytes 393224 | tf_op jit(solution)/shard_map/ppermute | solution.py:212
  14.3 7.7 %collective-permute-start.8 = (f32[64,512]{1,0:T(8,128)S(1)}, f32[64,512]{1,0:T(8,128)S(1)}, u32[]{:S(2)}, u32[]{:S(2)}) collective-permute-start(f32[64,512]{1,0:T(8,128)S(1)} %copy-done.1), channel_id=1, source_target_pairs={{0,1},{1,0},{2,3},{3,2},{4,5},{5,4},{6,7},{7,6},{8,9},{9,8},{10,11... | collective-permute-start | bytes 393224 | tf_op jit(solution)/shard_map/ppermute | solution.py:218
  17.8 5.0 %collective-permute-start.9 = (f32[64,512]{1,0:T(8,128)S(1)}, f32[64,512]{1,0:T(8,128)S(1)}, u32[]{:S(2)}, u32[]{:S(2)}) collective-permute-start(f32[64,512]{1,0:T(8,128)S(1)} %get-tuple-element.20.refs_2_), channel_id=1, source_target_pairs={{0,1},{1,0},{2,3},{3,2},{4,5},{5,4},{6,7},{7,6},{8,9},{9,8},{10,11... | collective-permute-start | bytes 393224 | tf_op jit(solution)/shard_map/ppermute | solution.py:218
  21.1 8.4 %collective-permute-start.14 = (f32[2,64,512]{2,1,0:T(8,128)S(1)}, f32[2,64,512]{2,1,0:T(8,128)S(1)}, u32[]{:S(2)}, u32[]{:S(2)}) collective-permute-start(f32[2,64,512]{2,1,0:T(8,128)S(1)} %get-tuple-element.23), channel_id=1, source_target_pairs={{0,1},{1,0},{2,3},{3,2},{4,5},{5,4},{6,7},{7,6},{8,9},{9,8},{10,11... | collective-permute-start | bytes 786440 | tf_op jit(solution)/shard_map/ppermute | solution.py:218
  24.3 7.0 %collective-permute-start.10 = (f32[64,512]{1,0:T(8,128)S(1)}, f32[64,512]{1,0:T(8,128)S(1)}, u32[]{:S(2)}, u32[]{:S(2)}) collective-permute-start(f32[64,512]{1,0:T(8,128)S(1)} %mode2.1.refs_0_), channel_id=1, source_target_pairs={{0,8},{4,12},{8,0},{12,4},{16,24},{20,28},{24,16},{28,20},{1,9},{5... | collective-permute-start | bytes 393224 | tf_op jit(solution)/shard_map/ppermute | solution.py:212
  25.3 6.4 %collective-permute-start.11 = (f32[64,512]{1,0:T(8,128)S(1)}, f32[64,512]{1,0:T(8,128)S(1)}, u32[]{:S(2)}, u32[]{:S(2)}) collective-permute-start(f32[64,512]{1,0:T(8,128)S(1)} %mode2.1.refs_0_), channel_id=1, source_target_pairs={{0,16},{4,20},{8,24},{12,28},{16,0},{20,4},{24,8},{28,12},{1,17},{... | collective-permute-start | bytes 393224 | tf_op jit(solution)/shard_map/ppermute | solution.py:212
  27.4 5.9 %collective-permute-start.12 = (f32[64,512]{1,0:T(8,128)S(1)}, f32[64,512]{1,0:T(8,128)S(1)}, u32[]{:S(2)}, u32[]{:S(2)}) collective-permute-start(f32[64,512]{1,0:T(8,128)S(1)} %mode2.1.refs_0_), channel_id=1, source_target_pairs={{0,24},{4,28},{8,16},{12,20},{16,8},{20,12},{24,0},{28,4},{1,25},{... | collective-permute-start | bytes 393224 | tf_op jit(solution)/shard_map/ppermute | solution.py:212
  29.6 7.6 %collective-permute-start.15 = (f32[64,512]{1,0:T(8,128)S(1)}, f32[64,512]{1,0:T(8,128)S(1)}, u32[]{:S(2)}, u32[]{:S(2)}) collective-permute-start(f32[64,512]{1,0:T(8,128)S(1)} %get-tuple-element.26), channel_id=1, source_target_pairs={{0,2},{1,3},{2,0},{3,1},{4,6},{5,7},{6,4},{7,5},{8,10},{9,11},{10,... | collective-permute-start | bytes 393224 | tf_op jit(solution)/shard_map/ppermute | solution.py:218
  34.3 2.9 %collective-permute-start.13 = (f32[64,2048]{1,0:T(8,128)S(1)}, f32[64,2048]{1,0:T(8,128)S(1)}, u32[]{:S(2)}, u32[]{:S(2)}) collective-permute-start(f32[64,2048]{1,0:T(8,128)S(1)} %get-tuple-element.22), channel_id=1, source_target_pairs={{0,4},{4,0},{8,12},{12,8},{16,20},{20,16},{24,28},{28,24},{1,5},{5... | collective-permute-start | bytes 1572872 | tf_op jit(solution)/shard_map/ppermute | solution.py:215

commit v5 on v4

--- a/solution.py
+++ b/solution.py
@@ -42,7 +42,7 @@
             halves[slot, week, :, width:] = low
             return inner
 
-        return lax.fori_loop(0, weeks, one, carry, unroll=8)
+        return lax.fori_loop(0, weeks, one, carry, unroll=16)
 
     lax.fori_loop(0, count_ref[0, 0], work, 0)
 

time: 38.1 us -> 38.3 us (level)
  Pallas kernels: 7.51 us -> 10.7 us
  waiting for transfers between devices: 9.86 us -> 8.36 us
  starting transfers between devices: 19.2 us -> 17.9 us
    ppermute x5, waiting for transfers between devices: 5.32 us -> 2.55 us  [across_groups(): return lax.ppermute(value, 'items', [(i, i ^ step) for i in range(groups)])]
    pallas_call x1, Pallas kernels: 2.16 us -> 3.76 us  [on_device(): pl.pallas_call(functools.partial(mode1_kernel, units), out_shape=[array(g...]
    ppermute x5, starting transfers between devices: 7.37 us -> 6.06 us  [across_groups(): return lax.ppermute(value, 'items', [(i, i ^ step) for i in range(groups)])]
    ppermute x9, waiting for transfers between devices: 4.53 us -> 5.81 us  [across_chips(): lax.ppermute(value, 'users', [(i, i ^ 2 * step) for i in range(rows)])]
    pallas_call x1, Pallas kernels: 1.45 us -> 2.36 us  [on_device(): pl.pallas_call(functools.partial(mode2_kernel, units), out_shape=array(ra...]
    pallas_call x1, Pallas kernels: 1.2 us -> 1.89 us  [on_device(): pl.pallas_call(prepare_kernel, out_shape=[array(slots, weeks, height, 2 *...]
  transfers between devices with their start and end apart: 16 -> 16, of which waited for: 7 -> 7; matrix products, arithmetic and copies ran while one was open for 0% -> 0% of each run, Pallas kernels for 17% -> 25%
where the time goes in v5:
time: 38.3 us; the launch traced here: 38.5 us
  starting transfers between devices  17.9 us (47%)
  Pallas kernels  10.7 us (28%)
  waiting for transfers between devices  8.36 us (22%)
  between operations  1.47 us (4%)
    ppermute x9, starting transfers between devices, across_chips(): lax.ppermute(value, 'users', [(i, i ^ 2 * step) for i in range(rows)])  11.2 us
    ppermute x5, starting transfers between devices, across_groups(): return lax.ppermute(value, 'items', [(i, i ^ step) for i in range(groups)])  6.06 us
    ppermute x9, waiting for transfers between devices, across_chips(): lax.ppermute(value, 'users', [(i, i ^ 2 * step) for i in range(rows)])  5.81 us
    pallas_call x1, Pallas kernels, on_device(): pl.pallas_call(functools.partial(mode1_kernel, units), out_shape=[array(g...  3.76 us
    ppermute x5, waiting for transfers between devices, across_groups(): return lax.ppermute(value, 'items', [(i, i ^ step) for i in range(groups)])  2.55 us
    pallas_call x1, Pallas kernels, on_device(): pl.pallas_call(functools.partial(mode2_kernel, units), out_shape=array(ra...  2.36 us
    pallas_call x1, Pallas kernels, on_device(): pl.pallas_call(prepare_kernel, out_shape=[array(slots, weeks, height, 2 *...  1.89 us
    pallas_call x1, Pallas kernels, on_device(): pl.pallas_call(collect_kernel, out_shape=[array(*item_factor.shape)] * 2,...  0.95 us
  transfers between devices with their start and end apart: 16, of which 7 were waited for; matrix products, arithmetic and copies ran while one was open for 0% of the time, Pallas kernels for 25%

profile of v5, /device:TPU:0, one launch (start us, length us, event | category | flops | bytes accessed | tf_op | source)
XLA Modules:
  0.0 38.5 jit_solution(517846352791474960)
XLA Ops:
  0.7 0.5 %collective-permute-start.4 = (f32[64,2048]{1,0:T(8,128)}, f32[64,2048]{1,0:T(8,128)S(1)}, u32[]{:S(2)}, u32[]{:S(2)}) collective-permute-start(f32[64,2048]{1,0:T(8,128)} %own.3), channel_id=1, source_target_pairs={{0,4},{4,0},{8,12},{12,8},{16,20},{20,16},{24,28},{28,24},{1,5},{5... | collective-permute-start | bytes 1572872 | tf_op jit(solution)/shard_map/ppermute | solution.py:215
  1.2 2.6 %collective-permute-start = (s32[1,4]{1,0:T(1,128)}, s32[1,4]{1,0:T(1,128)S(1)}, u32[]{:S(2)}, u32[]{:S(2)}) collective-permute-start(s32[1,4]{1,0:T(1,128)} %bitcast.12), channel_id=1, source_target_pairs={{0,8},{4,12},{8,0},{12,4},{16,24},{20,28},{24,16},{28,20},{1,9},{5... | collective-permute-start | bytes 56 | tf_op jit(solution)/shard_map/ppermute | solution.py:212
  3.8 1.5 %collective-permute-start.1 = (s32[1,4]{1,0:T(1,128)}, s32[1,4]{1,0:T(1,128)S(1)}, u32[]{:S(2)}, u32[]{:S(2)}) collective-permute-start(s32[1,4]{1,0:T(1,128)} %bitcast.13), channel_id=1, source_target_pairs={{0,16},{4,20},{8,24},{12,28},{16,0},{20,4},{24,8},{28,12},{1,17},{... | collective-permute-start | bytes 56 | tf_op jit(solution)/shard_map/ppermute | solution.py:212
  5.3 0.0 collective-permute-start.2
  5.3 3.0 %collective-permute-start.3 = (f32[64,512]{1,0:T(8,128)}, f32[64,512]{1,0:T(8,128)S(1)}, u32[]{:S(2)}, u32[]{:S(2)}) collective-permute-start(f32[64,512]{1,0:T(8,128)} %refs_0_.1), channel_id=1, source_target_pairs={{0,2},{1,3},{2,0},{3,1},{4,6},{5,7},{6,4},{7,5},{8,10},{9,11},{10,... | collective-permute-start | bytes 393224 | tf_op jit(solution)/shard_map/ppermute | solution.py:218
  8.4 0.0 collective-permute-done
  8.4 0.0 collective-permute-done.1
  8.4 1.5 %collective-permute-done.2 = s32[1,4]{1,0:T(1,128)S(1)} collective-permute-done((s32[1,4]{1,0:T(1,128)}, s32[1,4]{1,0:T(1,128)S(1)}, u32[]{:S(2)}, u32[]{:S(2)}) %collective-permute-start.2) | collective-permute-done | bytes 48 | tf_op jit(solution)/shard_map/ppermute | solution.py:212
  9.9 0.0 collective-permute-done.4.sibling
  9.9 0.8 %serve.1 = (f32[64,512]{1,0:T(8,128)S(1)}, f32[64,512]{1,0:T(8,128)S(1)}, f32[64,512]{1,0:T(8,128)S(1)}) custom-call(s32[4,4]{1,0:T(4,128)S(1)} %pad_add_fusion.requests.ids, f32[64,2048]{1,0:T(8,128)S(1)} %copy-done, f32[64,2048]{1,0:T(8,128)S(1)} %collective-permute-done.4.sibling, f32[8,128]{1,0:T(8,128)S(1)} %hold.1._), custom_call_target="tpu_custom_call" | custom-call | flops 1073741824 | bytes 8388608 | tf_op jit(solution)/shard_map/serve/pallas_call | solution.py:236
  10.7 0.6 %collective-permute-start.5 = (f32[64,512]{1,0:T(8,128)S(1)}, f32[64,512]{1,0:T(8,128)S(1)}, u32[]{:S(2)}, u32[]{:S(2)}) collective-permute-start(f32[64,512]{1,0:T(8,128)S(1)} %get-tuple-element.14._), channel_id=1, source_target_pairs={{0,8},{4,12},{8,0},{12,4},{16,24},{20,28},{24,16},{28,20},{1,9},{5... | collective-permute-start | bytes 393224 | tf_op jit(solution)/shard_map/ppermute | solution.py:212
  11.3 1.0 %collective-permute-start.6 = (f32[64,512]{1,0:T(8,128)S(1)}, f32[64,512]{1,0:T(8,128)S(1)}, u32[]{:S(2)}, u32[]{:S(2)}) collective-permute-start(f32[64,512]{1,0:T(8,128)S(1)} %get-tuple-element.17), channel_id=1, source_target_pairs={{0,16},{4,20},{8,24},{12,28},{16,0},{20,4},{24,8},{28,12},{1,17},{... | collective-permute-start | bytes 393224 | tf_op jit(solution)/shard_map/ppermute | solution.py:212
  12.3 1.9 %collective-permute-start.7 = (f32[64,512]{1,0:T(8,128)S(1)}, f32[64,512]{1,0:T(8,128)S(1)}, u32[]{:S(2)}, u32[]{:S(2)}) collective-permute-start(f32[64,512]{1,0:T(8,128)S(1)} %get-tuple-element.18), channel_id=1, source_target_pairs={{0,24},{4,28},{8,16},{12,20},{16,8},{20,12},{24,0},{28,4},{1,25},{... | collective-permute-start | bytes 393224 | tf_op jit(solution)/shard_map/ppermute | solution.py:212
  14.3 1.6 %collective-permute-start.8 = (f32[64,512]{1,0:T(8,128)S(1)}, f32[64,512]{1,0:T(8,128)S(1)}, u32[]{:S(2)}, u32[]{:S(2)}) collective-permute-start(f32[64,512]{1,0:T(8,128)S(1)} %copy-done.1), channel_id=1, source_target_pairs={{0,1},{1,0},{2,3},{3,2},{4,5},{5,4},{6,7},{7,6},{8,9},{9,8},{10,11... | collective-permute-start | bytes 393224 | tf_op jit(solution)/shard_map/ppermute | solution.py:218
  16.6 1.9 %prepare.1 = (bf16[4,32,128,256]{3,2,1,0:T(8,128)(2,1)S(1)}, f32[32,64,128]{2,1,0:T(8,128)S(1)}, f32[64,512]{1,0:T(8,128)S(1)}) custom-call(s32[1,1]{1,0:T(1,128)S(6)} %copy.9.count_ref, f32[4,32,128,128]{3,2,1,0:T(8,128)S(1)} %bitcast.9, f32[32,64]{1,0:T(8,128)S(1)} %copy-done.2, f32[64,512]{1,0:T(8,128)S(1)} %collective-permute-done.3.users, ...), custom_call_target="tpu_custom_call" | custom-call | tf_op jit(solution)/shard_map/prepare/pallas_call | solution.py:247
  18.5 0.1 collective-permute-start.9
  18.5 0.4 %collective-permute-done.6.refs_1_ = f32[64,512]{1,0:T(8,128)S(1)} collective-permute-done((f32[64,512]{1,0:T(8,128)S(1)}, f32[64,512]{1,0:T(8,128)S(1)}, u32[]{:S(2)}, u32[]{:S(2)}) %collective-permute-start.6) | collective-permute-done | bytes 131104 | tf_op jit(solution)/shard_map/ppermute | solution.py:212
  19.0 3.8 %mode1.1 = (f32[2,64,512]{2,1,0:T(8,128)S(1)}, f32[2,64,512]{2,1,0:T(8,128)S(1)}) custom-call(s32[1,1]{1,0:T(1,128)S(6)} %copy.9.count_ref, s32[1,4]{1,0:T(1,128)S(1)} %bitcast.10, s32[1,4]{1,0:T(1,128)S(1)} %bitcast.16, f32[32,64,128]{2,1,0:T(8,128)S(1)} %get-tuple-element.15.spread, bf16[4,32,128,256]{3,2,1,0:T(8,128)(2,1)S(1)} %get-tuple-element.16.tiles, ...), custom_call_target="tpu_custom_call" | custom-call | flops 1073741824 | bytes 8388608 | tf_op jit(solution)/shard_map/mode1/pallas_call | solution.py:265
  22.7 0.1 collective-permute-start.14
  22.8 0.7 %collective-permute-done.9.refs_3_ = f32[64,512]{1,0:T(8,128)S(1)} collective-permute-done((f32[64,512]{1,0:T(8,128)S(1)}, f32[64,512]{1,0:T(8,128)S(1)}, u32[]{:S(2)}, u32[]{:S(2)}) %collective-permute-start.9) | collective-permute-done | bytes 131104 | tf_op jit(solution)/shard_map/ppermute | solution.py:218
  23.5 2.4 %mode2.1.refs_0_ = f32[64,512]{1,0:T(8,128)S(1)} custom-call(s32[1,1]{1,0:T(1,128)S(6)} %copy.9.count_ref, s32[1,4]{1,0:T(1,128)S(1)} %bitcast.11, f32[32,64,128]{2,1,0:T(8,128)S(1)} %get-tuple-element.15.spread, bf16[4,32,128,256]{3,2,1,0:T(8,128)(2,1)S(1)} %get-tuple-element.16.tiles, f32[2,64,512]{2,1,0:T(8,128)S(1)} %get-tuple-element.19._, ...), custom_call_target="tpu_custom_call" | custom-call | flops 2147483648 | bytes 16777216 | tf_op jit(solution)/shard_map/mode2/pallas_call | solution.py:283
  25.9 1.8 %collective-permute-start.10 = (f32[64,512]{1,0:T(8,128)S(1)}, f32[64,512]{1,0:T(8,128)S(1)}, u32[]{:S(2)}, u32[]{:S(2)}) collective-permute-start(f32[64,512]{1,0:T(8,128)S(1)} %mode2.1.refs_0_), channel_id=1, source_target_pairs={{0,8},{4,12},{8,0},{12,4},{16,24},{20,28},{24,16},{28,20},{1,9},{5... | collective-permute-start | bytes 393224 | tf_op jit(solution)/shard_map/ppermute | solution.py:212
  27.6 1.1 %collective-permute-start.11 = (f32[64,512]{1,0:T(8,128)S(1)}, f32[64,512]{1,0:T(8,128)S(1)}, u32[]{:S(2)}, u32[]{:S(2)}) collective-permute-start(f32[64,512]{1,0:T(8,128)S(1)} %mode2.1.refs_0_), channel_id=1, source_target_pairs={{0,16},{4,20},{8,24},{12,28},{16,0},{20,4},{24,8},{28,12},{1,17},{... | collective-permute-start | bytes 393224 | tf_op jit(solution)/shard_map/ppermute | solution.py:212
  28.8 0.6 %collective-permute-start.12 = (f32[64,512]{1,0:T(8,128)S(1)}, f32[64,512]{1,0:T(8,128)S(1)}, u32[]{:S(2)}, u32[]{:S(2)}) collective-permute-start(f32[64,512]{1,0:T(8,128)S(1)} %mode2.1.refs_0_), channel_id=1, source_target_pairs={{0,24},{4,28},{8,16},{12,20},{16,8},{20,12},{24,0},{28,4},{1,25},{... | collective-permute-start | bytes 393224 | tf_op jit(solution)/shard_map/ppermute | solution.py:212
  29.5 1.3 %collective-permute-start.15 = (f32[64,512]{1,0:T(8,128)S(1)}, f32[64,512]{1,0:T(8,128)S(1)}, u32[]{:S(2)}, u32[]{:S(2)}) collective-permute-start(f32[64,512]{1,0:T(8,128)S(1)} %get-tuple-element.26), channel_id=1, source_target_pairs={{0,2},{1,3},{2,0},{3,1},{4,6},{5,7},{6,4},{7,5},{8,10},{9,11},{10,... | collective-permute-start | bytes 393224 | tf_op jit(solution)/shard_map/ppermute | solution.py:218
  30.7 0.2 collective-permute-done.10.refs_1_
  30.9 1.7 %collective-permute-done.11.refs_2_ = f32[64,512]{1,0:T(8,128)S(1)} collective-permute-done((f32[64,512]{1,0:T(8,128)S(1)}, f32[64,512]{1,0:T(8,128)S(1)}, u32[]{:S(2)}, u32[]{:S(2)}) %collective-permute-start.11) | collective-permute-done | bytes 131104 | tf_op jit(solution)/shard_map/ppermute | solution.py:212
  32.6 2.0 %collective-permute-done.12.refs_3_ = f32[64,512]{1,0:T(8,128)S(1)} collective-permute-done((f32[64,512]{1,0:T(8,128)S(1)}, f32[64,512]{1,0:T(8,128)S(1)}, u32[]{:S(2)}, u32[]{:S(2)}) %collective-permute-start.12) | collective-permute-done | bytes 131104 | tf_op jit(solution)/shard_map/ppermute | solution.py:212
  34.6 1.0 %collect.1 = (f32[64,2048]{1,0:T(8,128)S(1)}, f32[64,2048]{1,0:T(8,128)S(1)}) custom-call(s32[4,4]{1,0:T(4,128)S(1)} %pad_add_fusion.requests.ids, f32[64,512]{1,0:T(8,128)S(1)} %mode2.1.refs_0_, f32[64,512]{1,0:T(8,128)S(1)} %collective-permute-done.10.refs_1_, f32[64,512]{1,0:T(8,128)S(1)} %collective-permute-done.11.refs_2_, ...), custom_call_target="tpu_custom_call" | custom-call | tf_op jit(solution)/shard_map/collect/pallas_call | solution.py:301
  35.6 0.1 collective-permute-start.13
  35.7 1.9 %collective-permute-done.15.arrived = f32[64,512]{1,0:T(8,128)S(1)} collective-permute-done((f32[64,512]{1,0:T(8,128)S(1)}, f32[64,512]{1,0:T(8,128)S(1)}, u32[]{:S(2)}, u32[]{:S(2)}) %collective-permute-start.15) | collective-permute-done | bytes 131104 | tf_op jit(solution)/shard_map/ppermute | solution.py:218
  37.6 0.9 %finish_items.1 = (f32[64,2048]{1,0:T(8,128)}, f32[64,512]{1,0:T(8,128)}) custom-call(f32[64,2048]{1,0:T(8,128)S(1)} %get-tuple-element.21.own, f32[64,2048]{1,0:T(8,128)S(1)} %collective-permute-done.13.arrived, f32[64,512]{1,0:T(8,128)S(1)} %finish_users.1.users), custom_call_target="tpu_custom_call" | custom-call | tf_op jit(solution)/shard_map/finish_items/pallas_call | solution.py:323
  (25 shorter events, 0.1 us)
Async XLA Ops:
  0.6 9.3 %copy-start = (f32[64,2048]{1,0:T(8,128)S(1)}, f32[64,2048]{1,0:T(8,128)}, u32[]{:S(2)}) copy-start(f32[64,2048]{1,0:T(8,128)} %own.3) | copy-start | bytes 1572868
  0.6 9.2 %copy-start.4 = (s32[1,1,4]{2,1,0:T(1,128)S(1)}, s32[1,1,4]{2,1,0:T(1,128)}, u32[]{:S(2)}) copy-start(s32[1,1,4]{2,1,0:T(1,128)} %param.9) | copy-start | bytes 52
  0.7 9.2 %collective-permute-start.4 = (f32[64,2048]{1,0:T(8,128)}, f32[64,2048]{1,0:T(8,128)S(1)}, u32[]{:S(2)}, u32[]{:S(2)}) collective-permute-start(f32[64,2048]{1,0:T(8,128)} %own.3), channel_id=1, source_target_pairs={{0,4},{4,0},{8,12},{12,8},{16,20},{20,16},{24,28},{28,24},{1,5},{5... | collective-permute-start | bytes 1572872 | tf_op jit(solution)/shard_map/ppermute | solution.py:215
  1.2 15.4 %slice-start = ((s8[8388608]{0:T(1024)(128)(4,1)}), s8[4194304]{0:T(1024)(128)(4,1)S(1)}, s32[]{:S(2)}) async-start(s8[8388608]{0:T(1024)(128)(4,1)} %bitcast.7), calls=%async_computation | async-start | bytes 8388608
  1.2 13.1 %copy-start.1 = (f32[64,512]{1,0:T(8,128)S(1)}, f32[64,512]{1,0:T(8,128)}, u32[]{:S(2)}) copy-start(f32[64,512]{1,0:T(8,128)} %refs_0_.1) | copy-start | bytes 393220
  1.2 15.4 %slice-start.1 = ((s8[8388608]{0:T(1024)(128)(4,1)}), s8[4194304]{0:T(1024)(128)(4,1)S(1)}, s32[]{:S(2)}) async-start(s8[8388608]{0:T(1024)(128)(4,1)} %bitcast.7), calls=%async_computation.1 | async-start | bytes 8388608
  1.2 15.4 %copy-start.2 = (f32[32,64]{1,0:T(8,128)S(1)}, f32[32,64]{1,0:T(8,128)}, u32[]{:S(2)}) copy-start(f32[32,64]{1,0:T(8,128)} %week_factor.1) | copy-start | bytes 24580
  1.2 7.2 %collective-permute-start = (s32[1,4]{1,0:T(1,128)}, s32[1,4]{1,0:T(1,128)S(1)}, u32[]{:S(2)}, u32[]{:S(2)}) collective-permute-start(s32[1,4]{1,0:T(1,128)} %bitcast.12), channel_id=1, source_target_pairs={{0,8},{4,12},{8,0},{12,4},{16,24},{20,28},{24,16},{28,20},{1,9},{5... | collective-permute-start | bytes 56 | tf_op jit(solution)/shard_map/ppermute | solution.py:212
  3.8 4.6 %collective-permute-start.1 = (s32[1,4]{1,0:T(1,128)}, s32[1,4]{1,0:T(1,128)S(1)}, u32[]{:S(2)}, u32[]{:S(2)}) collective-permute-start(s32[1,4]{1,0:T(1,128)} %bitcast.13), channel_id=1, source_target_pairs={{0,16},{4,20},{8,24},{12,28},{16,0},{20,4},{24,8},{28,12},{1,17},{... | collective-permute-start | bytes 56 | tf_op jit(solution)/shard_map/ppermute | solution.py:212
  5.3 4.6 %collective-permute-start.2 = (s32[1,4]{1,0:T(1,128)}, s32[1,4]{1,0:T(1,128)S(1)}, u32[]{:S(2)}, u32[]{:S(2)}) collective-permute-start(s32[1,4]{1,0:T(1,128)} %bitcast.14), channel_id=1, source_target_pairs={{0,24},{4,28},{8,16},{12,20},{16,8},{20,12},{24,0},{28,4},{1,25},{... | collective-permute-start | bytes 56 | tf_op jit(solution)/shard_map/ppermute | solution.py:212
  5.3 11.2 %collective-permute-start.3 = (f32[64,512]{1,0:T(8,128)}, f32[64,512]{1,0:T(8,128)S(1)}, u32[]{:S(2)}, u32[]{:S(2)}) collective-permute-start(f32[64,512]{1,0:T(8,128)} %refs_0_.1), channel_id=1, source_target_pairs={{0,2},{1,3},{2,0},{3,1},{4,6},{5,7},{6,4},{7,5},{8,10},{9,11},{10,... | collective-permute-start | bytes 393224 | tf_op jit(solution)/shard_map/ppermute | solution.py:218
  8.4 10.6 %copy-start.3 = (s32[1,1,4]{2,1,0:T(1,128)S(1)}, s32[1,1,4]{2,1,0:T(1,128)}, u32[]{:S(2)}) copy-start(s32[1,1,4]{2,1,0:T(1,128)} %param.8) | copy-start | bytes 52
  10.7 7.8 %collective-permute-start.5 = (f32[64,512]{1,0:T(8,128)S(1)}, f32[64,512]{1,0:T(8,128)S(1)}, u32[]{:S(2)}, u32[]{:S(2)}) collective-permute-start(f32[64,512]{1,0:T(8,128)S(1)} %get-tuple-element.14._), channel_id=1, source_target_pairs={{0,8},{4,12},{8,0},{12,4},{16,24},{20,28},{24,16},{28,20},{1,9},{5... | collective-permute-start | bytes 393224 | tf_op jit(solution)/shard_map/ppermute | solution.py:212
  11.3 7.6 %collective-permute-start.6 = (f32[64,512]{1,0:T(8,128)S(1)}, f32[64,512]{1,0:T(8,128)S(1)}, u32[]{:S(2)}, u32[]{:S(2)}) collective-permute-start(f32[64,512]{1,0:T(8,128)S(1)} %get-tuple-element.17), channel_id=1, source_target_pairs={{0,16},{4,20},{8,24},{12,28},{16,0},{20,4},{24,8},{28,12},{1,17},{... | collective-permute-start | bytes 393224 | tf_op jit(solution)/shard_map/ppermute | solution.py:212
  12.3 6.6 %collective-permute-start.7 = (f32[64,512]{1,0:T(8,128)S(1)}, f32[64,512]{1,0:T(8,128)S(1)}, u32[]{:S(2)}, u32[]{:S(2)}) collective-permute-start(f32[64,512]{1,0:T(8,128)S(1)} %get-tuple-element.18), channel_id=1, source_target_pairs={{0,24},{4,28},{8,16},{12,20},{16,8},{20,12},{24,0},{28,4},{1,25},{... | collective-permute-start | bytes 393224 | tf_op jit(solution)/shard_map/ppermute | solution.py:212
  14.3 8.5 %collective-permute-start.8 = (f32[64,512]{1,0:T(8,128)S(1)}, f32[64,512]{1,0:T(8,128)S(1)}, u32[]{:S(2)}, u32[]{:S(2)}) collective-permute-start(f32[64,512]{1,0:T(8,128)S(1)} %copy-done.1), channel_id=1, source_target_pairs={{0,1},{1,0},{2,3},{3,2},{4,5},{5,4},{6,7},{7,6},{8,9},{9,8},{10,11... | collective-permute-start | bytes 393224 | tf_op jit(solution)/shard_map/ppermute | solution.py:218
  18.5 5.0 %collective-permute-start.9 = (f32[64,512]{1,0:T(8,128)S(1)}, f32[64,512]{1,0:T(8,128)S(1)}, u32[]{:S(2)}, u32[]{:S(2)}) collective-permute-start(f32[64,512]{1,0:T(8,128)S(1)} %get-tuple-element.20.refs_2_), channel_id=1, source_target_pairs={{0,1},{1,0},{2,3},{3,2},{4,5},{5,4},{6,7},{7,6},{8,9},{9,8},{10,11... | collective-permute-start | bytes 393224 | tf_op jit(solution)/shard_map/ppermute | solution.py:218
  22.7 6.7 %collective-permute-start.14 = (f32[2,64,512]{2,1,0:T(8,128)S(1)}, f32[2,64,512]{2,1,0:T(8,128)S(1)}, u32[]{:S(2)}, u32[]{:S(2)}) collective-permute-start(f32[2,64,512]{2,1,0:T(8,128)S(1)} %get-tuple-element.23), channel_id=1, source_target_pairs={{0,1},{1,0},{2,3},{3,2},{4,5},{5,4},{6,7},{7,6},{8,9},{9,8},{10,11... | collective-permute-start | bytes 786440 | tf_op jit(solution)/shard_map/ppermute | solution.py:218
  25.9 5.1 %collective-permute-start.10 = (f32[64,512]{1,0:T(8,128)S(1)}, f32[64,512]{1,0:T(8,128)S(1)}, u32[]{:S(2)}, u32[]{:S(2)}) collective-permute-start(f32[64,512]{1,0:T(8,128)S(1)} %mode2.1.refs_0_), channel_id=1, source_target_pairs={{0,8},{4,12},{8,0},{12,4},{16,24},{20,28},{24,16},{28,20},{1,9},{5... | collective-permute-start | bytes 393224 | tf_op jit(solution)/shard_map/ppermute | solution.py:212
  27.6 5.0 %collective-permute-start.11 = (f32[64,512]{1,0:T(8,128)S(1)}, f32[64,512]{1,0:T(8,128)S(1)}, u32[]{:S(2)}, u32[]{:S(2)}) collective-permute-start(f32[64,512]{1,0:T(8,128)S(1)} %mode2.1.refs_0_), channel_id=1, source_target_pairs={{0,16},{4,20},{8,24},{12,28},{16,0},{20,4},{24,8},{28,12},{1,17},{... | collective-permute-start | bytes 393224 | tf_op jit(solution)/shard_map/ppermute | solution.py:212
  28.8 5.9 %collective-permute-start.12 = (f32[64,512]{1,0:T(8,128)S(1)}, f32[64,512]{1,0:T(8,128)S(1)}, u32[]{:S(2)}, u32[]{:S(2)}) collective-permute-start(f32[64,512]{1,0:T(8,128)S(1)} %mode2.1.refs_0_), channel_id=1, source_target_pairs={{0,24},{4,28},{8,16},{12,20},{16,8},{20,12},{24,0},{28,4},{1,25},{... | collective-permute-start | bytes 393224 | tf_op jit(solution)/shard_map/ppermute | solution.py:212
  29.5 8.1 %collective-permute-start.15 = (f32[64,512]{1,0:T(8,128)S(1)}, f32[64,512]{1,0:T(8,128)S(1)}, u32[]{:S(2)}, u32[]{:S(2)}) collective-permute-start(f32[64,512]{1,0:T(8,128)S(1)} %get-tuple-element.26), channel_id=1, source_target_pairs={{0,2},{1,3},{2,0},{3,1},{4,6},{5,7},{6,4},{7,5},{8,10},{9,11},{10,... | collective-permute-start | bytes 393224 | tf_op jit(solution)/shard_map/ppermute | solution.py:218
  35.6 2.0 %collective-permute-start.13 = (f32[64,2048]{1,0:T(8,128)S(1)}, f32[64,2048]{1,0:T(8,128)S(1)}, u32[]{:S(2)}, u32[]{:S(2)}) collective-permute-start(f32[64,2048]{1,0:T(8,128)S(1)} %get-tuple-element.22), channel_id=1, source_target_pairs={{0,4},{4,0},{8,12},{12,8},{16,20},{20,16},{24,28},{28,24},{1,5},{5... | collective-permute-start | bytes 1572872 | tf_op jit(solution)/shard_map/ppermute | solution.py:215
